TPU v7x, 32 devices: a whole 2x2x4 slice. The times are simulated.
32 devices in a mesh: dp: 8 (over z, y), group: 4 (over x, core).
Axes of the slice: x: 2, y: 2, z: 4, core: 2. Of those that a mesh axis runs over, the one named last changes fastest.
Arguments:
- context: bfloat16 [12288, 768], P(('dp', 'group')), may hold values from -6 to 6
- segment_ids: int32 [32, 384], P(('dp', 'group')), may hold values from 0 to 3, never falling along the last dimension, each value on 1 to 192 neighbouring positions
- target_index: int32 [32, 4, 4, 40], P(('dp', 'group')), may hold values from 0 to 195
- target_length: int32 [32, 4, 4], P(('dp', 'group')), may hold values from 1 to 40, as said below
- pos_table: float32 [196, 384], replicated, may hold values from -1 to 1
- params: float32 [2066304], replicated
- first_moment: float32 [2066304], P('dp')
- second_moment: float32 [2066304], P('dp')
- cotangent: bfloat16 [32, 1024, 384], P(('dp', 'group')), may hold values from -6 to 6
Outputs:
- block_out: bfloat16 [32, 1024, 384], P(('dp', 'group'))
- context_grad: bfloat16 [12288, 768], P(('dp', 'group'))
- new_params: float32 [2066304], replicated
- new_first: float32 [2066304], P('dp')
- new_second: float32 [2066304], P('dp')
Inputs may be any that keep to these rules, and one draw needn't show every extreme that they name: `target_length`: each packed row has at least one target block of length 40.
All inputs are finite; a program needn't handle non-finite values.
Results may differ from a plain program's by a relative error of at most 0.015.
Values may be sent and summed in bfloat16 or wider, within the bound.
No kernel may reach another device: no remote copies, remote signals or barrier semaphores. Data moves between devices by JAX's collectives and lax.ppermute only.
A program may use at most 256 MiB of HBM per device.

v0:
```python
import functools

import jax
import jax.numpy as jnp
from jax import lax
from jax.experimental import pallas as pl
from jax.experimental.pallas import tpu as pltpu
from jax.sharding import PartitionSpec as P

D_IN = 768
D = 384
HEADS = 12
HD = 32
FF = 1536
GRID = 196
BLOCKS = 4
TMAX = 40
STEP = 10
IMG = 4
CTX = 384
TGT = IMG * BLOCKS * TMAX
L = CTX + TGT
NP = D_IN * D + 4 * D * D + 2 * D * FF + 5 * D
LANES = 128
GROUPS = D // LANES
PER = LANES // HD
WIN = 200
KEYS = WIN + TMAX
WIDE = 256
TILE = 256
MLP_TILE = 512
CHUNK = 512

ROW_IN = 0
ROW_QKV = D_IN * D // LANES
ROW_OUT = ROW_QKV + 3 * D * D // LANES
ROW_UP = ROW_OUT + D * D // LANES
ROW_DOWN = ROW_UP + D * FF // LANES
ROW_SMALL = ROW_DOWN + FF * D // LANES
ROWS_ALL = NP // LANES
SMALL = 5 * D
SMALL_ROWS = SMALL // LANES
SMALL_PAD = 16

norm_eps = 1e-06
mask_value = -1e30
LOG2E = 1.4426950408889634
SCALE = HD**-0.5
F32 = jnp.float32
BF16 = jnp.bfloat16
VMEM_CAP = 64000 * 1024


def dot(a, b):
    return jnp.dot(a, b, preferred_element_type=F32)


def dot_nt(a, b):
    return lax.dot_general(a, b, (((1,), (1,)), ((), ())), preferred_element_type=F32)


def dot_tn(a, b):
    return lax.dot_general(a, b, (((0,), (0,)), ((), ())), preferred_element_type=F32)


def ceil_to(n, m):
    return -(-n // m) * m


class Plan:
    def __init__(self, n_dp, n_group):
        self.n_dp, self.n_group = n_dp, n_group
        self.share = NP // n_dp
        self.row0 = [d * self.share // LANES for d in range(n_dp)]
        self.lane0 = [d * self.share % LANES for d in range(n_dp)]
        most = max(ceil_to(o + self.share, LANES) // LANES for o in self.lane0)
        self.sub = ceil_to(-(-most // (2 * n_group)), 16)
        self.piece = 2 * self.sub
        self.shard_rows = self.piece * n_group
        self.n_hi, self.half = n_group // 2, n_dp // 2
        self.quarter = self.half // 2
        self.early0 = n_dp // 2
        assert self.early0 * self.share >= ROW_OUT * LANES
        self.helper = 2 * (self.half - 1 - self.quarter) + 1
        self.tail = ROW_SMALL - self.row0[-1]
        self.flat_rows = ceil_to(max(r + self.shard_rows for r in self.row0), 16)
        self.mid_rows = ceil_to(self.row0[self.early0 - 1] + self.shard_rows - ROW_OUT, 8)
        self.cut = ceil_to(self.early0 * self.share, 8 * LANES) // LANES


def layer_norm_parts(x):
    mu = jnp.mean(x, axis=-1, keepdims=True)
    xc = x - mu
    rstd = lax.rsqrt(jnp.mean(xc * xc, axis=-1, keepdims=True) + norm_eps)
    return xc * rstd, rstd


def layer_norm_back(dy, gain, xhat, rstd):
    dx = dy * gain
    a = jnp.mean(dx, axis=-1, keepdims=True)
    b = jnp.mean(dx * xhat, axis=-1, keepdims=True)
    return rstd * (dx - a - xhat * b)


def reciprocal(x):
    r = pl.reciprocal(x, approx=True)
    return r * (2.0 - x * r)


def gelu_both(x):
    z = jnp.abs(x) * (0.5**0.5)
    t = reciprocal(1.0 + 0.3275911 * z)
    e = jnp.exp2(x * x * (-0.5 * LOG2E))
    poly = ((((1.061405429 * t - 1.453152027) * t + 1.421413741) * t - 0.284496736) * t + 0.254829592) * t
    tail = 0.5 * poly * e
    cdf = jnp.where(x >= 0, 1.0 - tail, tail)
    pdf = e * 0.3989422804014327
    return x * cdf, cdf + x * pdf


def head_masks(first, count, width):
    lane = lax.broadcasted_iota(jnp.int32, (1, width), 1)
    return [(lane // HD == first + h).astype(F32) for h in range(count)]


def stack_heads(x, masks):
    return jnp.concatenate([x * m for m in masks], axis=0)


def diagonal(x, rows):
    return jnp.concatenate(
        [x[h * HD : (h + 1) * HD, h * rows : (h + 1) * rows] for h in range(PER)], axis=0
    )


def stack_six(x, masks):
    gap = jnp.zeros((WIDE // 2 - 3 * TMAX, WIDE), F32)
    parts = [x * m for m in masks]
    return jnp.concatenate(parts[:3] + [gap] + parts[3:] + [gap], axis=0).astype(BF16)


def fold_six(x, masks):
    total = None
    for h in range(6):
        at = (h // 3) * (WIDE // 2) + (h % 3) * TMAX
        part = x[at : at + TMAX] * masks[h]
        total = part if total is None else total + part
    return total


def half_masks(half):
    lane = lax.broadcasted_iota(jnp.int32, (1, WIDE), 1)
    head = (lane + half * LANES) // HD
    return [(head == 6 * half + h).astype(F32) for h in range(6)]


def half_slice(half, part):
    return pl.ds(pl.multiple_of(part * D + half * LANES, LANES), WIDE)


def lane_slice(g, part):
    return pl.ds(pl.multiple_of(part * D + g * LANES, LANES), LANES)


def prep_kernel(
    plan,
    own_s,
    params_hbm, index_ref, pos_ref,
    vec, own_ref,
    w_in_hbm, w_qkv_hbm, w_out_hbm, w_up_hbm, w_down_hbm, stream_hbm,
    pbuf, w_in_b, w_qkv_b, w_out_b, w_up_b, w_down_b, stream, hot_ref, sems, out_sems,
):
    spans = [
        (ROW_SMALL, SMALL_ROWS), (ROW_IN, ROW_QKV - ROW_IN), (ROW_QKV, ROW_OUT - ROW_QKV),
        (ROW_OUT, ROW_UP - ROW_OUT), (ROW_UP, ROW_DOWN - ROW_UP), (ROW_DOWN, ROW_SMALL - ROW_DOWN),
    ]
    copies = [
        pltpu.make_async_copy(params_hbm.at[pl.ds(r, n)], pbuf.at[pl.ds(r, n)], sems.at[i])
        for i, (r, n) in enumerate(spans)
    ]
    for c in copies:
        c.start()
    outgoing = []

    def send_out(src, dst):
        copy = pltpu.make_async_copy(src, dst, out_sems.at[len(outgoing)])
        copy.start()
        outgoing.append(copy)

    def take(base, rows, tiles, dst, step):
        def body(i, _):
            for c in range(tiles):
                src = pl.ds(base + i * (step * tiles) + c, step, stride=tiles)
                dst[pl.ds(pl.multiple_of(i * step, step), step), c * LANES : (c + 1) * LANES] = pbuf[src, :].astype(BF16)
            return 0
        lax.fori_loop(0, rows // step, body, 0)

    eye = lax.broadcasted_iota(jnp.int32, (TMAX, TMAX), 0) == lax.broadcasted_iota(jnp.int32, (TMAX, TMAX), 1)
    grid_id = lax.broadcasted_iota(jnp.int32, (TMAX, GRID), 1)
    for j in range(IMG * BLOCKS):
        row = index_ref[0, j // BLOCKS, j % BLOCKS : j % BLOCKS + 1, :]
        col = jnp.sum(jnp.where(eye, row, 0), axis=1, keepdims=True)
        hot_ref[j * TMAX : (j + 1) * TMAX, :] = (col == grid_id).astype(F32)

    copies[0].wait()
    vec[...] = jnp.zeros_like(vec)
    for k in range(5):
        for c in range(D // LANES):
            vec[k : k + 1, c * LANES : (c + 1) * LANES] = pbuf[pl.ds(ROW_SMALL + k * 3 + c, 1), :]
    mask_tok = vec[4:5, :]
    pos = pos_ref[...]
    pos_hi = pos.astype(BF16)
    pos_lo = (pos - pos_hi.astype(F32)).astype(BF16)
    for i in range(TGT // 128):
        rows = slice(i * 128, (i + 1) * 128)
        hot = hot_ref[rows, :].astype(BF16)
        stream[rows, :] = mask_tok + (dot(hot, pos_hi) + dot(hot, pos_lo))
    send_out(stream, stream_hbm)

    for n, (base, rows, tiles, dst, out, step) in enumerate((
        (ROW_IN, D_IN, 3, w_in_b, w_in_hbm, 128), (ROW_QKV, D, 9, w_qkv_b, w_qkv_hbm, 128),
        (ROW_OUT, D, 3, w_out_b, w_out_hbm, 128), (ROW_UP, D, 12, w_up_b, w_up_hbm, 128),
        (ROW_DOWN, FF, 3, w_down_b, w_down_hbm, 128),
    )):
        copies[1 + n].wait()
        take(base, rows, tiles, dst, step)
        send_out(dst, out)
    for i in range(2):
        own_ref[i] = pbuf[pl.ds(own_s[8 + i], plan.sub), :]
    for copy in outgoing:
        copy.wait()


def place_pieces(own_s, dst, parts, rows):
    n = len(parts)
    for r, part in enumerate(parts):
        at = pl.multiple_of(lax.rem(own_s[6] + (n - r), n) * rows, 16)
        dst[pl.ds(at, rows), :] = part


def window(seg_s, img):
    return pl.multiple_of(jnp.minimum(seg_s[img] // 8 * 8, CTX - WIN), 8)


def forward_kernel(
    plan,
    len_s, own_s,
    vec, ctx_own, ctx_got, seg_row, cot_hbm,
    w_in_hbm, w_qkv_hbm, w_out_hbm, w_up_hbm, w_down_hbm, target_hbm,
    small_out, keep_ref, send_ref, seg_s,
    out_ref, mid_ref, ctx_hbm, stream_hbm, qkv_hbm, probs_c_hbm, probs_t_hbm, d_mixed_hbm, d_middle_hbm,
    w_in_b, w_qkv_b, w_out_b, w_up_b, w_down_b, ctx, stream, qkv, probs_c, probs_t,
    mixed, mixed_b, d_mixed, d_branch, d_middle, normed, bias, v_t, second, active, d_lift, e_down, gflat, live_col, cot, out_s,
    sems, out_sems,
):
    copies = [
        pltpu.make_async_copy(src, dst, sems.at[i])
        for i, (src, dst) in enumerate((
            (w_in_hbm, w_in_b), (w_qkv_hbm, w_qkv_b), (target_hbm, stream.at[pl.ds(CTX, TGT)]),
            (w_out_hbm, w_out_b), (w_up_hbm, w_up_b), (w_down_hbm, w_down_b), (cot_hbm, cot),
        ))
    ]
    for c in copies:
        c.start()
    outgoing = []

    def send_out(src, dst):
        copy = pltpu.make_async_copy(src, dst, out_sems.at[len(outgoing)])
        copy.start()
        outgoing.append(copy)

    gain1, bias1, gain2, bias2 = [vec[k : k + 1, :] for k in range(4)]
    seg = seg_row[...]
    for i in range(IMG + 1):
        seg_s[i] = jnp.sum((seg < i).astype(jnp.int32))
    row_id = lax.broadcasted_iota(jnp.int32, (CTX, CTX), 0)
    row_image = sum((row_id >= seg_s[i]).astype(jnp.int32) for i in range(1, IMG))
    bias[...] = jnp.where(row_image == seg, 0.0, mask_value)
    live_col[0:CTX, :] = jnp.ones((CTX, LANES), F32)
    slot_id = lax.broadcasted_iota(jnp.int32, (TMAX, LANES), 0)
    for j in range(IMG * BLOCKS):
        live_col[CTX + j * TMAX : CTX + (j + 1) * TMAX, :] = (slot_id < len_s[0, j // BLOCKS, j % BLOCKS]).astype(F32)

    stored = ctx_own.shape[0] // plan.n_group
    first = ctx_own[pl.ds(pl.multiple_of(own_s[6] * stored, 16), stored), :]
    place_pieces(own_s, ctx, [first] + [ref[...] for ref in ctx_got], stored)
    send_out(ctx, ctx_hbm)
    copies[0].wait()
    stream[0:CTX, :] = dot(ctx[...], w_in_b[...])
    copies[2].wait()
    send_out(stream, stream_hbm)
    copies[1].wait()

    def qkv_body(i, _):
        rows = pl.ds(pl.multiple_of(i * TILE, TILE), TILE)
        xhat, _r = layer_norm_parts(stream[rows, :])
        n = (xhat * gain1 + bias1).astype(BF16)
        normed[rows, :] = n
        qkv[rows, :] = dot(n, w_qkv_b[...]).astype(BF16).astype(F32)
        return 0

    lax.fori_loop(0, L // TILE, qkv_body, 0, unroll=4)

    send_out(qkv, qkv_hbm)
    masks = head_masks(0, PER, LANES)
    c2 = SCALE * LOG2E
    for g in range(GROUPS):
        v_t[g * LANES : (g + 1) * LANES, :] = qkv[0:CTX, 2 * D + g * LANES : 2 * D + (g + 1) * LANES].T.astype(BF16)

    def softmax_down(t):
        p = jnp.exp2(t - jnp.max(t, axis=0, keepdims=True))
        return (p * (1.0 / jnp.sum(p, axis=0, keepdims=True))).astype(BF16)

    def ctx_body(i, _):
        g, chunk = i // 3, i % 3
        rows = pl.ds(pl.multiple_of(chunk * LANES, LANES), LANES)
        lanes = pl.ds(pl.multiple_of(g * LANES, LANES), LANES)
        q = stack_heads(qkv[rows, lane_slice(g, 0)], masks).astype(BF16)
        st = dot_nt(qkv[0:CTX, lane_slice(g, 1)].astype(BF16), q)
        for h in range(PER):
            cols = slice(h * LANES, (h + 1) * LANES)
            probs_c[i, :, cols] = softmax_down(st[:, cols] * c2 + bias[:, rows])
        o = dot(v_t[lanes, :], probs_c[i])
        mixed[rows, lanes] = diagonal(o, LANES).T
        return 0

    lax.fori_loop(0, GROUPS * 3, ctx_body, 0, unroll=3)
    send_out(probs_c, probs_c_hbm)

    key_id = lax.broadcasted_iota(jnp.int32, (KEYS, 1), 0)
    mixed[CTX:, :] = jnp.zeros((TGT, D), F32)

    def tgt_body(i, _):
        half, img = i // IMG, i % IMG
        hmasks = half_masks(half)
        first = window(seg_s, img)
        kw = qkv[pl.ds(first, WIN), half_slice(half, 1)]
        vw = qkv[pl.ds(first, WIN), half_slice(half, 2)]
        lo, hi = seg_s[img] - first, seg_s[img + 1] - first
        in_win = (key_id >= lo) & (key_id < hi) & (key_id < WIN)
        units = []
        for blk in range(BLOCKS):
            j = img * BLOCKS + blk
            rows = pl.ds(pl.multiple_of(CTX + j * TMAX, 8), TMAX)
            k = jnp.concatenate([kw, qkv[rows, half_slice(half, 1)]], axis=0).astype(BF16)
            v = jnp.concatenate([vw, qkv[rows, half_slice(half, 2)]], axis=0).astype(BF16)
            q = stack_six(qkv[rows, half_slice(half, 0)], hmasks)
            ok = in_win | ((key_id >= WIN) & (key_id < WIN + len_s[0, img, blk]))
            units.append((rows, v, dot_nt(k, q), jnp.where(ok, 0.0, mask_value)))
        for blk, (rows, v, st, bias_col) in enumerate(units):
            for n in range(2):
                cols = slice(n * LANES, (n + 1) * LANES)
                probs_t[i * BLOCKS + blk, :, cols] = softmax_down(st[:, cols] * c2 + bias_col)
        for blk, (rows, v, st, bias_col) in enumerate(units):
            o = dot_tn(probs_t[i * BLOCKS + blk], v)
            mixed[rows, pl.ds(pl.multiple_of(half * LANES, LANES), WIDE)] += fold_six(o, hmasks)
        return 0

    lax.fori_loop(0, 2 * IMG, tgt_body, 0, unroll=2)
    send_out(probs_t, probs_t_hbm)

    for c in copies[3:]:
        c.wait()

    def mixed_of(rows):
        low = mixed[rows, :].astype(BF16)
        mixed_b[rows, :] = low
        return low

    def block_body(i, carry):
        dg2, db2 = carry
        rows = pl.ds(pl.multiple_of(i * MLP_TILE, MLP_TILE), MLP_TILE)
        live = live_col[rows, 0:1]
        middle = stream[rows, :] + dot(mixed_of(rows), w_out_b[...])
        xhat, rstd = layer_norm_parts(middle)
        sec = (xhat * gain2 + bias2).astype(BF16)
        second[rows, :] = sec
        top = live * cot[rows, :].astype(F32)
        e = top.astype(BF16)
        e_down[rows, :] = e
        out = middle
        d_second = jnp.zeros((MLP_TILE, D), F32)
        for j in range(FF // CHUNK):
            cols = slice(j * CHUNK, (j + 1) * CHUNK)
            lifted = dot(sec, w_up_b[:, cols])
            act, slope = gelu_both(lifted)
            act = act.astype(BF16)
            active[rows, cols] = act
            dl = (dot_nt(e, w_down_b[cols, :]) * slope).astype(BF16)
            d_lift[rows, cols] = dl
            out = out + dot(act, w_down_b[cols, :])
            d_second = d_second + dot_nt(dl, w_up_b[:, cols])
        out_s[rows, :] = (live * out).astype(BF16)
        dm = top + layer_norm_back(d_second, gain2, xhat, rstd)
        d_middle[rows, :] = dm
        db = dm.astype(BF16)
        d_branch[rows, :] = db
        d_mixed[rows, :] = dot_nt(db, w_out_b[...])
        dg2 = dg2 + jnp.sum(d_second * xhat, axis=0, keepdims=True)
        db2 = db2 + jnp.sum(d_second, axis=0, keepdims=True)
        return dg2, db2

    zero = jnp.zeros((1, D), F32)
    dg2, db2 = lax.fori_loop(0, L // MLP_TILE, block_body, (zero, zero))
    small_out[...] = jnp.concatenate([dg2, db2, jnp.zeros((6, D), F32)], axis=0)

    send_out(out_s, out_ref)
    send_out(d_mixed, d_mixed_hbm)
    send_out(d_middle, d_middle_hbm)

    end = ROW_SMALL - ROW_OUT
    gflat[end:, :] = jnp.zeros((gflat.shape[0] - end, LANES), F32)

    g = dot_tn(mixed_b[...], d_branch[...])
    for c in range(3):
        gflat[pl.ds(c, D, stride=3), :] = g[:, c * LANES : (c + 1) * LANES]

    def up_body(j, _):
        cols = pl.ds(pl.multiple_of(j * CHUNK, CHUNK), CHUNK)
        g = dot_tn(second[...], d_lift[:, cols])
        for c in range(CHUNK // LANES):
            gflat[pl.ds(ROW_UP - ROW_OUT + CHUNK // LANES * j + c, D, stride=12), :] = g[:, c * LANES : (c + 1) * LANES]
        return 0

    lax.fori_loop(0, FF // CHUNK, up_body, 0, unroll=3)

    send_out(gflat.at[pl.ds(0, plan.mid_rows)], mid_ref)

    def down_body(j, _):
        cols = pl.ds(pl.multiple_of(j * D, D), D)
        g = dot_tn(active[:, cols], e_down[...])
        for c in range(3):
            gflat[pl.ds(ROW_DOWN - ROW_OUT + j * (3 * D) + c, D, stride=3), :] = g[:, c * LANES : (c + 1) * LANES]
        return 0

    lax.fori_loop(0, 4, down_body, 0, unroll=4)

    store_pieces(plan, gflat, ROW_OUT, range(plan.early0, plan.n_dp), plan.quarter, own_s[1], keep_ref, send_ref)
    for copy in outgoing:
        copy.wait()


def store_pieces(plan, gflat, base, shards, hi0, core, keep_ref, send_ref, extra=None):
    for d in shards:
        for q in range(plan.n_group):
            start = plan.row0[d] - base + q * plan.piece
            blocks = [gflat[start + n * plan.sub : start + (n + 1) * plan.sub, :].astype(BF16) for n in range(2)]

            def put(ref):
                for n in range(2):
                    ref[q // 2, d % 2, d // 2 - hi0, n, 0 : plan.sub, :] = blocks[n]
                    if extra is not None:
                        ref[q // 2, d % 2, d // 2 - hi0, n, plan.sub :, :] = extra

            @pl.when(core == q % 2)
            def _():
                put(keep_ref)

            @pl.when(core != q % 2)
            def _():
                put(send_ref)


def attention_back_kernel(
    plan,
    seg_s, own_s, qkv_hbm, probs_c_hbm, probs_t_hbm, d_mixed_hbm, one_hbm, two_hbm,
    dpk, mine_ref, other_ref, qkv, probs_c, probs_t, d_mixed, d_qkv, k_t, mom, tail, sems,
):
    incoming = {}
    for n, (name, src, dst) in enumerate((
        ("qkv", qkv_hbm, qkv), ("d_mixed", d_mixed_hbm, d_mixed), ("probs_c", probs_c_hbm, probs_c),
        ("probs_t", probs_t_hbm, probs_t),
    )):
        incoming[name] = pltpu.make_async_copy(src, dst, sems.at[n])
        incoming[name].start()

    tail0 = plan.tail // 8 * 8
    moments = []
    for i, src in enumerate((one_hbm, two_hbm)):
        moments.append(pltpu.make_async_copy(src.at[pl.ds(own_s[4], plan.piece + 8)], mom.at[i], sems.at[4 + 2 * i]))
        moments.append(pltpu.make_async_copy(src.at[pl.ds(tail0, 32)], tail.at[i], sems.at[5 + 2 * i]))
    for copy in moments:
        copy.start()

    d_qkv[...] = jnp.zeros_like(d_qkv)
    masks = head_masks(0, PER, LANES)
    incoming["qkv"].wait()
    for g in range(GROUPS):
        k_t[g * LANES : (g + 1) * LANES, :] = qkv[0:CTX, D + g * LANES : D + (g + 1) * LANES].T.astype(BF16)
    incoming["d_mixed"].wait()
    incoming["probs_c"].wait()

    def back_down(p, dp):
        p = p.astype(F32)
        delta = jnp.sum(p * dp, axis=0, keepdims=True)
        return (p * (dp - delta)).astype(BF16)

    def ctx_body(i, _):
        g, chunk = i // 3, i % 3
        rows = pl.ds(pl.multiple_of(chunk * LANES, LANES), LANES)
        lanes = pl.ds(pl.multiple_of(g * LANES, LANES), LANES)
        do = stack_heads(d_mixed[rows, lanes], masks).astype(BF16)
        dpt = dot_nt(qkv[0:CTX, lane_slice(g, 2)].astype(BF16), do)
        ds = []
        for h in range(PER):
            cols = slice(h * LANES, (h + 1) * LANES)
            ds.append(back_down(probs_c[i, :, cols], dpt[:, cols]))
        ds = jnp.concatenate(ds, axis=1)
        q = stack_heads(qkv[rows, lane_slice(g, 0)], masks).astype(BF16)
        d_qkv[rows, lane_slice(g, 0)] = diagonal(dot(k_t[lanes, :], ds), LANES).T
        d_qkv[0:CTX, lane_slice(g, 1)] += dot(ds, q)
        d_qkv[0:CTX, lane_slice(g, 2)] += dot(probs_c[i], do)
        return 0

    lax.fori_loop(0, GROUPS * 3, ctx_body, 0, unroll=3)
    incoming["probs_t"].wait()

    def tgt_body(i, _):
        half, img = i // IMG, i % IMG
        hmasks = half_masks(half)
        first = window(seg_s, img)
        win = pl.ds(first, WIN)
        kw = qkv[win, half_slice(half, 1)]
        vw = qkv[win, half_slice(half, 2)]
        units = []
        for blk in range(BLOCKS):
            rows = pl.ds(pl.multiple_of(CTX + (img * BLOCKS + blk) * TMAX, 8), TMAX)
            v = jnp.concatenate([vw, qkv[rows, half_slice(half, 2)]], axis=0).astype(BF16)
            do = stack_six(d_mixed[rows, pl.ds(pl.multiple_of(half * LANES, LANES), WIDE)], hmasks)
            units.append((rows, do, dot_nt(v, do)))
        dkw = jnp.zeros((WIN, WIDE), F32)
        dvw = jnp.zeros((WIN, WIDE), F32)
        for blk, (rows, do, dpt) in enumerate(units):
            p = probs_t[i * BLOCKS + blk]
            ds = jnp.concatenate(
                [back_down(p[:, n * LANES : (n + 1) * LANES], dpt[:, n * LANES : (n + 1) * LANES]) for n in range(2)],
                axis=1,
            )
            k = jnp.concatenate([kw, qkv[rows, half_slice(half, 1)]], axis=0).astype(BF16)
            q = stack_six(qkv[rows, half_slice(half, 0)], hmasks)
            d_qkv[rows, half_slice(half, 0)] += fold_six(dot_tn(ds, k), hmasks)
            dk = dot(ds, q)
            dv = dot(p, do)
            d_qkv[rows, half_slice(half, 1)] += dk[WIN:]
            d_qkv[rows, half_slice(half, 2)] += dv[WIN:]
            dkw = dkw + dk[:WIN]
            dvw = dvw + dv[:WIN]
        d_qkv[win, half_slice(half, 1)] += dkw
        d_qkv[win, half_slice(half, 2)] += dvw
        return 0

    lax.fori_loop(0, 2 * IMG, tgt_body, 0, unroll=2)
    for copy in moments:
        copy.wait()
    lane = lax.broadcasted_iota(jnp.int32, (1, LANES), 1)
    for i in range(2):
        turned = pltpu.roll(mom[i], own_s[5], 1)
        aligned = jnp.where(lane >= own_s[5], turned[8:], turned[7:-1])
        mine_ref[i] = aligned[: plan.sub]
        other_ref[i, 0 : plan.sub, :] = aligned[plan.sub :]
        turned = pltpu.roll(tail[i], own_s[5], 1)
        aligned = jnp.where(lane >= own_s[5], turned[1:], turned[:-1])
        at = plan.tail - tail0 + 7
        other_ref[i, plan.sub : plan.sub + SMALL_PAD, :] = aligned[at : at + SMALL_PAD]

    def round_body(i, _):
        rows = pl.ds(pl.multiple_of(i * 128, 128), 128)
        dpk[rows, 0 : 2 * D] = (d_qkv[rows, 0 : 2 * D] * SCALE).astype(BF16)
        dpk[rows, 2 * D :] = d_qkv[rows, 2 * D :].astype(BF16)
        return 0

    lax.fori_loop(0, L // 128, round_body, 0, unroll=8)


def backward_kernel(
    plan,
    own_s,
    vec, small_in, mid_ref, dpk,
    w_in_hbm, w_qkv_hbm, ctx_hbm, stream_hbm, d_middle_hbm,
    keep_ref, send_ref, same_ref, cross_ref,
    w_in_b, w_qkv_b, ctx_ref, stream, d_middle, normed, d_hidden, ctx_grad, small_flat, gflat, sems,
):
    incoming = {}
    for n, (name, src, dst) in enumerate((
        ("w_qkv", w_qkv_hbm, w_qkv_b), ("stream", stream_hbm, stream), ("d_middle", d_middle_hbm, d_middle),
        ("w_in", w_in_hbm, w_in_b), ("ctx", ctx_hbm, ctx_ref),
    )):
        incoming[name] = pltpu.make_async_copy(src, dst, sems.at[n])
        incoming[name].start()
    gain1, bias1 = vec[0:1, :], vec[1:2, :]
    gflat[ROW_OUT : ROW_OUT + plan.mid_rows, :] = mid_ref[...]
    for name in ("w_qkv", "stream", "d_middle"):
        incoming[name].wait()

    def row_body(i, carry):
        dg1, db1, dmask = carry
        rows = pl.ds(pl.multiple_of(i * 128, 128), 128)
        xhat, rstd = layer_norm_parts(stream[rows, :])
        normed[rows, :] = (xhat * gain1 + bias1).astype(BF16)
        d_normed = dot_nt(dpk[rows, :], w_qkv_b[...])
        d_stream = d_middle[rows, :] + layer_norm_back(d_normed, gain1, xhat, rstd)
        dg1 = dg1 + jnp.sum(d_normed * xhat, axis=0, keepdims=True)
        db1 = db1 + jnp.sum(d_normed, axis=0, keepdims=True)
        is_tgt = (i >= CTX // 128).astype(F32)
        dmask = dmask + is_tgt * jnp.sum(d_stream, axis=0, keepdims=True)

        @pl.when(i < CTX // 128)
        def _():
            d_hidden[rows, :] = d_stream.astype(BF16)

        return dg1, db1, dmask

    zero = jnp.zeros((1, D), F32)
    dg1, db1, dmask = lax.fori_loop(0, L // 128, row_body, (zero, zero, zero), unroll=8)
    for k, row in enumerate((dg1, db1, small_in[0:1, :], small_in[1:2, :], dmask)):
        for c in range(3):
            small_flat[3 * k + c : 3 * k + c + 1, :] = row[:, c * LANES : (c + 1) * LANES]
    small_flat[SMALL_ROWS:, :] = jnp.zeros((SMALL_PAD - SMALL_ROWS, LANES), F32)

    incoming["w_in"].wait()
    incoming["ctx"].wait()
    ctx_grad[...] = dot_nt(d_hidden[...], w_in_b[...]).astype(BF16)
    stored = CTX // plan.n_group
    for a in range(plan.n_hi):
        hi = lax.rem(own_s[2] + a, plan.n_hi) * 2
        for ref, core in ((same_ref, own_s[1]), (cross_ref, 1 - own_s[1])):
            ref[a] = ctx_grad[pl.ds(pl.multiple_of((hi + core) * stored, 16), stored), :]
    for j in range(2):
        g = dot_tn(ctx_ref[:, j * D : (j + 1) * D], d_hidden[...])
        for c in range(3):
            gflat[pl.ds(ROW_IN + j * 3 * D + c, D, stride=3), :] = g[:, c * LANES : (c + 1) * LANES]
    def qkv_body(j, _):
        g = dot_tn(normed[...], dpk[:, pl.ds(pl.multiple_of(j * D, D), D)])
        for c in range(3):
            gflat[pl.ds(ROW_QKV + 3 * j + c, D, stride=9), :] = g[:, c * LANES : (c + 1) * LANES]
        return 0

    lax.fori_loop(0, 3, qkv_body, 0)
    store_pieces(plan, gflat, 0, range(plan.early0), 0, own_s[1], keep_ref, send_ref, small_flat[...].astype(BF16))


def vmem(n):
    return [pl.BlockSpec(memory_space=pltpu.VMEM)] * n


def smem(n):
    return [pl.BlockSpec(memory_space=pltpu.SMEM)] * n


def shape(dims, dtype):
    return jax.ShapeDtypeStruct(dims, dtype)


def fetch_blocks(plan, own_s, refs, rels, dst, sems):
    for i, (ref, (c_rel, a_rel, b_rel)) in enumerate(zip(refs, rels)):
        core = lax.rem(own_s[1] + c_rel, 2)
        hi = lax.rem(own_s[2] + a_rel, plan.n_hi)
        lo = lax.rem(own_s[3] + b_rel, 2)
        for t in range(plan.quarter):
            pltpu.make_async_copy(ref.at[t], dst.at[core, hi, lo, t], sems.at[core, hi, lo, t]).start()


def wait_shard(plan, d, hi0, dst, sems):
    t = d // 2 - hi0
    for core in range(2):
        for hi in range(plan.n_hi):
            at = dst.at[core, hi, d % 2, t]
            pltpu.make_async_copy(at, at, sems.at[core, hi, d % 2, t]).wait()


def put_rows(plan, shards, hi0, src, out, base):
    for d in shards:
        lane0 = plan.lane0[d]
        rows = ceil_to(lane0 + plan.share, LANES) // LANES
        for q in range(plan.n_group):
            for n in range(2):
                start = q * plan.piece + n * plan.sub
                count = min(plan.sub, rows - start)
                if count <= 0:
                    continue
                block = src[q % 2, q // 2, d % 2, d // 2 - hi0, n, 0 : plan.sub, :].astype(F32)
                at = plan.row0[d] + start - base
                if start == 0 and lane0:
                    lane = lax.broadcasted_iota(jnp.int32, (1, LANES), 1)
                    out[at : at + 1, :] = jnp.where(lane < lane0, out[at : at + 1, :], block[0:1])
                    out[at + 1 : at + count, :] = block[1:count]
                else:
                    out[at : at + count, :] = block[:count]


def write_shards(plan, shards, hi0, blocks, fetched, buf, base, out_hbm, done, ends, sems):
    copies = []
    step = max(1, len(shards) // 4)
    for n, d in enumerate(shards):
        wait_shard(plan, d, hi0, blocks, fetched)
        put_rows(plan, [d], hi0, blocks, buf, base)
        if (n + 1) % step == 0 or n + 1 == len(shards):
            upto = ends(d)
            copies.append(pltpu.make_async_copy(
                buf.at[pl.ds(done - base, upto - done)], out_hbm.at[pl.ds(done, upto - done)], sems.at[len(copies)]
            ))
            copies[-1].start()
            done = upto
    return copies


def early_kernel(plan, own_s, near, far, out_hbm, edge_ref, blocks, buf, fetched, sems):
    rels = [(c, a, b) for c in range(2) for b in range(2) for a in range(plan.n_hi)]
    refs = [src.at[i] for src in (near, far) for i in range(2 * plan.n_hi)]
    fetch_blocks(plan, own_s, refs, rels, blocks, fetched)
    base = plan.cut - 8
    buf[0:8, :] = jnp.zeros((8, LANES), F32)
    copies = write_shards(
        plan, range(plan.early0, plan.n_dp), plan.quarter, blocks, fetched, buf, base, out_hbm, plan.cut,
        lambda d: ROW_SMALL if d + 1 == plan.n_dp else plan.row0[d + 1] // 8 * 8, sems,
    )
    edge_ref[...] = buf[0:8, :]
    for copy in copies:
        copy.wait()


def late_kernel(plan, own_s, refs, edge_ref, done_hbm, out_hbm, blocks, buf, tail, fetched, sems):
    rels = [(c, a, b) for c in range(2) for a in range(plan.n_hi) for b in range(2)]
    fetch_blocks(plan, own_s, refs, rels, blocks, fetched)

    def ends(d):
        if d + 1 < plan.early0:
            return plan.row0[d + 1] // 8 * 8
        at, lane0 = plan.row0[d + 1], plan.lane0[d + 1]
        if at < plan.cut:
            lane = lax.broadcasted_iota(jnp.int32, (1, LANES), 1)
            row = lax.broadcasted_iota(jnp.int32, (plan.cut - at, 1), 0)
            mine = buf[at : plan.cut, :]
            buf[at : plan.cut, :] = jnp.where((row == 0) & (lane < lane0), mine, edge_ref[at - plan.cut + 8 :, :])
        return plan.cut

    copies = write_shards(plan, range(plan.early0), 0, blocks, fetched, buf, 0, out_hbm, 0, ends, sems)
    small = blocks[0, 0, plan.helper % 2, plan.helper // 2, 0, plan.sub :, :].astype(F32)
    tail[...] = small[:SMALL_ROWS]
    copies.append(pltpu.make_async_copy(tail, out_hbm.at[pl.ds(ROW_SMALL, SMALL_ROWS)], sems.at[7]))
    copies[-1].start()
    for copy in copies:
        copy.wait()


def gradient_kernel(plan, own_s, same, cross, given, ctx_same, ctx_cross, *rest):
    ctx_far, (grad_ref, ctx_ref, grad) = rest[: plan.n_hi - 1], rest[plan.n_hi - 1 :]
    rows, stored = plan.shard_rows, ctx_ref.shape[0] // plan.n_group
    for a in range(plan.n_hi):
        back = lax.rem(own_s[2] + plan.n_hi - a, plan.n_hi) * 2
        ahead = lax.rem(own_s[2] + a, plan.n_hi) * 2
        for n, core in enumerate((own_s[1], 1 - own_s[1])):
            at = pl.multiple_of((back + core) * stored, 16)
            ctx_ref[pl.ds(at, stored), :] = ctx_far[a - 1][n] if a else (ctx_cross if n else ctx_same)[0]
            at = pl.multiple_of((ahead + core) * plan.piece, 16)
            grad[pl.ds(at, plan.piece), :] = (cross if n else same)[a].astype(F32)
    grad[rows:, :] = jnp.zeros((8, LANES), F32)

    @pl.when(own_s[7] == plan.n_dp - 1)
    def _():
        at = ROW_SMALL - plan.row0[-1]
        grad[at : at + SMALL_ROWS, :] = given[plan.sub :, :].astype(F32)[:SMALL_ROWS]

    lane = lax.broadcasted_iota(jnp.int32, (1, LANES), 1)
    back = LANES - own_s[5]
    for i in range(plan.n_group):
        at = slice(i * plan.piece, (i + 1) * plan.piece)
        turned = pltpu.roll(grad[i * plan.piece : (i + 1) * plan.piece + 8, :], back, 1)
        g = jnp.where(lane < back, turned[: plan.piece], turned[1 : plan.piece + 1])
        grad_ref[at, :] = g


def adam(weight, grad, one, two):
    first = 0.5 * one + 0.5 * grad
    second = 0.6 * two + 0.4 * grad * grad
    step = (first / (1.0 - 0.5**STEP)) / (jnp.sqrt(second / (1.0 - 0.6**STEP)) + 1e-08)
    return weight - 0.05 * (step + 0.05 * weight)


def after(value, *others):
    return lax.optimization_barrier((value, others))[0]


def build(mesh):
    n_dp, n_group = mesh.shape["dp"], mesh.shape["group"]
    plan = Plan(n_dp, n_group)
    both = ("dp", "group")
    n_hi, half, quarter = plan.n_hi, plan.half, plan.quarter
    piece, sub = plan.piece, plan.sub
    any_spec = pl.BlockSpec(memory_space=pl.ANY)
    brief = pl.CostEstimate(flops=0, bytes_accessed=0, transcendentals=0)
    params_of = pltpu.CompilerParams(vmem_limit_bytes=VMEM_CAP)

    def pairs(move):
        out = []
        for d in range(n_dp):
            for g in range(n_group):
                ghi, glo, dhi, dlo = move(g // 2, g % 2, d // 2, d % 2)
                out.append((d * n_group + g, (dhi * 2 + dlo) * n_group + ghi * 2 + glo))
        return out

    core_pairs = pairs(lambda gh, gl, dh, dl: (gh, 1 - gl, dh, dl))
    swap_pairs = pairs(lambda gh, gl, dh, dl: (gh, gl, (dh + quarter) % half, dl))

    def xy_pairs(a, b):
        return pairs(lambda gh, gl, dh, dl: ((gh + a) % n_hi, gl, dh, (dl + b) % 2))

    def z_pairs(r):
        return pairs(lambda gh, gl, dh, dl: (gh, gl, (dh + r) % half, dl))

    def group_pairs(r):
        return [(i, (i + r) % n_group) for i in range(n_group)]

    rels = [(a, b) for a in range(n_hi) for b in range(2)]
    def pick(array, index):
        return lax.dynamic_index_in_dim(array, index, 0, keepdims=False)

    def slot_of(h, early):
        return (h % quarter) * 2 + (h // quarter + early) % 2

    def xy_blocks(keep, got, gh, dl):
        def block(a, b):
            i, j = (gh + a) % n_hi, (dl + b) % 2
            mine, theirs = pick(pick(keep, i), j), pick(pick(got, i), j)
            return (mine.astype(F32) + theirs.astype(F32)).astype(BF16)
        return [block(a, b) for a, b in rels]

    def xy_send(blocks):
        return [lax.ppermute(x, both, xy_pairs(a, b)) for x, (a, b) in zip(blocks[1:], rels[1:])]

    def z_blocks(block, arrived, dh, early):
        total = block.astype(F32)
        for part in arrived:
            total = total + part.astype(F32)
        total = total.astype(BF16)
        total = total.reshape((2 * quarter,) + total.shape[2:])
        return [pick(total, slot_of((dh + r) % half, early)) for r in range(half)]

    def z_send(blocks):
        return [lax.ppermute(x, both, z_pairs(r)) for r, x in enumerate(blocks) if r]

    def z_sum(block, arrived):
        total = block.astype(F32)
        for part in arrived:
            total = total + part.astype(F32)
        return total

    def z_gather(mine):
        return [lax.ppermute(mine, both, z_pairs(r)) for r in range(1, half)]

    def z_order(got, sender, early):
        blocks = []
        for t in range(quarter):
            for n in range(2):
                want = (t + early * quarter + n * quarter) % half
                block = got[0]
                for i in range(1, half):
                    block = jnp.where(sender(i) == want, got[i], block)
                blocks.append(block)
        return jnp.stack(blocks).reshape((quarter, 2) + blocks[0].shape)

    def xy_gather(block):
        return [lax.ppermute(block, both, xy_pairs(-a, -b)) for a, b in rels[1:]]

    def core_gather(blocks):
        return [lax.ppermute(b, both, core_pairs) for b in blocks]

    def per_device(
        context, segment_ids, target_index, target_length, pos_table, params, first_moment, second_moment, cotangent
    ):
        stored = context.shape[0] // n_group
        dp, me = lax.axis_index("dp"), lax.axis_index("group")
        gh, gl, dh, dl = me // 2, me % 2, dp // 2, dp % 2
        share = plan.share

        ctx_got = [
            lax.ppermute(
                lax.dynamic_slice_in_dim(context, (me + r) % n_group * stored, stored), "group", group_pairs(r)
            )
            for r in range(1, n_group)
        ]

        lane0 = (dp * share) % LANES

        def own_row(early):
            t = dh % quarter + early * quarter
            n = (dh // quarter + early) % 2
            return ((t * 2 + dl) * share) // LANES + me * piece + n * sub

        own_s = jnp.stack(
            [0 * me, gl, gh, dl, me * piece, lane0, me, dp, own_row(0), own_row(1)]
        ).astype(jnp.int32)
        params2 = params.reshape(ROWS_ALL, LANES)

        weights = [((D_IN, D), BF16), ((D, 3 * D), BF16), ((D, D), BF16), ((D, FF), BF16), ((FF, D), BF16)]
        prep = pl.pallas_call(
            functools.partial(prep_kernel, plan),
            out_shape=[shape((8, D), F32), shape((2, sub, LANES), F32)]
            + [shape(*w) for w in weights] + [shape((TGT, D), F32)],
            in_specs=smem(1) + [any_spec] + vmem(2),
            out_specs=vmem(2) + [any_spec] * 6,
            scratch_shapes=[pltpu.VMEM((plan.flat_rows, LANES), F32)] + [pltpu.VMEM(*w) for w in weights] + [
                pltpu.VMEM((TGT, D), F32),
                pltpu.VMEM((TGT, GRID), F32),
                pltpu.SemaphoreType.DMA((6,)),
                pltpu.SemaphoreType.DMA((6,)),
            ],
            compiler_params=params_of,
        )(own_s, params2, target_index, pos_table)
        vec, own_w, w_in_b, w_qkv_b, w_out_b, w_up_b, w_down_b, target_rows = prep

        early_rows, late_rows = sub, sub + SMALL_PAD
        n_blocks = 2 * n_hi
        out_specs = [
            shape((8, D), F32),
            shape((n_hi, 2, quarter, 2, early_rows, LANES), BF16),
            shape((n_hi, 2, quarter, 2, early_rows, LANES), BF16),
            shape((8,), jnp.int32),
        ]
        saved = [
            ((CTX, D_IN), BF16),
            ((L, D), F32),
            ((L, 3 * D), F32),
            ((GROUPS * 3, CTX, PER * LANES), BF16),
            ((2 * IMG * BLOCKS, KEYS, WIDE), BF16),
            ((L, D), F32),
            ((L, D), F32),
        ]
        written = [
            ((L, D), BF16),
            ((plan.mid_rows, LANES), F32),
        ] + saved

        def forward(*refs):
            n = 2 + 2
            forward_kernel(plan, *refs[:n], refs[n : n + n_group - 1], *refs[n + n_group - 1 :])

        fwd = pl.pallas_call(
            forward,
            out_shape=out_specs + [shape(*s) for s in written],
            in_specs=smem(2) + vmem(2 + n_group - 1 + 1) + [any_spec] * 7,
            out_specs=vmem(3) + smem(1) + [any_spec] * len(written),
            scratch_shapes=[pltpu.VMEM(*w) for w in weights] + [pltpu.VMEM(*s) for s in saved[:5]] + [
                pltpu.VMEM((L, D), F32),
                pltpu.VMEM((L, D), BF16),
                pltpu.VMEM((L, D), F32),
                pltpu.VMEM((L, D), BF16),
                pltpu.VMEM((L, D), F32),
                pltpu.VMEM((L, D), BF16),
                pltpu.VMEM((CTX, CTX), F32),
                pltpu.VMEM((D, CTX), BF16),
                pltpu.VMEM((L, D), BF16),
                pltpu.VMEM((L, FF), BF16),
                pltpu.VMEM((L, FF), BF16),
                pltpu.VMEM((L, D), BF16),
                pltpu.VMEM((plan.flat_rows - ROW_OUT, LANES), F32),
                pltpu.VMEM((L, LANES), F32),
                pltpu.VMEM((L, D), BF16),
                pltpu.VMEM((L, D), BF16),
                pltpu.SemaphoreType.DMA((7,)),
                pltpu.SemaphoreType.DMA((len(written),)),
            ],
            compiler_params=params_of,
        )(
            target_length, own_s,
            vec, context, *ctx_got, segment_ids, cotangent[0],
            w_in_b, w_qkv_b, w_out_b, w_up_b, w_down_b, target_rows,
        )
        small_in, keep_e, send_e, seg_s, out, mid = fwd[: len(fwd) - len(saved)]
        ctx_s, stream_s, qkv_s, probs_c_s, probs_t_s, d_mixed_s, d_middle_s = fwd[len(fwd) - len(saved) :]

        got_e = lax.ppermute(send_e, both, core_pairs)
        spare = plan.shard_rows * LANES - share
        one2, two2 = [
            jnp.pad(m, (8 * LANES, spare)).reshape(8 + plan.shard_rows, LANES) for m in after((first_moment, second_moment), seg_s)
        ]

        xy_e = xy_blocks(keep_e, got_e, gh, dl)
        xy_got_e = xy_send(xy_e)
        qkv_s = after(qkv_s, *xy_e)

        dpk, own_mom, other_mom = pl.pallas_call(
            functools.partial(attention_back_kernel, plan),
            out_shape=[
                shape((L, 3 * D), BF16), shape((2, sub, LANES), F32), shape((2, sub + SMALL_PAD, LANES), F32),
            ],
            in_specs=smem(2) + [any_spec] * 6,
            out_specs=vmem(3),
            scratch_shapes=[pltpu.VMEM(*s) for s in saved[2:6]] + [
                pltpu.VMEM((L, 3 * D), F32),
                pltpu.VMEM((D, CTX), BF16),
                pltpu.VMEM((2, piece + 8, LANES), F32),
                pltpu.VMEM((2, 32, LANES), F32),
                pltpu.SemaphoreType.DMA((8,)),
            ],
            compiler_params=params_of,
            cost_estimate=pl.CostEstimate(flops=10**10, bytes_accessed=20 * 10**6, transcendentals=0),
        )(seg_s, own_s, qkv_s, probs_c_s, probs_t_s, d_mixed_s, one2, two2)

        xy_got_e = [after(x, dpk) for x in xy_got_e]
        z_e = z_blocks(xy_e[0], xy_got_e, dh, 1)
        z_got_e = z_send(z_e)
        swapped = lax.ppermute(other_mom, both, swap_pairs)
        dpk = after(dpk, *z_e)

        bwd_out = [
            shape((n_hi, 2, quarter, 2, late_rows, LANES), BF16),
            shape((n_hi, 2, quarter, 2, late_rows, LANES), BF16),
            shape((n_hi, stored, D_IN), BF16),
            shape((n_hi, stored, D_IN), BF16),
        ]
        bwd = pl.pallas_call(
            functools.partial(backward_kernel, plan),
            out_shape=bwd_out,
            in_specs=smem(1) + vmem(4) + [any_spec] * 5,
            out_specs=vmem(len(bwd_out)),
            scratch_shapes=[
                pltpu.VMEM((D_IN, D), BF16),
                pltpu.VMEM((D, 3 * D), BF16),
                pltpu.VMEM((CTX, D_IN), BF16),
                pltpu.VMEM((L, D), F32),
                pltpu.VMEM((L, D), F32),
                pltpu.VMEM((L, D), BF16),
                pltpu.VMEM((CTX, D), BF16),
                pltpu.VMEM((CTX, D_IN), BF16),
                pltpu.VMEM((SMALL_PAD, LANES), F32),
                pltpu.VMEM((ROW_OUT + plan.mid_rows, LANES), F32),
                pltpu.SemaphoreType.DMA((5,)),
            ],
            compiler_params=params_of,
            cost_estimate=pl.CostEstimate(flops=5 * 10**9, bytes_accessed=15 * 10**6, transcendentals=0),
        )(own_s, vec, small_in, mid, dpk, w_in_b, w_qkv_b, ctx_s, stream_s, d_middle_s)
        keep_l, send_l, ctx_same, ctx_cross = bwd

        upper = dh // quarter
        own_is_late = upper == 0

        def moments_of(early):
            return jnp.where(upper == early, own_mom, swapped[:, :sub])

        def all_after(values, *others):
            return [after(x, *others) for x in values]

        def joint(*groups):
            return lax.optimization_barrier(groups)

        z_got_e, swapped = joint(all_after(z_got_e, keep_l), after(swapped, keep_l))
        tails = swapped[:, sub:]
        got_l = lax.ppermute(after(send_l, *z_got_e), both, core_pairs)
        own_e = z_sum(z_e[0], z_got_e)
        mom = moments_of(1)
        new_e = adam(own_w[1], own_e, mom[0], mom[1]).astype(BF16)
        ctx_cross = lax.ppermute(after(ctx_cross, *z_got_e), both, core_pairs)
        got_l, ctx_cross, new_e = joint(got_l, ctx_cross, new_e)
        ctx_pairs = [jnp.stack([ctx_same[a], ctx_cross[a]]) for a in range(1, n_hi)]

        xy_l = xy_blocks(keep_l, got_l, gh, dl)
        xy_got_l, z_new_e, own_e = joint(xy_send(xy_l), z_gather(after(new_e, *xy_l)), own_e)

        z_l = z_blocks(xy_l[0], xy_got_l, dh, 0)
        block_e = z_order([new_e] + list(z_new_e), lambda i: (dh - i) % half, 1)[None]
        z_got_l, near_e, ctx_far = joint(
            z_send(z_l), [lax.ppermute(block_e, both, xy_pairs(-a, 0)) for a in range(1, n_hi)],
            [lax.ppermute(after(ctx_pairs[a - 1], *z_l), both, xy_pairs(a, 0)) for a in range(1, n_hi)],
        )
        own_l = z_sum(z_l[0], z_got_l)
        small_sum = own_l[sub:]
        small_w = jnp.pad(params[NP - SMALL :].reshape(SMALL_ROWS, LANES), ((0, SMALL_PAD - SMALL_ROWS), (0, 0)))
        mom = moments_of(0)
        new_l = jnp.concatenate([
            adam(own_w[0], own_l[:sub], mom[0], mom[1]), adam(small_w, small_sum, tails[0], tails[1])
        ]).astype(BF16)

        near_e = jnp.concatenate([block_e] + list(near_e))
        give = jnp.where(own_is_late, own_e, own_l[:sub])
        give = jnp.concatenate([give, small_sum]).astype(BF16)
        have = jnp.where(own_is_late, own_l[:sub], own_e).astype(BF16)
        z_new_l, y_near_e, taken = joint(
            z_gather(new_l), lax.ppermute(near_e, both, xy_pairs(0, 1)), lax.ppermute(give, both, swap_pairs)
        )

        block_l = z_order([new_l] + list(z_new_l), lambda i: (dh - i) % half, 0)
        near_e = jnp.concatenate([near_e, y_near_e])
        near_l = xy_gather(block_l)
        far_e = lax.ppermute(after(near_e, block_l), both, core_pairs)
        own = jnp.concatenate([have, taken[:sub]])
        quarters = jnp.stack(
            [own] + [lax.ppermute(after(own, block_l), both, xy_pairs(-a, 0)) for a in range(1, n_hi)]
        )
        other_quarters = lax.ppermute(quarters, both, core_pairs)

        n_parts = 2 * n_blocks
        base = plan.cut - 8

        half_done, edge = pl.pallas_call(
            functools.partial(early_kernel, plan),
            out_shape=[shape((ROWS_ALL, LANES), F32), shape((8, LANES), F32)],
            in_specs=smem(1) + [pl.BlockSpec(memory_space=pltpu.HBM)] * 2,
            out_specs=[any_spec, pl.BlockSpec(memory_space=pltpu.VMEM)],
            scratch_shapes=[
                pltpu.VMEM((2, n_hi, 2, quarter, 2, early_rows, LANES), BF16),
                pltpu.VMEM((plan.flat_rows - base, LANES), F32),
                pltpu.SemaphoreType.DMA((2, n_hi, 2, quarter)),
                pltpu.SemaphoreType.DMA((8,)),
            ],
            compiler_params=params_of,
            cost_estimate=brief,
        )(after(own_s, block_l), near_e, far_e)

        grad, context_grad = pl.pallas_call(
            functools.partial(gradient_kernel, plan),
            out_shape=[shape((plan.shard_rows, LANES), F32), shape(context.shape, BF16)],
            in_specs=smem(1) + vmem(5 + n_hi - 1),
            out_specs=vmem(2),
            scratch_shapes=[pltpu.VMEM((plan.shard_rows + 8, LANES), F32)],
            compiler_params=params_of,
            cost_estimate=brief,
        )(after(own_s, edge), quarters, other_quarters, taken, ctx_same, ctx_cross, *ctx_far)
        near_l, half_done, edge, grad = joint(near_l, half_done, edge, grad)
        near_l = [block_l] + list(near_l)
        all_l = near_l + core_gather(near_l)
        grad = grad.reshape(-1)[:share]
        new_first = 0.5 * first_moment + 0.5 * grad
        new_second = 0.6 * second_moment + 0.4 * grad * grad

        def late(own_ref, *refs):
            late_kernel(plan, own_ref, refs[:n_parts], *refs[n_parts:])

        new_params = pl.pallas_call(
            late,
            out_shape=shape((ROWS_ALL, LANES), F32),
            in_specs=smem(1) + [pl.BlockSpec(memory_space=pltpu.HBM)] * n_parts + vmem(1) + [any_spec],
            out_specs=any_spec,
            scratch_shapes=[
                pltpu.VMEM((2, n_hi, 2, quarter, 2, late_rows, LANES), BF16),
                pltpu.VMEM((plan.row0[plan.early0 - 1] + plan.shard_rows, LANES), F32),
                pltpu.VMEM((SMALL_ROWS, LANES), F32),
                pltpu.SemaphoreType.DMA((2, n_hi, 2, quarter)),
                pltpu.SemaphoreType.DMA((8,)),
            ],
            input_output_aliases={n_parts + 2: 0},
            compiler_params=params_of,
        )(after(own_s, new_first, new_second), *all_l, edge, half_done)

        return out[None], context_grad, new_params.reshape(-1), new_first, new_second

    return per_device


def solution(mesh):
    return jax.shard_map(
        build(mesh),
        mesh=mesh,
        in_specs=(
            P(("dp", "group"), None),
            P(("dp", "group"), None),
            P(("dp", "group"), None, None, None),
            P(("dp", "group"), None, None),
            P(),
            P(),
            P("dp"),
            P("dp"),
            P(("dp", "group"), None, None),
        ),
        out_specs=(P(("dp", "group"), None, None), P(("dp", "group"), None), P(), P("dp"), P("dp")),
        check_vma=False,
    )
```

profile of v0, /device:TPU:1, one launch (start us, length us, event | category | flops | bytes accessed | tf_op | source)
XLA Modules:
  0.0 172.0 jit_solution(12707242570855591426)
XLA Ops:
  0.7 1.1 constant_dynamic-slice_fusion
  1.8 2.7 %collective-permute-start = (bf16[96,768]{1,0:T(8,128)(2,1)S(1)}, bf16[96,768]{1,0:T(8,128)(2,1)S(1)}, u32[]{:S(2)}, u32[]{:S(2)}) collective-permute-start(bf16[96,768]{1,0:T(8,128)(2,1)S(1)} %get-tuple-element.183), channel_id=1, source_target_pairs={{0,1},{1,2},{2,3},{3,0},{4,5},{5,6},{6,7},{7,4},{8,9},{9,10},{10,1... | collective-permute-start | bytes 442376 | tf_op jit(solution)/shard_map/ppermute | solution.py:877
  5.6 7.5 %shard_map.128 = (f32[8,384]{1,0:T(8,128)}, f32[2,256,128]{2,1,0:T(8,128)}, bf16[768,384]{1,0:T(8,128)(2,1)}, bf16[384,1152]{1,0:T(8,128)(2,1)}, bf16[384,384]{1...) custom-call(s32[10]{0:T(128)} %stack.81.own_s.refs_1_.own_ref, ...), custom_call_target="tpu_custom_call" | custom-call | tf_op jit(solution)/shard_map/pallas_call | solution.py:896
  13.9 34.4 %shard_map.129 = (f32[8,384]{1,0:T(8,128)}, bf16[2,2,2,2,256,128]{5,4,3,2,1,0:T(8,128)(2,1)}, bf16[2,2,2,2,256,128]{5,4,3,2,1,0:T(8,128)(2,1)}, s32[8]{0:T(128)}...) custom-call(s32[1,4,4]{2,1,0:T(4,128)} %refs_0_.1, ...), custom_call_target="tpu_custom_call" | custom-call | tf_op jit(solution)/shard_map/pallas_call | solution.py:938
  48.3 1.4 collective-permute-start.3
  49.7 2.8 %pad_bitcast_fusion = (f32[2056,128]{1,0:T(8,128)}, f32[2056,128]{1,0:T(8,128)}) fusion(f32[258288]{0:T(1024)S(1)} %copy-done.1, f32[258288]{0:T(1024)} %param.15), kind=kLoop, calls=%fused_computation.1 | loop fusion | bytes 4171648 | tf_op jit(solution)/shard_map/reshape | solution.py:975
  52.5 1.1 fusion.7
  53.6 1.2 collective-permute-start.6
  54.8 1.2 collective-permute-start.5
  56.2 19.2 %shard_map.130 = (bf16[1024,1152]{1,0:T(8,128)(2,1)}, f32[2,256,128]{2,1,0:T(8,128)}, f32[2,272,128]{2,1,0:T(8,128)}) custom-call(s32[8]{0:T(128)} %get-tuple-element.96.seg_s, s32[10]{0:T(128)} %stack.81.own_s.refs_1_.own_ref, f32[1024,1152]{1,0:T(8,128)} %get-tuple-element.100.qkv_hbm, bf16[9,384,512]{2,1,0:T(8,128)(2,1)} %get-tuple-element.101.probs_c_hbm, ...), custom_call_target="tpu_custom_call" | custom-call | flops 10000000000 | bytes 20000000 | tf_op jit(solution)/shard_map/pallas_call | solution.py:982
  75.4 2.4 %collective-permute-start.10 = (f32[2,272,128]{2,1,0:T(8,128)}, f32[2,272,128]{2,1,0:T(8,128)S(1)}, u32[]{:S(2)}, u32[]{:S(2)}) collective-permute-start(f32[2,272,128]{2,1,0:T(8,128)} %get-tuple-element.121), channel_id=1, source_target_pairs={{0,16},{1,17},{2,18},{3,19},{4,20},{5,21},{6,22},{7,23},{8,24},{9,... | collective-permute-start | bytes 835592 | tf_op jit(solution)/shard_map/ppermute | solution.py:1003
  77.8 1.1 add_convert_fusion.5
  78.9 1.4 collective-permute-start.7
  80.3 2.1 %collective-permute-start.9 = (bf16[256,128]{1,0:T(8,128)(2,1)S(1)}, bf16[256,128]{1,0:T(8,128)(2,1)S(1)}, u32[]{:S(2)}, u32[]{:S(2)}) collective-permute-start(bf16[256,128]{1,0:T(8,128)(2,1)S(1)} %get-tuple-element.199), channel_id=1, source_target_pairs={{0,24},{1,25},{2,26},{3,27},{4,28},{5,29},{6,30},{7,31},{8,0},{9,1... | collective-permute-start | bytes 196616 | tf_op jit(solution)/shard_map/ppermute | solution.py:840
  82.4 11.3 %shard_map.131 = (bf16[2,2,2,2,272,128]{5,4,3,2,1,0:T(8,128)(2,1)}, bf16[2,2,2,2,272,128]{5,4,3,2,1,0:T(8,128)(2,1)}, bf16[2,96,768]{2,1,0:T(8,128)(2,1)}, bf16[2,96,768]{2,1,0:T(8,128)(2,1)}) custom-call(s32[10]{0:T(128)} %stack.81.own_s.refs_1_.own_ref, f32[8,384]{1,0:T(8,128)} %get-tuple-element.87.refs_2_.vec, f32[8,384]{1,0:T(8,128)} %get-tuple-element.111.small_in, ...), custom_call_target="tpu_custom_call" | custom-call | flops 5000000000 | bytes 15000000 | tf_op jit(solution)/shard_map/pallas_call | solution.py:1012
  94.3 2.3 %collective-permute-start.11 = (bf16[2,2,2,2,272,128]{5,4,3,2,1,0:T(8,128)(2,1)}, bf16[2,2,2,2,272,128]{5,4,3,2,1,0:T(8,128)(2,1)S(1)}, u32[]{:S(2)}, u32[]{:S(2)}) collective-permute-start(bf16[2,2,2,2,272,128]{5,4,3,2,1,0:T(8,128)(2,1)} %get-tuple-element.128), channel_id=1, source_target_pairs={{0,1},{1,0},{2,3},{3,2},{4,5},{5,4},{6,7},{7,6},{8,9},{9,8},{10,11... | collective-permute-start | bytes 3342344 | tf_op jit(solution)/shard_map/ppermute | solution.py:1049
  98.2 1.1 fusion.27
  99.7 1.1 fusion.1
  100.8 1.2 collective-permute-start.13
  102.3 1.2 collective-permute-start.15
  103.4 1.0 collective-permute-start.16
  104.5 3.2 %collective-permute-start.17 = (bf16[256,128]{1,0:T(8,128)(2,1)S(1)}, bf16[256,128]{1,0:T(8,128)(2,1)S(1)}, u32[]{:S(2)}, u32[]{:S(2)}) collective-permute-start(bf16[256,128]{1,0:T(8,128)(2,1)S(1)} %get-tuple-element.133), channel_id=1, source_target_pairs={{0,16},{1,17},{2,18},{3,19},{4,20},{5,21},{6,22},{7,23},{8,24},{9,... | collective-permute-start | bytes 196616 | tf_op jit(solution)/shard_map/ppermute | solution.py:849
  107.7 1.3 collective-permute-done.16
  109.0 1.7 %collective-permute-start.18 = (bf16[256,128]{1,0:T(8,128)(2,1)S(1)}, bf16[256,128]{1,0:T(8,128)(2,1)S(1)}, u32[]{:S(2)}, u32[]{:S(2)}) collective-permute-start(bf16[256,128]{1,0:T(8,128)(2,1)S(1)} %get-tuple-element.133), channel_id=1, source_target_pairs={{0,24},{1,25},{2,26},{3,27},{4,28},{5,29},{6,30},{7,31},{8,0},{9,1... | collective-permute-start | bytes 196616 | tf_op jit(solution)/shard_map/ppermute | solution.py:849
  110.8 1.9 %collective-permute-done.17 = bf16[256,128]{1,0:T(8,128)(2,1)S(1)} collective-permute-done((bf16[256,128]{1,0:T(8,128)(2,1)S(1)}, bf16[256,128]{1,0:T(8,128)(2,1)S(1)}, u32[]{:S(2)}, u32[]{:S(2)}) %collective-permute-start.17) | collective-permute-done | bytes 65568 | tf_op jit(solution)/shard_map/ppermute | solution.py:849
  113.5 2.2 %collective-permute-done.15 = bf16[2,2,272,128]{3,2,1,0:T(8,128)(2,1)S(1)} collective-permute-done((bf16[2,2,272,128]{3,2,1,0:T(8,128)(2,1)}, bf16[2,2,272,128]{3,2,1,0:T(8,128)(2,1)S(1)}, u32[]{:S(2)}, u32[]{:S(2)}) %collective-permute-start.15) | collective-permute-done | bytes 278560 | tf_op jit(solution)/shard_map/ppermute | solution.py:829
  116.3 1.3 collective-permute-start.22
  117.6 1.0 collective-permute-start.19
  118.6 3.2 %collective-permute-start.20 = (bf16[272,128]{1,0:T(8,128)(2,1)S(1)}, bf16[272,128]{1,0:T(8,128)(2,1)S(1)}, u32[]{:S(2)}, u32[]{:S(2)}) collective-permute-start(bf16[272,128]{1,0:T(8,128)(2,1)S(1)} %get-tuple-element.191), channel_id=1, source_target_pairs={{0,16},{1,17},{2,18},{3,19},{4,20},{5,21},{6,22},{7,23},{8,24},{9,... | collective-permute-start | bytes 208904 | tf_op jit(solution)/shard_map/ppermute | solution.py:840
  123.2 1.5 collective-permute-done.20
  124.7 1.7 %collective-permute-done.21 = bf16[272,128]{1,0:T(8,128)(2,1)S(1)} collective-permute-done((bf16[272,128]{1,0:T(8,128)(2,1)S(1)}, bf16[272,128]{1,0:T(8,128)(2,1)S(1)}, u32[]{:S(2)}, u32[]{:S(2)}) %collective-permute-start.21) | collective-permute-done | bytes 69664 | tf_op jit(solution)/shard_map/ppermute | solution.py:840
  126.4 2.1 %collective-permute-done.22 = bf16[1,2,2,256,128]{4,3,2,1,0:T(8,128)(2,1)S(1)} collective-permute-done((bf16[1,2,2,256,128]{4,3,2,1,0:T(8,128)(2,1)S(1)}, bf16[1,2,2,256,128]{4,3,2,1,0:T(8,128)(2,1)S(1)}, u32[]{:S(2)}, u32[]{:S(2)}) %collective-permute-start.22) | collective-permute-done | bytes 262176 | tf_op jit(solution)/shard_map/ppermute | solution.py:1063
  129.6 1.3 collective-permute-start.27
  130.9 1.1 collective-permute-start.24
  131.9 3.2 %collective-permute-start.25 = (bf16[272,128]{1,0:T(8,128)(2,1)S(1)}, bf16[272,128]{1,0:T(8,128)(2,1)S(1)}, u32[]{:S(2)}, u32[]{:S(2)}) collective-permute-start(bf16[272,128]{1,0:T(8,128)(2,1)S(1)} %pad_maximum_fusion.7), channel_id=1, source_target_pairs={{0,16},{1,17},{2,18},{3,19},{4,20},{5,21},{6,22},{7,23},{8,24},{9,... | collective-permute-start | bytes 208904 | tf_op jit(solution)/shard_map/ppermute | solution.py:849
  135.1 1.3 collective-permute-start.28
  136.6 1.5 collective-permute-done.25
  139.0 3.6 %collective-permute-done.28.given = bf16[272,128]{1,0:T(8,128)(2,1)S(1)} collective-permute-done((bf16[272,128]{1,0:T(8,128)(2,1)S(1)}, bf16[272,128]{1,0:T(8,128)(2,1)S(1)}, u32[]{:S(2)}, u32[]{:S(2)}) %collective-permute-start.28) | collective-permute-done | bytes 69664 | tf_op jit(solution)/shard_map/ppermute | solution.py:1079
  143.0 2.8 %collective-permute-start.29 = (bf16[4,2,2,256,128]{4,3,2,1,0:T(8,128)(2,1)S(1)}, bf16[4,2,2,256,128]{4,3,2,1,0:T(8,128)(2,1)S(1)}, u32[]{:S(2)}, u32[]{:S(2)}) collective-permute-start(bf16[4,2,2,256,128]{4,3,2,1,0:T(8,128)(2,1)S(1)} %pad_maximum_fusion.near), channel_id=1, source_target_pairs={{0,1},{1,0},{2,3},{3,2},{4,5},{5,4},{6,7},{7,6},{8,9},{9,8},{10,11... | collective-permute-start | bytes 3145736 | tf_op jit(solution)/shard_map/ppermute | solution.py:1085
  146.4 1.2 collective-permute-start.33
  147.6 1.2 collective-permute-start.34
  148.8 2.1 %collective-permute-done.30 = bf16[512,128]{1,0:T(8,128)(2,1)S(1)} collective-permute-done((bf16[512,128]{1,0:T(8,128)(2,1)S(1)}, bf16[512,128]{1,0:T(8,128)(2,1)S(1)}, u32[]{:S(2)}, u32[]{:S(2)}) %collective-permute-start.30) | collective-permute-done | bytes 131104 | tf_op jit(solution)/shard_map/ppermute | solution.py:1088
  151.6 1.6 collective-permute-start.31
  154.2 4.9 %shard_map.132 = (f32[16143,128]{1,0:T(8,128)}, f32[8,128]{1,0:T(8,128)}) custom-call(s32[10]{0:T(128)} %stack.81.own_s.refs_1_.own_ref, bf16[4,2,2,256,128]{4,3,2,1,0:T(8,128)(2,1)} %copy-done, bf16[4,2,2,256,128]{4,3,2,1,0:T(8,128)(2,1)} %copy-done.5), custom_call_target="tpu_custom_call" | custom-call | tf_op jit(solution)/shard_map/pallas_call | solution.py:1095
  159.1 2.9 %shard_map.133 = (f32[2048,128]{1,0:T(8,128)}, bf16[384,768]{1,0:T(8,128)(2,1)}) custom-call(s32[10]{0:T(128)} %stack.81.own_s.refs_1_.own_ref, bf16[2,512,128]{2,1,0:T(8,128)(2,1)} %pad_maximum_fusion.5.same, bf16[2,512,128]{2,1,0:T(8,128)(2,1)} %collective-permute-done.31.cross, bf16[272,128]{1,0:T(8,128)(2,1)} %copy-done.11, ...), custom_call_target="tpu_custom_call" | custom-call | tf_op jit(solution)/shard_map/pallas_call | solution.py:1110
  162.7 1.0 collective-permute-start.36
  164.3 3.1 %fusion = (f32[258288]{0:T(1024)}, f32[258288]{0:T(1024)}) fusion(f32[258288]{0:T(1024)S(1)} %copy-done.2, f32[262144]{0:T(1024)} %bitcast.149, f32[258288]{0:T(1024)} %param.15), kind=kLoop, calls=%fused_computation.4 | loop fusion | flops 1549728 | bytes 5165760 | tf_op jit(solution)/shard_map/add | solution.py:1124
  167.4 4.5 %shard_map.134 = f32[16143,128]{1,0:T(8,128)} custom-call(s32[10]{0:T(128)} %stack.81.own_s.refs_1_.own_ref, bf16[2,2,272,128]{3,2,1,0:T(8,128)(2,1)} %bitcast.147, bf16[2,2,272,128]{3,2,1,0:T(8,128)(2,1)} %collective-permute-done.32.refs_1_, bf16[2,2,272,128]{3,2,1,0:T(8,128)(2,1)} %collective-permute-done.33.refs_2_, ...), custom_call_target="tpu_custom_call", output_to_operand_aliasing={{}: (10, {})} | custom-call | tf_op jit(solution)/shard_map/pallas_call | solution.py:1129
  (108 shorter events, 13.7 us)
Async XLA Ops:
  1.8 11.4 %collective-permute-start = (bf16[96,768]{1,0:T(8,128)(2,1)S(1)}, bf16[96,768]{1,0:T(8,128)(2,1)S(1)}, u32[]{:S(2)}, u32[]{:S(2)}) collective-permute-start(bf16[96,768]{1,0:T(8,128)(2,1)S(1)} %get-tuple-element.183), channel_id=1, source_target_pairs={{0,1},{1,2},{2,3},{3,0},{4,5},{5,6},{6,7},{7,4},{8,9},{9,10},{10,1... | collective-permute-start | bytes 442376 | tf_op jit(solution)/shard_map/ppermute | solution.py:877
  4.4 8.7 %collective-permute-start.1 = (bf16[96,768]{1,0:T(8,128)(2,1)S(1)}, bf16[96,768]{1,0:T(8,128)(2,1)S(1)}, u32[]{:S(2)}, u32[]{:S(2)}) collective-permute-start(bf16[96,768]{1,0:T(8,128)(2,1)S(1)} %get-tuple-element.182), channel_id=1, source_target_pairs={{0,2},{1,3},{2,0},{3,1},{4,6},{5,7},{6,4},{7,5},{8,10},{9,11},{10,... | collective-permute-start | bytes 442376 | tf_op jit(solution)/shard_map/ppermute | solution.py:877
  4.4 8.7 %collective-permute-start.2 = (bf16[96,768]{1,0:T(8,128)(2,1)S(1)}, bf16[96,768]{1,0:T(8,128)(2,1)S(1)}, u32[]{:S(2)}, u32[]{:S(2)}) collective-permute-start(bf16[96,768]{1,0:T(8,128)(2,1)S(1)} %get-tuple-element.181), channel_id=1, source_target_pairs={{0,3},{1,0},{2,1},{3,2},{4,7},{5,4},{6,5},{7,6},{8,11},{9,8},{10,9... | collective-permute-start | bytes 442376 | tf_op jit(solution)/shard_map/ppermute | solution.py:877
  13.9 35.8 %copy-start.1 = (f32[258288]{0:T(1024)S(1)}, f32[258288]{0:T(1024)}, u32[]{:S(2)}) copy-start(f32[258288]{0:T(1024)} %param.16) | copy-start | bytes 3099460
  48.3 4.2 %collective-permute-start.3 = (bf16[2,2,2,2,256,128]{5,4,3,2,1,0:T(8,128)(2,1)}, bf16[2,2,2,2,256,128]{5,4,3,2,1,0:T(8,128)(2,1)S(1)}, u32[]{:S(2)}, u32[]{:S(2)}) collective-permute-start(bf16[2,2,2,2,256,128]{5,4,3,2,1,0:T(8,128)(2,1)} %get-tuple-element.99), channel_id=1, source_target_pairs={{0,1},{1,0},{2,3},{3,2},{4,5},{5,4},{6,7},{7,6},{8,9},{9,8},{10,11... | collective-permute-start | bytes 3145736 | tf_op jit(solution)/shard_map/ppermute | solution.py:972
  53.6 24.2 %collective-permute-start.6 = (bf16[2,2,256,128]{3,2,1,0:T(8,128)(2,1)}, bf16[2,2,256,128]{3,2,1,0:T(8,128)(2,1)S(1)}, u32[]{:S(2)}, u32[]{:S(2)}) collective-permute-start(bf16[2,2,256,128]{3,2,1,0:T(8,128)(2,1)} %get-tuple-element.176), channel_id=1, source_target_pairs={{0,6},{1,7},{2,4},{3,5},{4,2},{5,3},{6,0},{7,1},{8,14},{9,15},{10,... | collective-permute-start | bytes 786440 | tf_op jit(solution)/shard_map/ppermute | solution.py:829
  54.8 23.0 %collective-permute-start.5 = (bf16[2,2,256,128]{3,2,1,0:T(8,128)(2,1)}, bf16[2,2,256,128]{3,2,1,0:T(8,128)(2,1)S(1)}, u32[]{:S(2)}, u32[]{:S(2)}) collective-permute-start(bf16[2,2,256,128]{3,2,1,0:T(8,128)(2,1)} %get-tuple-element.175), channel_id=1, source_target_pairs={{0,2},{1,3},{2,0},{3,1},{4,6},{5,7},{6,4},{7,5},{8,10},{9,11},{10,... | collective-permute-start | bytes 786440 | tf_op jit(solution)/shard_map/ppermute | solution.py:829
  56.0 21.8 %collective-permute-start.4 = (bf16[2,2,256,128]{3,2,1,0:T(8,128)(2,1)}, bf16[2,2,256,128]{3,2,1,0:T(8,128)(2,1)}, u32[]{:S(2)}, u32[]{:S(2)}) collective-permute-start(bf16[2,2,256,128]{3,2,1,0:T(8,128)(2,1)} %get-tuple-element.177), channel_id=1, source_target_pairs={{0,4},{1,5},{2,6},{3,7},{4,0},{5,1},{6,2},{7,3},{8,12},{9,13},{10,... | collective-permute-start | bytes 786440 | tf_op jit(solution)/shard_map/ppermute | solution.py:829
  75.4 18.4 %collective-permute-start.10 = (f32[2,272,128]{2,1,0:T(8,128)}, f32[2,272,128]{2,1,0:T(8,128)S(1)}, u32[]{:S(2)}, u32[]{:S(2)}) collective-permute-start(f32[2,272,128]{2,1,0:T(8,128)} %get-tuple-element.121), channel_id=1, source_target_pairs={{0,16},{1,17},{2,18},{3,19},{4,20},{5,21},{6,22},{7,23},{8,24},{9,... | collective-permute-start | bytes 835592 | tf_op jit(solution)/shard_map/ppermute | solution.py:1003
  78.9 14.9 %collective-permute-start.7 = (bf16[256,128]{1,0:T(8,128)(2,1)S(1)}, bf16[256,128]{1,0:T(8,128)(2,1)S(1)}, u32[]{:S(2)}, u32[]{:S(2)}) collective-permute-start(bf16[256,128]{1,0:T(8,128)(2,1)S(1)} %get-tuple-element.202), channel_id=1, source_target_pairs={{0,8},{1,9},{2,10},{3,11},{4,12},{5,13},{6,14},{7,15},{8,16},{9,17... | collective-permute-start | bytes 196616 | tf_op jit(solution)/shard_map/ppermute | solution.py:840
  80.3 14.0 %collective-permute-start.8 = (bf16[256,128]{1,0:T(8,128)(2,1)S(1)}, bf16[256,128]{1,0:T(8,128)(2,1)S(1)}, u32[]{:S(2)}, u32[]{:S(2)}) collective-permute-start(bf16[256,128]{1,0:T(8,128)(2,1)S(1)} %get-tuple-element.200), channel_id=1, source_target_pairs={{0,16},{1,17},{2,18},{3,19},{4,20},{5,21},{6,22},{7,23},{8,24},{9,... | collective-permute-start | bytes 196616 | tf_op jit(solution)/shard_map/ppermute | solution.py:840
  80.3 14.0 %collective-permute-start.9 = (bf16[256,128]{1,0:T(8,128)(2,1)S(1)}, bf16[256,128]{1,0:T(8,128)(2,1)S(1)}, u32[]{:S(2)}, u32[]{:S(2)}) collective-permute-start(bf16[256,128]{1,0:T(8,128)(2,1)S(1)} %get-tuple-element.199), channel_id=1, source_target_pairs={{0,24},{1,25},{2,26},{3,27},{4,28},{5,29},{6,30},{7,31},{8,0},{9,1... | collective-permute-start | bytes 196616 | tf_op jit(solution)/shard_map/ppermute | solution.py:840
  93.8 5.8 %copy-start.3 = (bf16[2,2,2,2,272,128]{5,4,3,2,1,0:T(8,128)(2,1)S(1)}, bf16[2,2,2,2,272,128]{5,4,3,2,1,0:T(8,128)(2,1)}, u32[]{:S(2)}) copy-start(bf16[2,2,2,2,272,128]{5,4,3,2,1,0:T(8,128)(2,1)} %get-tuple-element.117) | copy-start | bytes 3342340
  93.8 5.8 %copy-start.10 = (f32[2,272,128]{2,1,0:T(8,128)}, f32[2,272,128]{2,1,0:T(8,128)S(1)}, u32[]{:S(2)}) copy-start(f32[2,272,128]{2,1,0:T(8,128)S(1)} %collective-permute-done.10) | copy-start | bytes 835588
  94.3 5.3 %collective-permute-start.11 = (bf16[2,2,2,2,272,128]{5,4,3,2,1,0:T(8,128)(2,1)}, bf16[2,2,2,2,272,128]{5,4,3,2,1,0:T(8,128)(2,1)S(1)}, u32[]{:S(2)}, u32[]{:S(2)}) collective-permute-start(bf16[2,2,2,2,272,128]{5,4,3,2,1,0:T(8,128)(2,1)} %get-tuple-element.128), channel_id=1, source_target_pairs={{0,1},{1,0},{2,3},{3,2},{4,5},{5,4},{6,7},{7,6},{8,9},{9,8},{10,11... | collective-permute-start | bytes 3342344 | tf_op jit(solution)/shard_map/ppermute | solution.py:1049
  96.6 3.0 %collective-permute-start.12 = (bf16[2,96,768]{2,1,0:T(8,128)(2,1)}, bf16[2,96,768]{2,1,0:T(8,128)(2,1)S(1)}, u32[]{:S(2)}, u32[]{:S(2)}) collective-permute-start(bf16[2,96,768]{2,1,0:T(8,128)(2,1)} %get-tuple-element.130), channel_id=1, source_target_pairs={{0,1},{1,0},{2,3},{3,2},{4,5},{5,4},{6,7},{7,6},{8,9},{9,8},{10,11... | collective-permute-start | bytes 884744 | tf_op jit(solution)/shard_map/ppermute | solution.py:1053
  99.6 8.1 %copy-start.8 = (bf16[2,96,768]{2,1,0:T(8,128)(2,1)}, bf16[2,96,768]{2,1,0:T(8,128)(2,1)S(1)}, u32[]{:S(2)}) copy-start(bf16[2,96,768]{2,1,0:T(8,128)(2,1)S(1)} %collective-permute-done.12.ctx_cross) | copy-start | bytes 884740
  100.8 12.7 %collective-permute-start.13 = (bf16[2,2,272,128]{3,2,1,0:T(8,128)(2,1)}, bf16[2,2,272,128]{3,2,1,0:T(8,128)(2,1)S(1)}, u32[]{:S(2)}, u32[]{:S(2)}) collective-permute-start(bf16[2,2,272,128]{3,2,1,0:T(8,128)(2,1)} %get-tuple-element.174), channel_id=1, source_target_pairs={{0,4},{1,5},{2,6},{3,7},{4,0},{5,1},{6,2},{7,3},{8,12},{9,13},{10,... | collective-permute-start | bytes 835592 | tf_op jit(solution)/shard_map/ppermute | solution.py:829
  102.0 11.5 %collective-permute-start.14 = (bf16[2,2,272,128]{3,2,1,0:T(8,128)(2,1)}, bf16[2,2,272,128]{3,2,1,0:T(8,128)(2,1)S(1)}, u32[]{:S(2)}, u32[]{:S(2)}) collective-permute-start(bf16[2,2,272,128]{3,2,1,0:T(8,128)(2,1)} %get-tuple-element.173), channel_id=1, source_target_pairs={{0,2},{1,3},{2,0},{3,1},{4,6},{5,7},{6,4},{7,5},{8,10},{9,11},{10,... | collective-permute-start | bytes 835592 | tf_op jit(solution)/shard_map/ppermute | solution.py:829
  102.3 13.4 %collective-permute-start.15 = (bf16[2,2,272,128]{3,2,1,0:T(8,128)(2,1)}, bf16[2,2,272,128]{3,2,1,0:T(8,128)(2,1)S(1)}, u32[]{:S(2)}, u32[]{:S(2)}) collective-permute-start(bf16[2,2,272,128]{3,2,1,0:T(8,128)(2,1)} %get-tuple-element.172), channel_id=1, source_target_pairs={{0,6},{1,7},{2,4},{3,5},{4,2},{5,3},{6,0},{7,1},{8,14},{9,15},{10,... | collective-permute-start | bytes 835592 | tf_op jit(solution)/shard_map/ppermute | solution.py:829
  103.4 5.6 %collective-permute-start.16 = (bf16[256,128]{1,0:T(8,128)(2,1)S(1)}, bf16[256,128]{1,0:T(8,128)(2,1)S(1)}, u32[]{:S(2)}, u32[]{:S(2)}) collective-permute-start(bf16[256,128]{1,0:T(8,128)(2,1)S(1)} %get-tuple-element.133), channel_id=1, source_target_pairs={{0,8},{1,9},{2,10},{3,11},{4,12},{5,13},{6,14},{7,15},{8,16},{9,17... | collective-permute-start | bytes 196616 | tf_op jit(solution)/shard_map/ppermute | solution.py:849
  104.5 8.2 %collective-permute-start.17 = (bf16[256,128]{1,0:T(8,128)(2,1)S(1)}, bf16[256,128]{1,0:T(8,128)(2,1)S(1)}, u32[]{:S(2)}, u32[]{:S(2)}) collective-permute-start(bf16[256,128]{1,0:T(8,128)(2,1)S(1)} %get-tuple-element.133), channel_id=1, source_target_pairs={{0,16},{1,17},{2,18},{3,19},{4,20},{5,21},{6,22},{7,23},{8,24},{9,... | collective-permute-start | bytes 196616 | tf_op jit(solution)/shard_map/ppermute | solution.py:849
  109.0 4.5 %collective-permute-start.18 = (bf16[256,128]{1,0:T(8,128)(2,1)S(1)}, bf16[256,128]{1,0:T(8,128)(2,1)S(1)}, u32[]{:S(2)}, u32[]{:S(2)}) collective-permute-start(bf16[256,128]{1,0:T(8,128)(2,1)S(1)} %get-tuple-element.133), channel_id=1, source_target_pairs={{0,24},{1,25},{2,26},{3,27},{4,28},{5,29},{6,30},{7,31},{8,0},{9,1... | collective-permute-start | bytes 196616 | tf_op jit(solution)/shard_map/ppermute | solution.py:849
  115.8 13.6 %copy-start.12 = (f32[2,256,128]{2,1,0:T(8,128)S(1)}, f32[2,256,128]{2,1,0:T(8,128)}, u32[]{:S(2)}) copy-start(f32[2,256,128]{2,1,0:T(8,128)} %get-tuple-element.95) | copy-start | bytes 786436
  115.9 12.7 %collective-permute-start.23 = (bf16[2,96,768]{2,1,0:T(8,128)(2,1)S(1)}, bf16[2,96,768]{2,1,0:T(8,128)(2,1)S(1)}, u32[]{:S(2)}, u32[]{:S(2)}) collective-permute-start(bf16[2,96,768]{2,1,0:T(8,128)(2,1)S(1)} %pad_maximum_fusion.2), channel_id=1, source_target_pairs={{0,2},{1,3},{2,0},{3,1},{4,6},{5,7},{6,4},{7,5},{8,10},{9,11},{10,... | collective-permute-start | bytes 884744 | tf_op jit(solution)/shard_map/ppermute | solution.py:1064
  116.3 12.3 %collective-permute-start.22 = (bf16[1,2,2,256,128]{4,3,2,1,0:T(8,128)(2,1)S(1)}, bf16[1,2,2,256,128]{4,3,2,1,0:T(8,128)(2,1)S(1)}, u32[]{:S(2)}, u32[]{:S(2)}) collective-permute-start(bf16[1,2,2,256,128]{4,3,2,1,0:T(8,128)(2,1)S(1)} %bitcast.139), channel_id=1, source_target_pairs={{0,2},{1,3},{2,0},{3,1},{4,6},{5,7},{6,4},{7,5},{8,10},{9,11},{10,... | collective-permute-start | bytes 786440 | tf_op jit(solution)/shard_map/ppermute | solution.py:1063
  117.6 5.7 %collective-permute-start.19 = (bf16[272,128]{1,0:T(8,128)(2,1)S(1)}, bf16[272,128]{1,0:T(8,128)(2,1)S(1)}, u32[]{:S(2)}, u32[]{:S(2)}) collective-permute-start(bf16[272,128]{1,0:T(8,128)(2,1)S(1)} %get-tuple-element.192), channel_id=1, source_target_pairs={{0,8},{1,9},{2,10},{3,11},{4,12},{5,13},{6,14},{7,15},{8,16},{9,17... | collective-permute-start | bytes 208904 | tf_op jit(solution)/shard_map/ppermute | solution.py:840
  118.6 6.1 %collective-permute-start.20 = (bf16[272,128]{1,0:T(8,128)(2,1)S(1)}, bf16[272,128]{1,0:T(8,128)(2,1)S(1)}, u32[]{:S(2)}, u32[]{:S(2)}) collective-permute-start(bf16[272,128]{1,0:T(8,128)(2,1)S(1)} %get-tuple-element.191), channel_id=1, source_target_pairs={{0,16},{1,17},{2,18},{3,19},{4,20},{5,21},{6,22},{7,23},{8,24},{9,... | collective-permute-start | bytes 208904 | tf_op jit(solution)/shard_map/ppermute | solution.py:840
  121.8 4.7 %collective-permute-start.21 = (bf16[272,128]{1,0:T(8,128)(2,1)S(1)}, bf16[272,128]{1,0:T(8,128)(2,1)S(1)}, u32[]{:S(2)}, u32[]{:S(2)}) collective-permute-start(bf16[272,128]{1,0:T(8,128)(2,1)S(1)} %get-tuple-element.190), channel_id=1, source_target_pairs={{0,24},{1,25},{2,26},{3,27},{4,28},{5,29},{6,30},{7,31},{8,0},{9,1... | collective-permute-start | bytes 208904 | tf_op jit(solution)/shard_map/ppermute | solution.py:840
  128.5 6.6 %copy-start.9 = (bf16[2,96,768]{2,1,0:T(8,128)(2,1)}, bf16[2,96,768]{2,1,0:T(8,128)(2,1)S(1)}, u32[]{:S(2)}) copy-start(bf16[2,96,768]{2,1,0:T(8,128)(2,1)S(1)} %collective-permute-done.23.rest_0_) | copy-start | bytes 884740
  129.6 13.1 %collective-permute-start.27 = (bf16[2,2,2,256,128]{4,3,2,1,0:T(8,128)(2,1)S(1)}, bf16[2,2,2,256,128]{4,3,2,1,0:T(8,128)(2,1)S(1)}, u32[]{:S(2)}, u32[]{:S(2)}) collective-permute-start(bf16[2,2,2,256,128]{4,3,2,1,0:T(8,128)(2,1)S(1)} %pad_maximum_fusion.1), channel_id=1, source_target_pairs={{0,4},{1,5},{2,6},{3,7},{4,0},{5,1},{6,2},{7,3},{8,12},{9,13},{10,... | collective-permute-start | bytes 1572872 | tf_op jit(solution)/shard_map/ppermute | solution.py:1079
  130.9 5.7 %collective-permute-start.24 = (bf16[272,128]{1,0:T(8,128)(2,1)S(1)}, bf16[272,128]{1,0:T(8,128)(2,1)S(1)}, u32[]{:S(2)}, u32[]{:S(2)}) collective-permute-start(bf16[272,128]{1,0:T(8,128)(2,1)S(1)} %pad_maximum_fusion.7), channel_id=1, source_target_pairs={{0,8},{1,9},{2,10},{3,11},{4,12},{5,13},{6,14},{7,15},{8,16},{9,17... | collective-permute-start | bytes 208904 | tf_op jit(solution)/shard_map/ppermute | solution.py:849
  131.9 6.1 %collective-permute-start.25 = (bf16[272,128]{1,0:T(8,128)(2,1)S(1)}, bf16[272,128]{1,0:T(8,128)(2,1)S(1)}, u32[]{:S(2)}, u32[]{:S(2)}) collective-permute-start(bf16[272,128]{1,0:T(8,128)(2,1)S(1)} %pad_maximum_fusion.7), channel_id=1, source_target_pairs={{0,16},{1,17},{2,18},{3,19},{4,20},{5,21},{6,22},{7,23},{8,24},{9,... | collective-permute-start | bytes 208904 | tf_op jit(solution)/shard_map/ppermute | solution.py:849
  135.1 4.0 %collective-permute-start.26 = (bf16[272,128]{1,0:T(8,128)(2,1)S(1)}, bf16[272,128]{1,0:T(8,128)(2,1)S(1)}, u32[]{:S(2)}, u32[]{:S(2)}) collective-permute-start(bf16[272,128]{1,0:T(8,128)(2,1)S(1)} %pad_maximum_fusion.7), channel_id=1, source_target_pairs={{0,24},{1,25},{2,26},{3,27},{4,28},{5,29},{6,30},{7,31},{8,0},{9,1... | collective-permute-start | bytes 208904 | tf_op jit(solution)/shard_map/ppermute | solution.py:849
  135.1 7.5 %collective-permute-start.28 = (bf16[272,128]{1,0:T(8,128)(2,1)S(1)}, bf16[272,128]{1,0:T(8,128)(2,1)S(1)}, u32[]{:S(2)}, u32[]{:S(2)}) collective-permute-start(bf16[272,128]{1,0:T(8,128)(2,1)S(1)} %pad_maximum_fusion.8), channel_id=1, source_target_pairs={{0,16},{1,17},{2,18},{3,19},{4,20},{5,21},{6,22},{7,23},{8,24},{9,... | collective-permute-start | bytes 208904 | tf_op jit(solution)/shard_map/ppermute | solution.py:1079
  142.9 11.2 %copy-start = (bf16[4,2,2,256,128]{4,3,2,1,0:T(8,128)(2,1)}, bf16[4,2,2,256,128]{4,3,2,1,0:T(8,128)(2,1)S(1)}, u32[]{:S(2)}) copy-start(bf16[4,2,2,256,128]{4,3,2,1,0:T(8,128)(2,1)S(1)} %pad_maximum_fusion.near) | copy-start | bytes 3145732
  143.0 16.1 %copy-start.4 = (bf16[4,272,128]{2,1,0:T(8,128)(2,1)}, bf16[4,272,128]{2,1,0:T(8,128)(2,1)S(1)}, u32[]{:S(2)}) copy-start(bf16[4,272,128]{2,1,0:T(8,128)(2,1)S(1)} %pad_maximum_fusion.3) | copy-start | bytes 835588
  143.0 10.2 %collective-permute-start.29 = (bf16[4,2,2,256,128]{4,3,2,1,0:T(8,128)(2,1)S(1)}, bf16[4,2,2,256,128]{4,3,2,1,0:T(8,128)(2,1)S(1)}, u32[]{:S(2)}, u32[]{:S(2)}) collective-permute-start(bf16[4,2,2,256,128]{4,3,2,1,0:T(8,128)(2,1)S(1)} %pad_maximum_fusion.near), channel_id=1, source_target_pairs={{0,1},{1,0},{2,3},{3,2},{4,5},{5,4},{6,7},{7,6},{8,9},{9,8},{10,11... | collective-permute-start | bytes 3145736 | tf_op jit(solution)/shard_map/ppermute | solution.py:1085
  145.8 5.1 %collective-permute-start.30 = (bf16[512,128]{1,0:T(8,128)(2,1)S(1)}, bf16[512,128]{1,0:T(8,128)(2,1)S(1)}, u32[]{:S(2)}, u32[]{:S(2)}) collective-permute-start(bf16[512,128]{1,0:T(8,128)(2,1)S(1)} %get-tuple-element.157), channel_id=1, source_target_pairs={{0,2},{1,3},{2,0},{3,1},{4,6},{5,7},{6,4},{7,5},{8,10},{9,11},{10,... | collective-permute-start | bytes 393224 | tf_op jit(solution)/shard_map/ppermute | solution.py:1088
  146.1 15.9 %collective-permute-start.32 = (bf16[2,2,272,128]{3,2,1,0:T(8,128)(2,1)S(1)}, bf16[2,2,272,128]{3,2,1,0:T(8,128)(2,1)}, u32[]{:S(2)}, u32[]{:S(2)}) collective-permute-start(bf16[2,2,272,128]{3,2,1,0:T(8,128)(2,1)S(1)} %bitcast.143), channel_id=1, source_target_pairs={{0,4},{1,5},{2,6},{3,7},{4,0},{5,1},{6,2},{7,3},{8,12},{9,13},{10,... | collective-permute-start | bytes 835592 | tf_op jit(solution)/shard_map/ppermute | solution.py:863
  146.4 15.6 %collective-permute-start.33 = (bf16[2,2,272,128]{3,2,1,0:T(8,128)(2,1)S(1)}, bf16[2,2,272,128]{3,2,1,0:T(8,128)(2,1)}, u32[]{:S(2)}, u32[]{:S(2)}) collective-permute-start(bf16[2,2,272,128]{3,2,1,0:T(8,128)(2,1)S(1)} %bitcast.144), channel_id=1, source_target_pairs={{0,2},{1,3},{2,0},{3,1},{4,6},{5,7},{6,4},{7,5},{8,10},{9,11},{10,... | collective-permute-start | bytes 835592 | tf_op jit(solution)/shard_map/ppermute | solution.py:863
  147.6 15.2 %collective-permute-start.34 = (bf16[2,2,272,128]{3,2,1,0:T(8,128)(2,1)S(1)}, bf16[2,2,272,128]{3,2,1,0:T(8,128)(2,1)}, u32[]{:S(2)}, u32[]{:S(2)}) collective-permute-start(bf16[2,2,272,128]{3,2,1,0:T(8,128)(2,1)S(1)} %bitcast.145), channel_id=1, source_target_pairs={{0,6},{1,7},{2,4},{3,5},{4,2},{5,3},{6,0},{7,1},{8,14},{9,15},{10,... | collective-permute-start | bytes 835592 | tf_op jit(solution)/shard_map/ppermute | solution.py:863
  151.6 7.5 %collective-permute-start.31 = (bf16[2,512,128]{2,1,0:T(8,128)(2,1)}, bf16[2,512,128]{2,1,0:T(8,128)(2,1)}, u32[]{:S(2)}, u32[]{:S(2)}) collective-permute-start(bf16[2,512,128]{2,1,0:T(8,128)(2,1)} %pad_maximum_fusion.5.same), channel_id=1, source_target_pairs={{0,1},{1,0},{2,3},{3,2},{4,5},{5,4},{6,7},{7,6},{8,9},{9,8},{10,11... | collective-permute-start | bytes 786440 | tf_op jit(solution)/shard_map/ppermute | solution.py:1090
  154.2 13.2 %collective-permute-start.35 = (bf16[2,2,272,128]{3,2,1,0:T(8,128)(2,1)S(1)}, bf16[2,2,272,128]{3,2,1,0:T(8,128)(2,1)}, u32[]{:S(2)}, u32[]{:S(2)}) collective-permute-start(bf16[2,2,272,128]{3,2,1,0:T(8,128)(2,1)S(1)} %bitcast.146), channel_id=1, source_target_pairs={{0,1},{1,0},{2,3},{3,2},{4,5},{5,4},{6,7},{7,6},{8,9},{9,8},{10,11... | collective-permute-start | bytes 835592 | tf_op jit(solution)/shard_map/ppermute | solution.py:866
  159.1 5.2 %copy-start.2 = (f32[258288]{0:T(1024)S(1)}, f32[258288]{0:T(1024)}, u32[]{:S(2)}) copy-start(f32[258288]{0:T(1024)} %param.16) | copy-start | bytes 3099460
  162.7 4.6 %collective-permute-start.36 = (bf16[2,2,272,128]{3,2,1,0:T(8,128)(2,1)}, bf16[2,2,272,128]{3,2,1,0:T(8,128)(2,1)}, u32[]{:S(2)}, u32[]{:S(2)}) collective-permute-start(bf16[2,2,272,128]{3,2,1,0:T(8,128)(2,1)} %collective-permute-done.32.refs_1_), channel_id=1, source_target_pairs={{0,1},{1,0},{2,3},{3,2},{4,5},{5,4},{6,7},{7,6},{8,9},{9,8},{10,11... | collective-permute-start | bytes 835592 | tf_op jit(solution)/shard_map/ppermute | solution.py:866
  163.8 3.6 %collective-permute-start.37 = (bf16[2,2,272,128]{3,2,1,0:T(8,128)(2,1)}, bf16[2,2,272,128]{3,2,1,0:T(8,128)(2,1)}, u32[]{:S(2)}, u32[]{:S(2)}) collective-permute-start(bf16[2,2,272,128]{3,2,1,0:T(8,128)(2,1)} %collective-permute-done.33.refs_2_), channel_id=1, source_target_pairs={{0,1},{1,0},{2,3},{3,2},{4,5},{5,4},{6,7},{7,6},{8,9},{9,8},{10,11... | collective-permute-start | bytes 835592 | tf_op jit(solution)/shard_map/ppermute | solution.py:866
  163.8 3.6 %collective-permute-start.38 = (bf16[2,2,272,128]{3,2,1,0:T(8,128)(2,1)}, bf16[2,2,272,128]{3,2,1,0:T(8,128)(2,1)}, u32[]{:S(2)}, u32[]{:S(2)}) collective-permute-start(bf16[2,2,272,128]{3,2,1,0:T(8,128)(2,1)} %collective-permute-done.34.refs_3_), channel_id=1, source_target_pairs={{0,1},{1,0},{2,3},{3,2},{4,5},{5,4},{6,7},{7,6},{8,9},{9,8},{10,11... | collective-permute-start | bytes 835592 | tf_op jit(solution)/shard_map/ppermute | solution.py:866
  (10 other events, 21.2 us)
where the time goes:
time: 173 us; the launch traced here: 172 us
  Pallas kernels  84.7 us (49%)
  starting transfers between devices  46.1 us (27%)
  waiting for transfers between devices  22.1 us (13%)
  other arithmetic  10.8 us (6%)
  local copies, waits for them, and re-layouts  7.12 us (4%)
    pallas_call x1, Pallas kernels, per_device(): pl.pallas_call(forward, out_shape=out_specs + [shape(*s) for s in written...  34.4 us
    pallas_call x1, Pallas kernels, per_device(): pl.pallas_call(functools.partial(attention_back_kernel, plan), out_shape=...  19.2 us
    pallas_call x1, Pallas kernels, per_device(): pl.pallas_call(functools.partial(backward_kernel, plan), out_shape=bwd_ou...  11.3 us
    ppermute x6, starting transfers between devices, z_gather(): return [lax.ppermute(mine, both, z_pairs(r)) for r in range(1, half)]  10.2 us
    ppermute x6, starting transfers between devices, z_send(): lax.ppermute(x, both, z_pairs(r))  7.7 us
    pallas_call x1, Pallas kernels, per_device(): pl.pallas_call(functools.partial(prep_kernel, plan), out_shape=[shape((8,...  7.54 us
    ppermute x6, waiting for transfers between devices, z_gather(): return [lax.ppermute(mine, both, z_pairs(r)) for r in range(1, half)]  6.6 us
    ppermute x6, starting transfers between devices, xy_send(): lax.ppermute(x, both, xy_pairs(a, b))  5.3 us
  transfers between devices with their start and end apart: 39, of which 16 were waited for; matrix products, arithmetic and copies ran while one was open for 7% of the time, Pallas kernels for 27%

commit v1 on v0

--- a/solution.py
+++ b/solution.py
@@ -324,7 +324,7 @@
         mixed[rows, lanes] = diagonal(o, LANES).T
         return 0
 
-    lax.fori_loop(0, GROUPS * 3, ctx_body, 0, unroll=3)
+    lax.fori_loop(0, GROUPS * 3, ctx_body, 0, unroll=9)
     send_out(probs_c, probs_c_hbm)
 
     key_id = lax.broadcasted_iota(jnp.int32, (KEYS, 1), 0)
@@ -575,8 +575,8 @@
 def backward_kernel(
     plan,
     own_s,
-    vec, small_in, mid_ref, dpk,
-    w_in_hbm, w_qkv_hbm, ctx_hbm, stream_hbm, d_middle_hbm,
+    vec, small_in, dpk,
+    mid_hbm, w_in_hbm, w_qkv_hbm, ctx_hbm, stream_hbm, d_middle_hbm,
     keep_ref, send_ref, same_ref, cross_ref,
     w_in_b, w_qkv_b, ctx_ref, stream, d_middle, normed, d_hidden, ctx_grad, small_flat, gflat, sems,
 ):
@@ -584,11 +584,11 @@
     for n, (name, src, dst) in enumerate((
         ("w_qkv", w_qkv_hbm, w_qkv_b), ("stream", stream_hbm, stream), ("d_middle", d_middle_hbm, d_middle),
         ("w_in", w_in_hbm, w_in_b), ("ctx", ctx_hbm, ctx_ref),
+        ("mid", mid_hbm, gflat.at[pl.ds(ROW_OUT, plan.mid_rows)]),
     )):
         incoming[name] = pltpu.make_async_copy(src, dst, sems.at[n])
         incoming[name].start()
     gain1, bias1 = vec[0:1, :], vec[1:2, :]
-    gflat[ROW_OUT : ROW_OUT + plan.mid_rows, :] = mid_ref[...]
     for name in ("w_qkv", "stream", "d_middle"):
         incoming[name].wait()
 
@@ -636,6 +636,7 @@
         return 0
 
     lax.fori_loop(0, 3, qkv_body, 0)
+    incoming["mid"].wait()
     store_pieces(plan, gflat, 0, range(plan.early0), 0, own_s[1], keep_ref, send_ref, small_flat[...].astype(BF16))
 
 
@@ -1012,7 +1013,7 @@
         bwd = pl.pallas_call(
             functools.partial(backward_kernel, plan),
             out_shape=bwd_out,
-            in_specs=smem(1) + vmem(4) + [any_spec] * 5,
+            in_specs=smem(1) + vmem(3) + [any_spec] * 6,
             out_specs=vmem(len(bwd_out)),
             scratch_shapes=[
                 pltpu.VMEM((D_IN, D), BF16),
@@ -1025,11 +1026,11 @@
                 pltpu.VMEM((CTX, D_IN), BF16),
                 pltpu.VMEM((SMALL_PAD, LANES), F32),
                 pltpu.VMEM((ROW_OUT + plan.mid_rows, LANES), F32),
-                pltpu.SemaphoreType.DMA((5,)),
+                pltpu.SemaphoreType.DMA((6,)),
             ],
             compiler_params=params_of,
             cost_estimate=pl.CostEstimate(flops=5 * 10**9, bytes_accessed=15 * 10**6, transcendentals=0),
-        )(own_s, vec, small_in, mid, dpk, w_in_b, w_qkv_b, ctx_s, stream_s, d_middle_s)
+        )(own_s, vec, small_in, dpk, mid, w_in_b, w_qkv_b, ctx_s, stream_s, d_middle_s)
         keep_l, send_l, ctx_same, ctx_cross = bwd
 
         upper = dh // quarter

time: 173 us -> 172 us (level)
  transfers between devices with their start and end apart: 39 -> 39, of which waited for: 16 -> 16; matrix products, arithmetic and copies ran while one was open for 7% -> 7% of each run, Pallas kernels for 27% -> 26%
where the time goes in v1:
time: 172 us; the launch traced here: 171 us
  Pallas kernels  83.4 us (48%)
  starting transfers between devices  46 us (27%)
  waiting for transfers between devices  22.8 us (13%)
  other arithmetic  10.8 us (6%)
  local copies, waits for them, and re-layouts  7.12 us (4%)
    pallas_call x1, Pallas kernels, per_device(): pl.pallas_call(forward, out_shape=out_specs + [shape(*s) for s in written...  33.5 us
    pallas_call x1, Pallas kernels, per_device(): pl.pallas_call(functools.partial(attention_back_kernel, plan), out_shape=...  19.2 us
    pallas_call x1, Pallas kernels, per_device(): pl.pallas_call(functools.partial(backward_kernel, plan), out_shape=bwd_ou...  10.8 us
    ppermute x6, starting transfers between devices, z_gather(): return [lax.ppermute(mine, both, z_pairs(r)) for r in range(1, half)]  10.2 us
    ppermute x6, starting transfers between devices, z_send(): lax.ppermute(x, both, z_pairs(r))  7.68 us
    pallas_call x1, Pallas kernels, per_device(): pl.pallas_call(functools.partial(prep_kernel, plan), out_shape=[shape((8,...  7.54 us
    ppermute x6, waiting for transfers between devices, z_gather(): return [lax.ppermute(mine, both, z_pairs(r)) for r in range(1, half)]  6.6 us
    ppermute x6, starting transfers between devices, xy_send(): lax.ppermute(x, both, xy_pairs(a, b))  5.3 us
  transfers between devices with their start and end apart: 39, of which 16 were waited for; matrix products, arithmetic and copies ran while one was open for 7% of the time, Pallas kernels for 26%

profile of v1, /device:TPU:1, one launch (start us, length us, event | category | flops | bytes accessed | tf_op | source)
XLA Modules:
  0.0 171.3 jit_solution(736169085235397141)
XLA Ops:
  0.7 1.1 constant_dynamic-slice_fusion
  1.8 2.7 %collective-permute-start = (bf16[96,768]{1,0:T(8,128)(2,1)S(1)}, bf16[96,768]{1,0:T(8,128)(2,1)S(1)}, u32[]{:S(2)}, u32[]{:S(2)}) collective-permute-start(bf16[96,768]{1,0:T(8,128)(2,1)S(1)} %get-tuple-element.183), channel_id=1, source_target_pairs={{0,1},{1,2},{2,3},{3,0},{4,5},{5,6},{6,7},{7,4},{8,9},{9,10},{10,1... | collective-permute-start | bytes 442376 | tf_op jit(solution)/shard_map/ppermute | solution.py:878
  5.6 7.5 %shard_map.128 = (f32[8,384]{1,0:T(8,128)}, f32[2,256,128]{2,1,0:T(8,128)}, bf16[768,384]{1,0:T(8,128)(2,1)}, bf16[384,1152]{1,0:T(8,128)(2,1)}, bf16[384,384]{1...) custom-call(s32[10]{0:T(128)} %stack.81.own_s.refs_1_.own_ref, ...), custom_call_target="tpu_custom_call" | custom-call | tf_op jit(solution)/shard_map/pallas_call | solution.py:897
  13.9 33.5 %shard_map.129 = (f32[8,384]{1,0:T(8,128)}, bf16[2,2,2,2,256,128]{5,4,3,2,1,0:T(8,128)(2,1)}, bf16[2,2,2,2,256,128]{5,4,3,2,1,0:T(8,128)(2,1)}, s32[8]{0:T(128)}...) custom-call(s32[1,4,4]{2,1,0:T(4,128)} %refs_0_.1, ...), custom_call_target="tpu_custom_call" | custom-call | tf_op jit(solution)/shard_map/pallas_call | solution.py:939
  47.4 1.5 collective-permute-start.3
  48.9 2.8 %pad_bitcast_fusion = (f32[2056,128]{1,0:T(8,128)}, f32[2056,128]{1,0:T(8,128)}) fusion(f32[258288]{0:T(1024)S(1)} %copy-done.1, f32[258288]{0:T(1024)} %param.15), kind=kLoop, calls=%fused_computation.1 | loop fusion | bytes 4171648 | tf_op jit(solution)/shard_map/reshape | solution.py:976
  51.7 1.1 fusion.7
  52.8 1.2 collective-permute-start.6
  54.0 1.2 collective-permute-start.5
  55.5 19.2 %shard_map.130 = (bf16[1024,1152]{1,0:T(8,128)(2,1)}, f32[2,256,128]{2,1,0:T(8,128)}, f32[2,272,128]{2,1,0:T(8,128)}) custom-call(s32[8]{0:T(128)} %get-tuple-element.96.seg_s, s32[10]{0:T(128)} %stack.81.own_s.refs_1_.own_ref, f32[1024,1152]{1,0:T(8,128)} %get-tuple-element.100.qkv_hbm, bf16[9,384,512]{2,1,0:T(8,128)(2,1)} %get-tuple-element.101.probs_c_hbm, ...), custom_call_target="tpu_custom_call" | custom-call | flops 10000000000 | bytes 20000000 | tf_op jit(solution)/shard_map/pallas_call | solution.py:983
  74.7 2.3 %collective-permute-start.10 = (f32[2,272,128]{2,1,0:T(8,128)}, f32[2,272,128]{2,1,0:T(8,128)S(1)}, u32[]{:S(2)}, u32[]{:S(2)}) collective-permute-start(f32[2,272,128]{2,1,0:T(8,128)} %get-tuple-element.121), channel_id=1, source_target_pairs={{0,16},{1,17},{2,18},{3,19},{4,20},{5,21},{6,22},{7,23},{8,24},{9,... | collective-permute-start | bytes 835592 | tf_op jit(solution)/shard_map/ppermute | solution.py:1004
  77.0 1.1 add_convert_fusion.5
  78.2 1.4 collective-permute-start.7
  79.6 2.1 %collective-permute-start.9 = (bf16[256,128]{1,0:T(8,128)(2,1)S(1)}, bf16[256,128]{1,0:T(8,128)(2,1)S(1)}, u32[]{:S(2)}, u32[]{:S(2)}) collective-permute-start(bf16[256,128]{1,0:T(8,128)(2,1)S(1)} %get-tuple-element.199), channel_id=1, source_target_pairs={{0,24},{1,25},{2,26},{3,27},{4,28},{5,29},{6,30},{7,31},{8,0},{9,1... | collective-permute-start | bytes 196616 | tf_op jit(solution)/shard_map/ppermute | solution.py:841
  81.7 10.8 %shard_map.131 = (bf16[2,2,2,2,272,128]{5,4,3,2,1,0:T(8,128)(2,1)}, bf16[2,2,2,2,272,128]{5,4,3,2,1,0:T(8,128)(2,1)}, bf16[2,96,768]{2,1,0:T(8,128)(2,1)}, bf16[2,96,768]{2,1,0:T(8,128)(2,1)}) custom-call(s32[10]{0:T(128)} %stack.81.own_s.refs_1_.own_ref, f32[8,384]{1,0:T(8,128)} %get-tuple-element.87.refs_2_.vec, f32[8,384]{1,0:T(8,128)} %get-tuple-element.111.small_in, ...), custom_call_target="tpu_custom_call" | custom-call | flops 5000000000 | bytes 15000000 | tf_op jit(solution)/shard_map/pallas_call | solution.py:1013
  92.5 1.0 collective-permute-done.8
  93.6 2.3 %collective-permute-start.11 = (bf16[2,2,2,2,272,128]{5,4,3,2,1,0:T(8,128)(2,1)}, bf16[2,2,2,2,272,128]{5,4,3,2,1,0:T(8,128)(2,1)S(1)}, u32[]{:S(2)}, u32[]{:S(2)}) collective-permute-start(bf16[2,2,2,2,272,128]{5,4,3,2,1,0:T(8,128)(2,1)} %get-tuple-element.128), channel_id=1, source_target_pairs={{0,1},{1,0},{2,3},{3,2},{4,5},{5,4},{6,7},{7,6},{8,9},{9,8},{10,11... | collective-permute-start | bytes 3342344 | tf_op jit(solution)/shard_map/ppermute | solution.py:1050
  97.4 1.1 fusion.27
  98.9 1.1 fusion.1
  100.1 1.2 collective-permute-start.13
  101.5 1.2 collective-permute-start.15
  103.7 3.2 %collective-permute-start.17 = (bf16[256,128]{1,0:T(8,128)(2,1)S(1)}, bf16[256,128]{1,0:T(8,128)(2,1)S(1)}, u32[]{:S(2)}, u32[]{:S(2)}) collective-permute-start(bf16[256,128]{1,0:T(8,128)(2,1)S(1)} %get-tuple-element.133), channel_id=1, source_target_pairs={{0,16},{1,17},{2,18},{3,19},{4,20},{5,21},{6,22},{7,23},{8,24},{9,... | collective-permute-start | bytes 196616 | tf_op jit(solution)/shard_map/ppermute | solution.py:850
  107.0 1.3 collective-permute-done.16
  108.3 1.7 %collective-permute-start.18 = (bf16[256,128]{1,0:T(8,128)(2,1)S(1)}, bf16[256,128]{1,0:T(8,128)(2,1)S(1)}, u32[]{:S(2)}, u32[]{:S(2)}) collective-permute-start(bf16[256,128]{1,0:T(8,128)(2,1)S(1)} %get-tuple-element.133), channel_id=1, source_target_pairs={{0,24},{1,25},{2,26},{3,27},{4,28},{5,29},{6,30},{7,31},{8,0},{9,1... | collective-permute-start | bytes 196616 | tf_op jit(solution)/shard_map/ppermute | solution.py:850
  110.0 1.9 %collective-permute-done.17 = bf16[256,128]{1,0:T(8,128)(2,1)S(1)} collective-permute-done((bf16[256,128]{1,0:T(8,128)(2,1)S(1)}, bf16[256,128]{1,0:T(8,128)(2,1)S(1)}, u32[]{:S(2)}, u32[]{:S(2)}) %collective-permute-start.17) | collective-permute-done | bytes 65568 | tf_op jit(solution)/shard_map/ppermute | solution.py:850
  112.7 2.2 %collective-permute-done.15 = bf16[2,2,272,128]{3,2,1,0:T(8,128)(2,1)S(1)} collective-permute-done((bf16[2,2,272,128]{3,2,1,0:T(8,128)(2,1)}, bf16[2,2,272,128]{3,2,1,0:T(8,128)(2,1)S(1)}, u32[]{:S(2)}, u32[]{:S(2)}) %collective-permute-start.15) | collective-permute-done | bytes 278560 | tf_op jit(solution)/shard_map/ppermute | solution.py:830
  115.4 1.4 collective-permute-start.22
  117.8 3.2 %collective-permute-start.20 = (bf16[272,128]{1,0:T(8,128)(2,1)S(1)}, bf16[272,128]{1,0:T(8,128)(2,1)S(1)}, u32[]{:S(2)}, u32[]{:S(2)}) collective-permute-start(bf16[272,128]{1,0:T(8,128)(2,1)S(1)} %get-tuple-element.191), channel_id=1, source_target_pairs={{0,16},{1,17},{2,18},{3,19},{4,20},{5,21},{6,22},{7,23},{8,24},{9,... | collective-permute-start | bytes 208904 | tf_op jit(solution)/shard_map/ppermute | solution.py:841
  122.5 1.5 collective-permute-done.20
  123.9 1.7 %collective-permute-done.21 = bf16[272,128]{1,0:T(8,128)(2,1)S(1)} collective-permute-done((bf16[272,128]{1,0:T(8,128)(2,1)S(1)}, bf16[272,128]{1,0:T(8,128)(2,1)S(1)}, u32[]{:S(2)}, u32[]{:S(2)}) %collective-permute-start.21) | collective-permute-done | bytes 69664 | tf_op jit(solution)/shard_map/ppermute | solution.py:841
  125.7 2.1 %collective-permute-done.22 = bf16[1,2,2,256,128]{4,3,2,1,0:T(8,128)(2,1)S(1)} collective-permute-done((bf16[1,2,2,256,128]{4,3,2,1,0:T(8,128)(2,1)S(1)}, bf16[1,2,2,256,128]{4,3,2,1,0:T(8,128)(2,1)S(1)}, u32[]{:S(2)}, u32[]{:S(2)}) %collective-permute-start.22) | collective-permute-done | bytes 262176 | tf_op jit(solution)/shard_map/ppermute | solution.py:1064
  128.9 1.3 collective-permute-start.27
  130.1 1.0 collective-permute-start.24
  131.2 3.2 %collective-permute-start.25 = (bf16[272,128]{1,0:T(8,128)(2,1)S(1)}, bf16[272,128]{1,0:T(8,128)(2,1)S(1)}, u32[]{:S(2)}, u32[]{:S(2)}) collective-permute-start(bf16[272,128]{1,0:T(8,128)(2,1)S(1)} %pad_maximum_fusion.7), channel_id=1, source_target_pairs={{0,16},{1,17},{2,18},{3,19},{4,20},{5,21},{6,22},{7,23},{8,24},{9,... | collective-permute-start | bytes 208904 | tf_op jit(solution)/shard_map/ppermute | solution.py:850
  134.5 1.2 collective-permute-start.28
  135.8 1.5 collective-permute-done.25
  138.3 3.6 %collective-permute-done.28.given = bf16[272,128]{1,0:T(8,128)(2,1)S(1)} collective-permute-done((bf16[272,128]{1,0:T(8,128)(2,1)S(1)}, bf16[272,128]{1,0:T(8,128)(2,1)S(1)}, u32[]{:S(2)}, u32[]{:S(2)}) %collective-permute-start.28) | collective-permute-done | bytes 69664 | tf_op jit(solution)/shard_map/ppermute | solution.py:1080
  142.2 2.8 %collective-permute-start.29 = (bf16[4,2,2,256,128]{4,3,2,1,0:T(8,128)(2,1)S(1)}, bf16[4,2,2,256,128]{4,3,2,1,0:T(8,128)(2,1)S(1)}, u32[]{:S(2)}, u32[]{:S(2)}) collective-permute-start(bf16[4,2,2,256,128]{4,3,2,1,0:T(8,128)(2,1)S(1)} %pad_maximum_fusion.near), channel_id=1, source_target_pairs={{0,1},{1,0},{2,3},{3,2},{4,5},{5,4},{6,7},{7,6},{8,9},{9,8},{10,11... | collective-permute-start | bytes 3145736 | tf_op jit(solution)/shard_map/ppermute | solution.py:1086
  145.6 1.2 collective-permute-start.33
  146.8 1.2 collective-permute-start.34
  148.0 2.1 %collective-permute-done.30 = bf16[512,128]{1,0:T(8,128)(2,1)S(1)} collective-permute-done((bf16[512,128]{1,0:T(8,128)(2,1)S(1)}, bf16[512,128]{1,0:T(8,128)(2,1)S(1)}, u32[]{:S(2)}, u32[]{:S(2)}) %collective-permute-start.30) | collective-permute-done | bytes 131104 | tf_op jit(solution)/shard_map/ppermute | solution.py:1089
  150.8 1.6 collective-permute-start.31
  152.4 1.0 copy-done.5
  153.4 4.9 %shard_map.132 = (f32[16143,128]{1,0:T(8,128)}, f32[8,128]{1,0:T(8,128)}) custom-call(s32[10]{0:T(128)} %stack.81.own_s.refs_1_.own_ref, bf16[4,2,2,256,128]{4,3,2,1,0:T(8,128)(2,1)} %copy-done, bf16[4,2,2,256,128]{4,3,2,1,0:T(8,128)(2,1)} %copy-done.5), custom_call_target="tpu_custom_call" | custom-call | tf_op jit(solution)/shard_map/pallas_call | solution.py:1096
  158.4 2.9 %shard_map.133 = (f32[2048,128]{1,0:T(8,128)}, bf16[384,768]{1,0:T(8,128)(2,1)}) custom-call(s32[10]{0:T(128)} %stack.81.own_s.refs_1_.own_ref, bf16[2,512,128]{2,1,0:T(8,128)(2,1)} %pad_maximum_fusion.5.same, bf16[2,512,128]{2,1,0:T(8,128)(2,1)} %collective-permute-done.31.cross, bf16[272,128]{1,0:T(8,128)(2,1)} %copy-done.11, ...), custom_call_target="tpu_custom_call" | custom-call | tf_op jit(solution)/shard_map/pallas_call | solution.py:1111
  162.0 1.0 collective-permute-start.36
  163.5 3.1 %fusion = (f32[258288]{0:T(1024)}, f32[258288]{0:T(1024)}) fusion(f32[258288]{0:T(1024)S(1)} %copy-done.2, f32[262144]{0:T(1024)} %bitcast.149, f32[258288]{0:T(1024)} %param.15), kind=kLoop, calls=%fused_computation.4 | loop fusion | flops 1549728 | bytes 5165760 | tf_op jit(solution)/shard_map/add | solution.py:1125
  166.6 4.5 %shard_map.134 = f32[16143,128]{1,0:T(8,128)} custom-call(s32[10]{0:T(128)} %stack.81.own_s.refs_1_.own_ref, bf16[2,2,272,128]{3,2,1,0:T(8,128)(2,1)} %bitcast.147, bf16[2,2,272,128]{3,2,1,0:T(8,128)(2,1)} %collective-permute-done.32.refs_1_, bf16[2,2,272,128]{3,2,1,0:T(8,128)(2,1)} %collective-permute-done.33.refs_2_, ...), custom_call_target="tpu_custom_call", output_to_operand_aliasing={{}: (10, {})} | custom-call | tf_op jit(solution)/shard_map/pallas_call | solution.py:1130
  (108 shorter events, 14.2 us)
Async XLA Ops:
  1.8 11.4 %collective-permute-start = (bf16[96,768]{1,0:T(8,128)(2,1)S(1)}, bf16[96,768]{1,0:T(8,128)(2,1)S(1)}, u32[]{:S(2)}, u32[]{:S(2)}) collective-permute-start(bf16[96,768]{1,0:T(8,128)(2,1)S(1)} %get-tuple-element.183), channel_id=1, source_target_pairs={{0,1},{1,2},{2,3},{3,0},{4,5},{5,6},{6,7},{7,4},{8,9},{9,10},{10,1... | collective-permute-start | bytes 442376 | tf_op jit(solution)/shard_map/ppermute | solution.py:878
  4.4 8.7 %collective-permute-start.1 = (bf16[96,768]{1,0:T(8,128)(2,1)S(1)}, bf16[96,768]{1,0:T(8,128)(2,1)S(1)}, u32[]{:S(2)}, u32[]{:S(2)}) collective-permute-start(bf16[96,768]{1,0:T(8,128)(2,1)S(1)} %get-tuple-element.182), channel_id=1, source_target_pairs={{0,2},{1,3},{2,0},{3,1},{4,6},{5,7},{6,4},{7,5},{8,10},{9,11},{10,... | collective-permute-start | bytes 442376 | tf_op jit(solution)/shard_map/ppermute | solution.py:878
  4.4 8.7 %collective-permute-start.2 = (bf16[96,768]{1,0:T(8,128)(2,1)S(1)}, bf16[96,768]{1,0:T(8,128)(2,1)S(1)}, u32[]{:S(2)}, u32[]{:S(2)}) collective-permute-start(bf16[96,768]{1,0:T(8,128)(2,1)S(1)} %get-tuple-element.181), channel_id=1, source_target_pairs={{0,3},{1,0},{2,1},{3,2},{4,7},{5,4},{6,5},{7,6},{8,11},{9,8},{10,9... | collective-permute-start | bytes 442376 | tf_op jit(solution)/shard_map/ppermute | solution.py:878
  13.9 35.0 %copy-start.1 = (f32[258288]{0:T(1024)S(1)}, f32[258288]{0:T(1024)}, u32[]{:S(2)}) copy-start(f32[258288]{0:T(1024)} %param.16) | copy-start | bytes 3099460
  47.4 4.3 %collective-permute-start.3 = (bf16[2,2,2,2,256,128]{5,4,3,2,1,0:T(8,128)(2,1)}, bf16[2,2,2,2,256,128]{5,4,3,2,1,0:T(8,128)(2,1)S(1)}, u32[]{:S(2)}, u32[]{:S(2)}) collective-permute-start(bf16[2,2,2,2,256,128]{5,4,3,2,1,0:T(8,128)(2,1)} %get-tuple-element.99), channel_id=1, source_target_pairs={{0,1},{1,0},{2,3},{3,2},{4,5},{5,4},{6,7},{7,6},{8,9},{9,8},{10,11... | collective-permute-start | bytes 3145736 | tf_op jit(solution)/shard_map/ppermute | solution.py:973
  52.8 24.2 %collective-permute-start.6 = (bf16[2,2,256,128]{3,2,1,0:T(8,128)(2,1)}, bf16[2,2,256,128]{3,2,1,0:T(8,128)(2,1)S(1)}, u32[]{:S(2)}, u32[]{:S(2)}) collective-permute-start(bf16[2,2,256,128]{3,2,1,0:T(8,128)(2,1)} %get-tuple-element.176), channel_id=1, source_target_pairs={{0,6},{1,7},{2,4},{3,5},{4,2},{5,3},{6,0},{7,1},{8,14},{9,15},{10,... | collective-permute-start | bytes 786440 | tf_op jit(solution)/shard_map/ppermute | solution.py:830
  54.0 23.0 %collective-permute-start.5 = (bf16[2,2,256,128]{3,2,1,0:T(8,128)(2,1)}, bf16[2,2,256,128]{3,2,1,0:T(8,128)(2,1)S(1)}, u32[]{:S(2)}, u32[]{:S(2)}) collective-permute-start(bf16[2,2,256,128]{3,2,1,0:T(8,128)(2,1)} %get-tuple-element.175), channel_id=1, source_target_pairs={{0,2},{1,3},{2,0},{3,1},{4,6},{5,7},{6,4},{7,5},{8,10},{9,11},{10,... | collective-permute-start | bytes 786440 | tf_op jit(solution)/shard_map/ppermute | solution.py:830
  55.2 21.8 %collective-permute-start.4 = (bf16[2,2,256,128]{3,2,1,0:T(8,128)(2,1)}, bf16[2,2,256,128]{3,2,1,0:T(8,128)(2,1)}, u32[]{:S(2)}, u32[]{:S(2)}) collective-permute-start(bf16[2,2,256,128]{3,2,1,0:T(8,128)(2,1)} %get-tuple-element.177), channel_id=1, source_target_pairs={{0,4},{1,5},{2,6},{3,7},{4,0},{5,1},{6,2},{7,3},{8,12},{9,13},{10,... | collective-permute-start | bytes 786440 | tf_op jit(solution)/shard_map/ppermute | solution.py:830
  74.7 17.8 %collective-permute-start.10 = (f32[2,272,128]{2,1,0:T(8,128)}, f32[2,272,128]{2,1,0:T(8,128)S(1)}, u32[]{:S(2)}, u32[]{:S(2)}) collective-permute-start(f32[2,272,128]{2,1,0:T(8,128)} %get-tuple-element.121), channel_id=1, source_target_pairs={{0,16},{1,17},{2,18},{3,19},{4,20},{5,21},{6,22},{7,23},{8,24},{9,... | collective-permute-start | bytes 835592 | tf_op jit(solution)/shard_map/ppermute | solution.py:1004
  78.2 14.3 %collective-permute-start.7 = (bf16[256,128]{1,0:T(8,128)(2,1)S(1)}, bf16[256,128]{1,0:T(8,128)(2,1)S(1)}, u32[]{:S(2)}, u32[]{:S(2)}) collective-permute-start(bf16[256,128]{1,0:T(8,128)(2,1)S(1)} %get-tuple-element.202), channel_id=1, source_target_pairs={{0,8},{1,9},{2,10},{3,11},{4,12},{5,13},{6,14},{7,15},{8,16},{9,17... | collective-permute-start | bytes 196616 | tf_op jit(solution)/shard_map/ppermute | solution.py:841
  79.5 14.0 %collective-permute-start.8 = (bf16[256,128]{1,0:T(8,128)(2,1)S(1)}, bf16[256,128]{1,0:T(8,128)(2,1)S(1)}, u32[]{:S(2)}, u32[]{:S(2)}) collective-permute-start(bf16[256,128]{1,0:T(8,128)(2,1)S(1)} %get-tuple-element.200), channel_id=1, source_target_pairs={{0,16},{1,17},{2,18},{3,19},{4,20},{5,21},{6,22},{7,23},{8,24},{9,... | collective-permute-start | bytes 196616 | tf_op jit(solution)/shard_map/ppermute | solution.py:841
  79.6 14.0 %collective-permute-start.9 = (bf16[256,128]{1,0:T(8,128)(2,1)S(1)}, bf16[256,128]{1,0:T(8,128)(2,1)S(1)}, u32[]{:S(2)}, u32[]{:S(2)}) collective-permute-start(bf16[256,128]{1,0:T(8,128)(2,1)S(1)} %get-tuple-element.199), channel_id=1, source_target_pairs={{0,24},{1,25},{2,26},{3,27},{4,28},{5,29},{6,30},{7,31},{8,0},{9,1... | collective-permute-start | bytes 196616 | tf_op jit(solution)/shard_map/ppermute | solution.py:841
  92.5 6.4 %copy-start.3 = (bf16[2,2,2,2,272,128]{5,4,3,2,1,0:T(8,128)(2,1)S(1)}, bf16[2,2,2,2,272,128]{5,4,3,2,1,0:T(8,128)(2,1)}, u32[]{:S(2)}) copy-start(bf16[2,2,2,2,272,128]{5,4,3,2,1,0:T(8,128)(2,1)} %get-tuple-element.117) | copy-start | bytes 3342340
  92.5 6.4 %copy-start.10 = (f32[2,272,128]{2,1,0:T(8,128)}, f32[2,272,128]{2,1,0:T(8,128)S(1)}, u32[]{:S(2)}) copy-start(f32[2,272,128]{2,1,0:T(8,128)S(1)} %collective-permute-done.10) | copy-start | bytes 835588
  93.6 5.3 %collective-permute-start.11 = (bf16[2,2,2,2,272,128]{5,4,3,2,1,0:T(8,128)(2,1)}, bf16[2,2,2,2,272,128]{5,4,3,2,1,0:T(8,128)(2,1)S(1)}, u32[]{:S(2)}, u32[]{:S(2)}) collective-permute-start(bf16[2,2,2,2,272,128]{5,4,3,2,1,0:T(8,128)(2,1)} %get-tuple-element.128), channel_id=1, source_target_pairs={{0,1},{1,0},{2,3},{3,2},{4,5},{5,4},{6,7},{7,6},{8,9},{9,8},{10,11... | collective-permute-start | bytes 3342344 | tf_op jit(solution)/shard_map/ppermute | solution.py:1050
  95.9 3.0 %collective-permute-start.12 = (bf16[2,96,768]{2,1,0:T(8,128)(2,1)}, bf16[2,96,768]{2,1,0:T(8,128)(2,1)S(1)}, u32[]{:S(2)}, u32[]{:S(2)}) collective-permute-start(bf16[2,96,768]{2,1,0:T(8,128)(2,1)} %get-tuple-element.130), channel_id=1, source_target_pairs={{0,1},{1,0},{2,3},{3,2},{4,5},{5,4},{6,7},{7,6},{8,9},{9,8},{10,11... | collective-permute-start | bytes 884744 | tf_op jit(solution)/shard_map/ppermute | solution.py:1054
  98.9 8.1 %copy-start.8 = (bf16[2,96,768]{2,1,0:T(8,128)(2,1)}, bf16[2,96,768]{2,1,0:T(8,128)(2,1)S(1)}, u32[]{:S(2)}) copy-start(bf16[2,96,768]{2,1,0:T(8,128)(2,1)S(1)} %collective-permute-done.12.ctx_cross) | copy-start | bytes 884740
  100.1 12.7 %collective-permute-start.13 = (bf16[2,2,272,128]{3,2,1,0:T(8,128)(2,1)}, bf16[2,2,272,128]{3,2,1,0:T(8,128)(2,1)S(1)}, u32[]{:S(2)}, u32[]{:S(2)}) collective-permute-start(bf16[2,2,272,128]{3,2,1,0:T(8,128)(2,1)} %get-tuple-element.174), channel_id=1, source_target_pairs={{0,4},{1,5},{2,6},{3,7},{4,0},{5,1},{6,2},{7,3},{8,12},{9,13},{10,... | collective-permute-start | bytes 835592 | tf_op jit(solution)/shard_map/ppermute | solution.py:830
  101.3 11.5 %collective-permute-start.14 = (bf16[2,2,272,128]{3,2,1,0:T(8,128)(2,1)}, bf16[2,2,272,128]{3,2,1,0:T(8,128)(2,1)S(1)}, u32[]{:S(2)}, u32[]{:S(2)}) collective-permute-start(bf16[2,2,272,128]{3,2,1,0:T(8,128)(2,1)} %get-tuple-element.173), channel_id=1, source_target_pairs={{0,2},{1,3},{2,0},{3,1},{4,6},{5,7},{6,4},{7,5},{8,10},{9,11},{10,... | collective-permute-start | bytes 835592 | tf_op jit(solution)/shard_map/ppermute | solution.py:830
  101.5 13.4 %collective-permute-start.15 = (bf16[2,2,272,128]{3,2,1,0:T(8,128)(2,1)}, bf16[2,2,272,128]{3,2,1,0:T(8,128)(2,1)S(1)}, u32[]{:S(2)}, u32[]{:S(2)}) collective-permute-start(bf16[2,2,272,128]{3,2,1,0:T(8,128)(2,1)} %get-tuple-element.172), channel_id=1, source_target_pairs={{0,6},{1,7},{2,4},{3,5},{4,2},{5,3},{6,0},{7,1},{8,14},{9,15},{10,... | collective-permute-start | bytes 835592 | tf_op jit(solution)/shard_map/ppermute | solution.py:830
  102.7 5.6 %collective-permute-start.16 = (bf16[256,128]{1,0:T(8,128)(2,1)S(1)}, bf16[256,128]{1,0:T(8,128)(2,1)S(1)}, u32[]{:S(2)}, u32[]{:S(2)}) collective-permute-start(bf16[256,128]{1,0:T(8,128)(2,1)S(1)} %get-tuple-element.133), channel_id=1, source_target_pairs={{0,8},{1,9},{2,10},{3,11},{4,12},{5,13},{6,14},{7,15},{8,16},{9,17... | collective-permute-start | bytes 196616 | tf_op jit(solution)/shard_map/ppermute | solution.py:850
  103.7 8.2 %collective-permute-start.17 = (bf16[256,128]{1,0:T(8,128)(2,1)S(1)}, bf16[256,128]{1,0:T(8,128)(2,1)S(1)}, u32[]{:S(2)}, u32[]{:S(2)}) collective-permute-start(bf16[256,128]{1,0:T(8,128)(2,1)S(1)} %get-tuple-element.133), channel_id=1, source_target_pairs={{0,16},{1,17},{2,18},{3,19},{4,20},{5,21},{6,22},{7,23},{8,24},{9,... | collective-permute-start | bytes 196616 | tf_op jit(solution)/shard_map/ppermute | solution.py:850
  108.3 4.5 %collective-permute-start.18 = (bf16[256,128]{1,0:T(8,128)(2,1)S(1)}, bf16[256,128]{1,0:T(8,128)(2,1)S(1)}, u32[]{:S(2)}, u32[]{:S(2)}) collective-permute-start(bf16[256,128]{1,0:T(8,128)(2,1)S(1)} %get-tuple-element.133), channel_id=1, source_target_pairs={{0,24},{1,25},{2,26},{3,27},{4,28},{5,29},{6,30},{7,31},{8,0},{9,1... | collective-permute-start | bytes 196616 | tf_op jit(solution)/shard_map/ppermute | solution.py:850
  115.1 13.6 %copy-start.12 = (f32[2,256,128]{2,1,0:T(8,128)S(1)}, f32[2,256,128]{2,1,0:T(8,128)}, u32[]{:S(2)}) copy-start(f32[2,256,128]{2,1,0:T(8,128)} %get-tuple-element.95) | copy-start | bytes 786436
  115.2 12.7 %collective-permute-start.23 = (bf16[2,96,768]{2,1,0:T(8,128)(2,1)S(1)}, bf16[2,96,768]{2,1,0:T(8,128)(2,1)S(1)}, u32[]{:S(2)}, u32[]{:S(2)}) collective-permute-start(bf16[2,96,768]{2,1,0:T(8,128)(2,1)S(1)} %pad_maximum_fusion.2), channel_id=1, source_target_pairs={{0,2},{1,3},{2,0},{3,1},{4,6},{5,7},{6,4},{7,5},{8,10},{9,11},{10,... | collective-permute-start | bytes 884744 | tf_op jit(solution)/shard_map/ppermute | solution.py:1065
  115.4 12.4 %collective-permute-start.22 = (bf16[1,2,2,256,128]{4,3,2,1,0:T(8,128)(2,1)S(1)}, bf16[1,2,2,256,128]{4,3,2,1,0:T(8,128)(2,1)S(1)}, u32[]{:S(2)}, u32[]{:S(2)}) collective-permute-start(bf16[1,2,2,256,128]{4,3,2,1,0:T(8,128)(2,1)S(1)} %bitcast.139), channel_id=1, source_target_pairs={{0,2},{1,3},{2,0},{3,1},{4,6},{5,7},{6,4},{7,5},{8,10},{9,11},{10,... | collective-permute-start | bytes 786440 | tf_op jit(solution)/shard_map/ppermute | solution.py:1064
  116.8 5.6 %collective-permute-start.19 = (bf16[272,128]{1,0:T(8,128)(2,1)S(1)}, bf16[272,128]{1,0:T(8,128)(2,1)S(1)}, u32[]{:S(2)}, u32[]{:S(2)}) collective-permute-start(bf16[272,128]{1,0:T(8,128)(2,1)S(1)} %get-tuple-element.192), channel_id=1, source_target_pairs={{0,8},{1,9},{2,10},{3,11},{4,12},{5,13},{6,14},{7,15},{8,16},{9,17... | collective-permute-start | bytes 208904 | tf_op jit(solution)/shard_map/ppermute | solution.py:841
  117.8 6.1 %collective-permute-start.20 = (bf16[272,128]{1,0:T(8,128)(2,1)S(1)}, bf16[272,128]{1,0:T(8,128)(2,1)S(1)}, u32[]{:S(2)}, u32[]{:S(2)}) collective-permute-start(bf16[272,128]{1,0:T(8,128)(2,1)S(1)} %get-tuple-element.191), channel_id=1, source_target_pairs={{0,16},{1,17},{2,18},{3,19},{4,20},{5,21},{6,22},{7,23},{8,24},{9,... | collective-permute-start | bytes 208904 | tf_op jit(solution)/shard_map/ppermute | solution.py:841
  121.0 4.7 %collective-permute-start.21 = (bf16[272,128]{1,0:T(8,128)(2,1)S(1)}, bf16[272,128]{1,0:T(8,128)(2,1)S(1)}, u32[]{:S(2)}, u32[]{:S(2)}) collective-permute-start(bf16[272,128]{1,0:T(8,128)(2,1)S(1)} %get-tuple-element.190), channel_id=1, source_target_pairs={{0,24},{1,25},{2,26},{3,27},{4,28},{5,29},{6,30},{7,31},{8,0},{9,1... | collective-permute-start | bytes 208904 | tf_op jit(solution)/shard_map/ppermute | solution.py:841
  127.8 6.7 %copy-start.9 = (bf16[2,96,768]{2,1,0:T(8,128)(2,1)}, bf16[2,96,768]{2,1,0:T(8,128)(2,1)S(1)}, u32[]{:S(2)}) copy-start(bf16[2,96,768]{2,1,0:T(8,128)(2,1)S(1)} %collective-permute-done.23.rest_0_) | copy-start | bytes 884740
  128.9 13.0 %collective-permute-start.27 = (bf16[2,2,2,256,128]{4,3,2,1,0:T(8,128)(2,1)S(1)}, bf16[2,2,2,256,128]{4,3,2,1,0:T(8,128)(2,1)S(1)}, u32[]{:S(2)}, u32[]{:S(2)}) collective-permute-start(bf16[2,2,2,256,128]{4,3,2,1,0:T(8,128)(2,1)S(1)} %pad_maximum_fusion.1), channel_id=1, source_target_pairs={{0,4},{1,5},{2,6},{3,7},{4,0},{5,1},{6,2},{7,3},{8,12},{9,13},{10,... | collective-permute-start | bytes 1572872 | tf_op jit(solution)/shard_map/ppermute | solution.py:1080
  130.1 5.6 %collective-permute-start.24 = (bf16[272,128]{1,0:T(8,128)(2,1)S(1)}, bf16[272,128]{1,0:T(8,128)(2,1)S(1)}, u32[]{:S(2)}, u32[]{:S(2)}) collective-permute-start(bf16[272,128]{1,0:T(8,128)(2,1)S(1)} %pad_maximum_fusion.7), channel_id=1, source_target_pairs={{0,8},{1,9},{2,10},{3,11},{4,12},{5,13},{6,14},{7,15},{8,16},{9,17... | collective-permute-start | bytes 208904 | tf_op jit(solution)/shard_map/ppermute | solution.py:850
  131.2 6.1 %collective-permute-start.25 = (bf16[272,128]{1,0:T(8,128)(2,1)S(1)}, bf16[272,128]{1,0:T(8,128)(2,1)S(1)}, u32[]{:S(2)}, u32[]{:S(2)}) collective-permute-start(bf16[272,128]{1,0:T(8,128)(2,1)S(1)} %pad_maximum_fusion.7), channel_id=1, source_target_pairs={{0,16},{1,17},{2,18},{3,19},{4,20},{5,21},{6,22},{7,23},{8,24},{9,... | collective-permute-start | bytes 208904 | tf_op jit(solution)/shard_map/ppermute | solution.py:850
  134.3 4.0 %collective-permute-start.26 = (bf16[272,128]{1,0:T(8,128)(2,1)S(1)}, bf16[272,128]{1,0:T(8,128)(2,1)S(1)}, u32[]{:S(2)}, u32[]{:S(2)}) collective-permute-start(bf16[272,128]{1,0:T(8,128)(2,1)S(1)} %pad_maximum_fusion.7), channel_id=1, source_target_pairs={{0,24},{1,25},{2,26},{3,27},{4,28},{5,29},{6,30},{7,31},{8,0},{9,1... | collective-permute-start | bytes 208904 | tf_op jit(solution)/shard_map/ppermute | solution.py:850
  134.5 7.4 %collective-permute-start.28 = (bf16[272,128]{1,0:T(8,128)(2,1)S(1)}, bf16[272,128]{1,0:T(8,128)(2,1)S(1)}, u32[]{:S(2)}, u32[]{:S(2)}) collective-permute-start(bf16[272,128]{1,0:T(8,128)(2,1)S(1)} %pad_maximum_fusion.8), channel_id=1, source_target_pairs={{0,16},{1,17},{2,18},{3,19},{4,20},{5,21},{6,22},{7,23},{8,24},{9,... | collective-permute-start | bytes 208904 | tf_op jit(solution)/shard_map/ppermute | solution.py:1080
  142.1 11.2 %copy-start = (bf16[4,2,2,256,128]{4,3,2,1,0:T(8,128)(2,1)}, bf16[4,2,2,256,128]{4,3,2,1,0:T(8,128)(2,1)S(1)}, u32[]{:S(2)}) copy-start(bf16[4,2,2,256,128]{4,3,2,1,0:T(8,128)(2,1)S(1)} %pad_maximum_fusion.near) | copy-start | bytes 3145732
  142.2 16.1 %copy-start.4 = (bf16[4,272,128]{2,1,0:T(8,128)(2,1)}, bf16[4,272,128]{2,1,0:T(8,128)(2,1)S(1)}, u32[]{:S(2)}) copy-start(bf16[4,272,128]{2,1,0:T(8,128)(2,1)S(1)} %pad_maximum_fusion.3) | copy-start | bytes 835588
  142.2 10.2 %collective-permute-start.29 = (bf16[4,2,2,256,128]{4,3,2,1,0:T(8,128)(2,1)S(1)}, bf16[4,2,2,256,128]{4,3,2,1,0:T(8,128)(2,1)S(1)}, u32[]{:S(2)}, u32[]{:S(2)}) collective-permute-start(bf16[4,2,2,256,128]{4,3,2,1,0:T(8,128)(2,1)S(1)} %pad_maximum_fusion.near), channel_id=1, source_target_pairs={{0,1},{1,0},{2,3},{3,2},{4,5},{5,4},{6,7},{7,6},{8,9},{9,8},{10,11... | collective-permute-start | bytes 3145736 | tf_op jit(solution)/shard_map/ppermute | solution.py:1086
  145.1 5.1 %collective-permute-start.30 = (bf16[512,128]{1,0:T(8,128)(2,1)S(1)}, bf16[512,128]{1,0:T(8,128)(2,1)S(1)}, u32[]{:S(2)}, u32[]{:S(2)}) collective-permute-start(bf16[512,128]{1,0:T(8,128)(2,1)S(1)} %get-tuple-element.157), channel_id=1, source_target_pairs={{0,2},{1,3},{2,0},{3,1},{4,6},{5,7},{6,4},{7,5},{8,10},{9,11},{10,... | collective-permute-start | bytes 393224 | tf_op jit(solution)/shard_map/ppermute | solution.py:1089
  145.4 15.9 %collective-permute-start.32 = (bf16[2,2,272,128]{3,2,1,0:T(8,128)(2,1)S(1)}, bf16[2,2,272,128]{3,2,1,0:T(8,128)(2,1)}, u32[]{:S(2)}, u32[]{:S(2)}) collective-permute-start(bf16[2,2,272,128]{3,2,1,0:T(8,128)(2,1)S(1)} %bitcast.143), channel_id=1, source_target_pairs={{0,4},{1,5},{2,6},{3,7},{4,0},{5,1},{6,2},{7,3},{8,12},{9,13},{10,... | collective-permute-start | bytes 835592 | tf_op jit(solution)/shard_map/ppermute | solution.py:864
  145.6 15.7 %collective-permute-start.33 = (bf16[2,2,272,128]{3,2,1,0:T(8,128)(2,1)S(1)}, bf16[2,2,272,128]{3,2,1,0:T(8,128)(2,1)}, u32[]{:S(2)}, u32[]{:S(2)}) collective-permute-start(bf16[2,2,272,128]{3,2,1,0:T(8,128)(2,1)S(1)} %bitcast.144), channel_id=1, source_target_pairs={{0,2},{1,3},{2,0},{3,1},{4,6},{5,7},{6,4},{7,5},{8,10},{9,11},{10,... | collective-permute-start | bytes 835592 | tf_op jit(solution)/shard_map/ppermute | solution.py:864
  146.8 15.2 %collective-permute-start.34 = (bf16[2,2,272,128]{3,2,1,0:T(8,128)(2,1)S(1)}, bf16[2,2,272,128]{3,2,1,0:T(8,128)(2,1)}, u32[]{:S(2)}, u32[]{:S(2)}) collective-permute-start(bf16[2,2,272,128]{3,2,1,0:T(8,128)(2,1)S(1)} %bitcast.145), channel_id=1, source_target_pairs={{0,6},{1,7},{2,4},{3,5},{4,2},{5,3},{6,0},{7,1},{8,14},{9,15},{10,... | collective-permute-start | bytes 835592 | tf_op jit(solution)/shard_map/ppermute | solution.py:864
  150.8 7.5 %collective-permute-start.31 = (bf16[2,512,128]{2,1,0:T(8,128)(2,1)}, bf16[2,512,128]{2,1,0:T(8,128)(2,1)}, u32[]{:S(2)}, u32[]{:S(2)}) collective-permute-start(bf16[2,512,128]{2,1,0:T(8,128)(2,1)} %pad_maximum_fusion.5.same), channel_id=1, source_target_pairs={{0,1},{1,0},{2,3},{3,2},{4,5},{5,4},{6,7},{7,6},{8,9},{9,8},{10,11... | collective-permute-start | bytes 786440 | tf_op jit(solution)/shard_map/ppermute | solution.py:1091
  153.4 13.2 %collective-permute-start.35 = (bf16[2,2,272,128]{3,2,1,0:T(8,128)(2,1)S(1)}, bf16[2,2,272,128]{3,2,1,0:T(8,128)(2,1)}, u32[]{:S(2)}, u32[]{:S(2)}) collective-permute-start(bf16[2,2,272,128]{3,2,1,0:T(8,128)(2,1)S(1)} %bitcast.146), channel_id=1, source_target_pairs={{0,1},{1,0},{2,3},{3,2},{4,5},{5,4},{6,7},{7,6},{8,9},{9,8},{10,11... | collective-permute-start | bytes 835592 | tf_op jit(solution)/shard_map/ppermute | solution.py:867
  158.3 5.2 %copy-start.2 = (f32[258288]{0:T(1024)S(1)}, f32[258288]{0:T(1024)}, u32[]{:S(2)}) copy-start(f32[258288]{0:T(1024)} %param.16) | copy-start | bytes 3099460
  162.0 4.6 %collective-permute-start.36 = (bf16[2,2,272,128]{3,2,1,0:T(8,128)(2,1)}, bf16[2,2,272,128]{3,2,1,0:T(8,128)(2,1)}, u32[]{:S(2)}, u32[]{:S(2)}) collective-permute-start(bf16[2,2,272,128]{3,2,1,0:T(8,128)(2,1)} %collective-permute-done.32.refs_1_), channel_id=1, source_target_pairs={{0,1},{1,0},{2,3},{3,2},{4,5},{5,4},{6,7},{7,6},{8,9},{9,8},{10,11... | collective-permute-start | bytes 835592 | tf_op jit(solution)/shard_map/ppermute | solution.py:867
  163.0 3.6 %collective-permute-start.37 = (bf16[2,2,272,128]{3,2,1,0:T(8,128)(2,1)}, bf16[2,2,272,128]{3,2,1,0:T(8,128)(2,1)}, u32[]{:S(2)}, u32[]{:S(2)}) collective-permute-start(bf16[2,2,272,128]{3,2,1,0:T(8,128)(2,1)} %collective-permute-done.33.refs_2_), channel_id=1, source_target_pairs={{0,1},{1,0},{2,3},{3,2},{4,5},{5,4},{6,7},{7,6},{8,9},{9,8},{10,11... | collective-permute-start | bytes 835592 | tf_op jit(solution)/shard_map/ppermute | solution.py:867
  163.0 3.6 %collective-permute-start.38 = (bf16[2,2,272,128]{3,2,1,0:T(8,128)(2,1)}, bf16[2,2,272,128]{3,2,1,0:T(8,128)(2,1)}, u32[]{:S(2)}, u32[]{:S(2)}) collective-permute-start(bf16[2,2,272,128]{3,2,1,0:T(8,128)(2,1)} %collective-permute-done.34.refs_3_), channel_id=1, source_target_pairs={{0,1},{1,0},{2,3},{3,2},{4,5},{5,4},{6,7},{7,6},{8,9},{9,8},{10,11... | collective-permute-start | bytes 835592 | tf_op jit(solution)/shard_map/ppermute | solution.py:867
  (10 other events, 21.8 us)

commit v2 on v1

--- a/solution.py
+++ b/solution.py
@@ -29,7 +29,7 @@
 WIDE = 256
 TILE = 256
 MLP_TILE = 512
-CHUNK = 512
+CHUNK = 768
 
 ROW_IN = 0
 ROW_QKV = D_IN * D // LANES
@@ -422,7 +422,7 @@
             gflat[pl.ds(ROW_UP - ROW_OUT + CHUNK // LANES * j + c, D, stride=12), :] = g[:, c * LANES : (c + 1) * LANES]
         return 0
 
-    lax.fori_loop(0, FF // CHUNK, up_body, 0, unroll=3)
+    lax.fori_loop(0, FF // CHUNK, up_body, 0, unroll=True)
 
     send_out(gflat.at[pl.ds(0, plan.mid_rows)], mid_ref)
 

time: 172 us -> 171 us (level)
  transfers between devices with their start and end apart: 39 -> 39, of which waited for: 16 -> 16; matrix products, arithmetic and copies ran while one was open for 7% -> 7% of each run, Pallas kernels for 26% -> 27%
where the time goes in v2:
time: 171 us
  Pallas kernels  82.7 us (48%)
  starting transfers between devices  46.1 us (27%)
  waiting for transfers between devices  22.7 us (13%)
  other arithmetic  10.8 us (6%)
  local copies, waits for them, and re-layouts  7.12 us (4%)
    pallas_call x1, Pallas kernels, per_device(): pl.pallas_call(forward, out_shape=out_specs + [shape(*s) for s in written...  32.9 us
    pallas_call x1, Pallas kernels, per_device(): pl.pallas_call(functools.partial(attention_back_kernel, plan), out_shape=...  19.2 us
    pallas_call x1, Pallas kernels, per_device(): pl.pallas_call(functools.partial(backward_kernel, plan), out_shape=bwd_ou...  10.8 us
    ppermute x6, starting transfers between devices, z_gather(): return [lax.ppermute(mine, both, z_pairs(r)) for r in range(1, half)]  10.3 us
    ppermute x6, starting transfers between devices, z_send(): lax.ppermute(x, both, z_pairs(r))  7.67 us
    pallas_call x1, Pallas kernels, per_device(): pl.pallas_call(functools.partial(prep_kernel, plan), out_shape=[shape((8,...  7.54 us
    ppermute x6, waiting for transfers between devices, z_gather(): return [lax.ppermute(mine, both, z_pairs(r)) for r in range(1, half)]  6.6 us
    ppermute x6, starting transfers between devices, xy_send(): lax.ppermute(x, both, xy_pairs(a, b))  5.3 us
  transfers between devices with their start and end apart: 39, of which 16 were waited for; matrix products, arithmetic and copies ran while one was open for 7% of the time, Pallas kernels for 27%

profile of v2, /device:TPU:1, one launch (start us, length us, event | category | flops | bytes accessed | tf_op | source)
XLA Modules:
  0.0 170.7 jit_solution(17573726748554685145)
XLA Ops:
  0.7 1.1 constant_dynamic-slice_fusion
  1.8 2.7 %collective-permute-start = (bf16[96,768]{1,0:T(8,128)(2,1)S(1)}, bf16[96,768]{1,0:T(8,128)(2,1)S(1)}, u32[]{:S(2)}, u32[]{:S(2)}) collective-permute-start(bf16[96,768]{1,0:T(8,128)(2,1)S(1)} %get-tuple-element.183), channel_id=1, source_target_pairs={{0,1},{1,2},{2,3},{3,0},{4,5},{5,6},{6,7},{7,4},{8,9},{9,10},{10,1... | collective-permute-start | bytes 442376 | tf_op jit(solution)/shard_map/ppermute | solution.py:878
  5.6 7.5 %shard_map.128 = (f32[8,384]{1,0:T(8,128)}, f32[2,256,128]{2,1,0:T(8,128)}, bf16[768,384]{1,0:T(8,128)(2,1)}, bf16[384,1152]{1,0:T(8,128)(2,1)}, bf16[384,384]{1...) custom-call(s32[10]{0:T(128)} %stack.81.own_s.refs_1_.own_ref, ...), custom_call_target="tpu_custom_call" | custom-call | tf_op jit(solution)/shard_map/pallas_call | solution.py:897
  13.9 32.9 %shard_map.129 = (f32[8,384]{1,0:T(8,128)}, bf16[2,2,2,2,256,128]{5,4,3,2,1,0:T(8,128)(2,1)}, bf16[2,2,2,2,256,128]{5,4,3,2,1,0:T(8,128)(2,1)}, s32[8]{0:T(128)}...) custom-call(s32[1,4,4]{2,1,0:T(4,128)} %refs_0_.1, ...), custom_call_target="tpu_custom_call" | custom-call | tf_op jit(solution)/shard_map/pallas_call | solution.py:939
  46.8 1.5 collective-permute-start.3
  48.3 2.8 %pad_bitcast_fusion = (f32[2056,128]{1,0:T(8,128)}, f32[2056,128]{1,0:T(8,128)}) fusion(f32[258288]{0:T(1024)S(1)} %copy-done.1, f32[258288]{0:T(1024)} %param.15), kind=kLoop, calls=%fused_computation.1 | loop fusion | bytes 4171648 | tf_op jit(solution)/shard_map/reshape | solution.py:976
  51.1 1.1 fusion.7
  52.2 1.2 collective-permute-start.6
  53.4 1.2 collective-permute-start.5
  54.8 19.2 %shard_map.130 = (bf16[1024,1152]{1,0:T(8,128)(2,1)}, f32[2,256,128]{2,1,0:T(8,128)}, f32[2,272,128]{2,1,0:T(8,128)}) custom-call(s32[8]{0:T(128)} %get-tuple-element.96.seg_s, s32[10]{0:T(128)} %stack.81.own_s.refs_1_.own_ref, f32[1024,1152]{1,0:T(8,128)} %get-tuple-element.100.qkv_hbm, bf16[9,384,512]{2,1,0:T(8,128)(2,1)} %get-tuple-element.101.probs_c_hbm, ...), custom_call_target="tpu_custom_call" | custom-call | flops 10000000000 | bytes 20000000 | tf_op jit(solution)/shard_map/pallas_call | solution.py:983
  74.0 2.4 %collective-permute-start.10 = (f32[2,272,128]{2,1,0:T(8,128)}, f32[2,272,128]{2,1,0:T(8,128)S(1)}, u32[]{:S(2)}, u32[]{:S(2)}) collective-permute-start(f32[2,272,128]{2,1,0:T(8,128)} %get-tuple-element.121), channel_id=1, source_target_pairs={{0,16},{1,17},{2,18},{3,19},{4,20},{5,21},{6,22},{7,23},{8,24},{9,... | collective-permute-start | bytes 835592 | tf_op jit(solution)/shard_map/ppermute | solution.py:1004
  76.4 1.1 add_convert_fusion.5
  77.5 1.3 collective-permute-start.7
  78.9 2.1 %collective-permute-start.9 = (bf16[256,128]{1,0:T(8,128)(2,1)S(1)}, bf16[256,128]{1,0:T(8,128)(2,1)S(1)}, u32[]{:S(2)}, u32[]{:S(2)}) collective-permute-start(bf16[256,128]{1,0:T(8,128)(2,1)S(1)} %get-tuple-element.199), channel_id=1, source_target_pairs={{0,24},{1,25},{2,26},{3,27},{4,28},{5,29},{6,30},{7,31},{8,0},{9,1... | collective-permute-start | bytes 196616 | tf_op jit(solution)/shard_map/ppermute | solution.py:841
  81.0 10.8 %shard_map.131 = (bf16[2,2,2,2,272,128]{5,4,3,2,1,0:T(8,128)(2,1)}, bf16[2,2,2,2,272,128]{5,4,3,2,1,0:T(8,128)(2,1)}, bf16[2,96,768]{2,1,0:T(8,128)(2,1)}, bf16[2,96,768]{2,1,0:T(8,128)(2,1)}) custom-call(s32[10]{0:T(128)} %stack.81.own_s.refs_1_.own_ref, f32[8,384]{1,0:T(8,128)} %get-tuple-element.87.refs_2_.vec, f32[8,384]{1,0:T(8,128)} %get-tuple-element.111.small_in, ...), custom_call_target="tpu_custom_call" | custom-call | flops 5000000000 | bytes 15000000 | tf_op jit(solution)/shard_map/pallas_call | solution.py:1013
  91.9 1.0 collective-permute-done.8
  92.9 2.3 %collective-permute-start.11 = (bf16[2,2,2,2,272,128]{5,4,3,2,1,0:T(8,128)(2,1)}, bf16[2,2,2,2,272,128]{5,4,3,2,1,0:T(8,128)(2,1)S(1)}, u32[]{:S(2)}, u32[]{:S(2)}) collective-permute-start(bf16[2,2,2,2,272,128]{5,4,3,2,1,0:T(8,128)(2,1)} %get-tuple-element.128), channel_id=1, source_target_pairs={{0,1},{1,0},{2,3},{3,2},{4,5},{5,4},{6,7},{7,6},{8,9},{9,8},{10,11... | collective-permute-start | bytes 3342344 | tf_op jit(solution)/shard_map/ppermute | solution.py:1050
  96.8 1.1 fusion.27
  98.3 1.1 fusion.1
  99.4 1.2 collective-permute-start.13
  100.9 1.2 collective-permute-start.15
  102.1 1.0 collective-permute-start.16
  103.1 3.2 %collective-permute-start.17 = (bf16[256,128]{1,0:T(8,128)(2,1)S(1)}, bf16[256,128]{1,0:T(8,128)(2,1)S(1)}, u32[]{:S(2)}, u32[]{:S(2)}) collective-permute-start(bf16[256,128]{1,0:T(8,128)(2,1)S(1)} %get-tuple-element.133), channel_id=1, source_target_pairs={{0,16},{1,17},{2,18},{3,19},{4,20},{5,21},{6,22},{7,23},{8,24},{9,... | collective-permute-start | bytes 196616 | tf_op jit(solution)/shard_map/ppermute | solution.py:850
  106.3 1.3 collective-permute-done.16
  107.6 1.7 %collective-permute-start.18 = (bf16[256,128]{1,0:T(8,128)(2,1)S(1)}, bf16[256,128]{1,0:T(8,128)(2,1)S(1)}, u32[]{:S(2)}, u32[]{:S(2)}) collective-permute-start(bf16[256,128]{1,0:T(8,128)(2,1)S(1)} %get-tuple-element.133), channel_id=1, source_target_pairs={{0,24},{1,25},{2,26},{3,27},{4,28},{5,29},{6,30},{7,31},{8,0},{9,1... | collective-permute-start | bytes 196616 | tf_op jit(solution)/shard_map/ppermute | solution.py:850
  109.4 1.9 %collective-permute-done.17 = bf16[256,128]{1,0:T(8,128)(2,1)S(1)} collective-permute-done((bf16[256,128]{1,0:T(8,128)(2,1)S(1)}, bf16[256,128]{1,0:T(8,128)(2,1)S(1)}, u32[]{:S(2)}, u32[]{:S(2)}) %collective-permute-start.17) | collective-permute-done | bytes 65568 | tf_op jit(solution)/shard_map/ppermute | solution.py:850
  112.1 2.2 %collective-permute-done.15 = bf16[2,2,272,128]{3,2,1,0:T(8,128)(2,1)S(1)} collective-permute-done((bf16[2,2,272,128]{3,2,1,0:T(8,128)(2,1)}, bf16[2,2,272,128]{3,2,1,0:T(8,128)(2,1)S(1)}, u32[]{:S(2)}, u32[]{:S(2)}) %collective-permute-start.15) | collective-permute-done | bytes 278560 | tf_op jit(solution)/shard_map/ppermute | solution.py:830
  114.9 1.3 collective-permute-start.22
  117.2 3.2 %collective-permute-start.20 = (bf16[272,128]{1,0:T(8,128)(2,1)S(1)}, bf16[272,128]{1,0:T(8,128)(2,1)S(1)}, u32[]{:S(2)}, u32[]{:S(2)}) collective-permute-start(bf16[272,128]{1,0:T(8,128)(2,1)S(1)} %get-tuple-element.191), channel_id=1, source_target_pairs={{0,16},{1,17},{2,18},{3,19},{4,20},{5,21},{6,22},{7,23},{8,24},{9,... | collective-permute-start | bytes 208904 | tf_op jit(solution)/shard_map/ppermute | solution.py:841
  121.8 1.5 collective-permute-done.20
  123.3 1.7 %collective-permute-done.21 = bf16[272,128]{1,0:T(8,128)(2,1)S(1)} collective-permute-done((bf16[272,128]{1,0:T(8,128)(2,1)S(1)}, bf16[272,128]{1,0:T(8,128)(2,1)S(1)}, u32[]{:S(2)}, u32[]{:S(2)}) %collective-permute-start.21) | collective-permute-done | bytes 69664 | tf_op jit(solution)/shard_map/ppermute | solution.py:841
  125.1 2.1 %collective-permute-done.22 = bf16[1,2,2,256,128]{4,3,2,1,0:T(8,128)(2,1)S(1)} collective-permute-done((bf16[1,2,2,256,128]{4,3,2,1,0:T(8,128)(2,1)S(1)}, bf16[1,2,2,256,128]{4,3,2,1,0:T(8,128)(2,1)S(1)}, u32[]{:S(2)}, u32[]{:S(2)}) %collective-permute-start.22) | collective-permute-done | bytes 262176 | tf_op jit(solution)/shard_map/ppermute | solution.py:1064
  128.2 1.3 collective-permute-start.27
  129.5 1.0 collective-permute-start.24
  130.6 3.2 %collective-permute-start.25 = (bf16[272,128]{1,0:T(8,128)(2,1)S(1)}, bf16[272,128]{1,0:T(8,128)(2,1)S(1)}, u32[]{:S(2)}, u32[]{:S(2)}) collective-permute-start(bf16[272,128]{1,0:T(8,128)(2,1)S(1)} %pad_maximum_fusion.7), channel_id=1, source_target_pairs={{0,16},{1,17},{2,18},{3,19},{4,20},{5,21},{6,22},{7,23},{8,24},{9,... | collective-permute-start | bytes 208904 | tf_op jit(solution)/shard_map/ppermute | solution.py:850
  133.9 1.2 collective-permute-start.28
  135.2 1.5 collective-permute-done.25
  137.7 3.6 %collective-permute-done.28.given = bf16[272,128]{1,0:T(8,128)(2,1)S(1)} collective-permute-done((bf16[272,128]{1,0:T(8,128)(2,1)S(1)}, bf16[272,128]{1,0:T(8,128)(2,1)S(1)}, u32[]{:S(2)}, u32[]{:S(2)}) %collective-permute-start.28) | collective-permute-done | bytes 69664 | tf_op jit(solution)/shard_map/ppermute | solution.py:1080
  141.6 2.8 %collective-permute-start.29 = (bf16[4,2,2,256,128]{4,3,2,1,0:T(8,128)(2,1)S(1)}, bf16[4,2,2,256,128]{4,3,2,1,0:T(8,128)(2,1)S(1)}, u32[]{:S(2)}, u32[]{:S(2)}) collective-permute-start(bf16[4,2,2,256,128]{4,3,2,1,0:T(8,128)(2,1)S(1)} %pad_maximum_fusion.near), channel_id=1, source_target_pairs={{0,1},{1,0},{2,3},{3,2},{4,5},{5,4},{6,7},{7,6},{8,9},{9,8},{10,11... | collective-permute-start | bytes 3145736 | tf_op jit(solution)/shard_map/ppermute | solution.py:1086
  145.0 1.2 collective-permute-start.33
  146.2 1.2 collective-permute-start.34
  147.4 2.1 %collective-permute-done.30 = bf16[512,128]{1,0:T(8,128)(2,1)S(1)} collective-permute-done((bf16[512,128]{1,0:T(8,128)(2,1)S(1)}, bf16[512,128]{1,0:T(8,128)(2,1)S(1)}, u32[]{:S(2)}, u32[]{:S(2)}) %collective-permute-start.30) | collective-permute-done | bytes 131104 | tf_op jit(solution)/shard_map/ppermute | solution.py:1089
  150.2 1.6 collective-permute-start.31
  152.8 4.9 %shard_map.132 = (f32[16143,128]{1,0:T(8,128)}, f32[8,128]{1,0:T(8,128)}) custom-call(s32[10]{0:T(128)} %stack.81.own_s.refs_1_.own_ref, bf16[4,2,2,256,128]{4,3,2,1,0:T(8,128)(2,1)} %copy-done, bf16[4,2,2,256,128]{4,3,2,1,0:T(8,128)(2,1)} %copy-done.5), custom_call_target="tpu_custom_call" | custom-call | tf_op jit(solution)/shard_map/pallas_call | solution.py:1096
  157.7 2.9 %shard_map.133 = (f32[2048,128]{1,0:T(8,128)}, bf16[384,768]{1,0:T(8,128)(2,1)}) custom-call(s32[10]{0:T(128)} %stack.81.own_s.refs_1_.own_ref, bf16[2,512,128]{2,1,0:T(8,128)(2,1)} %pad_maximum_fusion.5.same, bf16[2,512,128]{2,1,0:T(8,128)(2,1)} %collective-permute-done.31.cross, bf16[272,128]{1,0:T(8,128)(2,1)} %copy-done.11, ...), custom_call_target="tpu_custom_call" | custom-call | tf_op jit(solution)/shard_map/pallas_call | solution.py:1111
  161.4 1.0 collective-permute-start.36
  162.9 3.1 %fusion = (f32[258288]{0:T(1024)}, f32[258288]{0:T(1024)}) fusion(f32[258288]{0:T(1024)S(1)} %copy-done.2, f32[262144]{0:T(1024)} %bitcast.149, f32[258288]{0:T(1024)} %param.15), kind=kLoop, calls=%fused_computation.4 | loop fusion | flops 1549728 | bytes 5165760 | tf_op jit(solution)/shard_map/add | solution.py:1125
  166.0 4.5 %shard_map.134 = f32[16143,128]{1,0:T(8,128)} custom-call(s32[10]{0:T(128)} %stack.81.own_s.refs_1_.own_ref, bf16[2,2,272,128]{3,2,1,0:T(8,128)(2,1)} %bitcast.147, bf16[2,2,272,128]{3,2,1,0:T(8,128)(2,1)} %collective-permute-done.32.refs_1_, bf16[2,2,272,128]{3,2,1,0:T(8,128)(2,1)} %collective-permute-done.33.refs_2_, ...), custom_call_target="tpu_custom_call", output_to_operand_aliasing={{}: (10, {})} | custom-call | tf_op jit(solution)/shard_map/pallas_call | solution.py:1130
  (108 shorter events, 14.4 us)
Async XLA Ops:
  1.8 11.4 %collective-permute-start = (bf16[96,768]{1,0:T(8,128)(2,1)S(1)}, bf16[96,768]{1,0:T(8,128)(2,1)S(1)}, u32[]{:S(2)}, u32[]{:S(2)}) collective-permute-start(bf16[96,768]{1,0:T(8,128)(2,1)S(1)} %get-tuple-element.183), channel_id=1, source_target_pairs={{0,1},{1,2},{2,3},{3,0},{4,5},{5,6},{6,7},{7,4},{8,9},{9,10},{10,1... | collective-permute-start | bytes 442376 | tf_op jit(solution)/shard_map/ppermute | solution.py:878
  4.4 8.7 %collective-permute-start.1 = (bf16[96,768]{1,0:T(8,128)(2,1)S(1)}, bf16[96,768]{1,0:T(8,128)(2,1)S(1)}, u32[]{:S(2)}, u32[]{:S(2)}) collective-permute-start(bf16[96,768]{1,0:T(8,128)(2,1)S(1)} %get-tuple-element.182), channel_id=1, source_target_pairs={{0,2},{1,3},{2,0},{3,1},{4,6},{5,7},{6,4},{7,5},{8,10},{9,11},{10,... | collective-permute-start | bytes 442376 | tf_op jit(solution)/shard_map/ppermute | solution.py:878
  4.4 8.7 %collective-permute-start.2 = (bf16[96,768]{1,0:T(8,128)(2,1)S(1)}, bf16[96,768]{1,0:T(8,128)(2,1)S(1)}, u32[]{:S(2)}, u32[]{:S(2)}) collective-permute-start(bf16[96,768]{1,0:T(8,128)(2,1)S(1)} %get-tuple-element.181), channel_id=1, source_target_pairs={{0,3},{1,0},{2,1},{3,2},{4,7},{5,4},{6,5},{7,6},{8,11},{9,8},{10,9... | collective-permute-start | bytes 442376 | tf_op jit(solution)/shard_map/ppermute | solution.py:878
  13.9 34.4 %copy-start.1 = (f32[258288]{0:T(1024)S(1)}, f32[258288]{0:T(1024)}, u32[]{:S(2)}) copy-start(f32[258288]{0:T(1024)} %param.16) | copy-start | bytes 3099460
  46.8 4.3 %collective-permute-start.3 = (bf16[2,2,2,2,256,128]{5,4,3,2,1,0:T(8,128)(2,1)}, bf16[2,2,2,2,256,128]{5,4,3,2,1,0:T(8,128)(2,1)S(1)}, u32[]{:S(2)}, u32[]{:S(2)}) collective-permute-start(bf16[2,2,2,2,256,128]{5,4,3,2,1,0:T(8,128)(2,1)} %get-tuple-element.99), channel_id=1, source_target_pairs={{0,1},{1,0},{2,3},{3,2},{4,5},{5,4},{6,7},{7,6},{8,9},{9,8},{10,11... | collective-permute-start | bytes 3145736 | tf_op jit(solution)/shard_map/ppermute | solution.py:973
  52.2 24.2 %collective-permute-start.6 = (bf16[2,2,256,128]{3,2,1,0:T(8,128)(2,1)}, bf16[2,2,256,128]{3,2,1,0:T(8,128)(2,1)S(1)}, u32[]{:S(2)}, u32[]{:S(2)}) collective-permute-start(bf16[2,2,256,128]{3,2,1,0:T(8,128)(2,1)} %get-tuple-element.176), channel_id=1, source_target_pairs={{0,6},{1,7},{2,4},{3,5},{4,2},{5,3},{6,0},{7,1},{8,14},{9,15},{10,... | collective-permute-start | bytes 786440 | tf_op jit(solution)/shard_map/ppermute | solution.py:830
  53.4 23.0 %collective-permute-start.5 = (bf16[2,2,256,128]{3,2,1,0:T(8,128)(2,1)}, bf16[2,2,256,128]{3,2,1,0:T(8,128)(2,1)S(1)}, u32[]{:S(2)}, u32[]{:S(2)}) collective-permute-start(bf16[2,2,256,128]{3,2,1,0:T(8,128)(2,1)} %get-tuple-element.175), channel_id=1, source_target_pairs={{0,2},{1,3},{2,0},{3,1},{4,6},{5,7},{6,4},{7,5},{8,10},{9,11},{10,... | collective-permute-start | bytes 786440 | tf_op jit(solution)/shard_map/ppermute | solution.py:830
  54.6 21.8 %collective-permute-start.4 = (bf16[2,2,256,128]{3,2,1,0:T(8,128)(2,1)}, bf16[2,2,256,128]{3,2,1,0:T(8,128)(2,1)}, u32[]{:S(2)}, u32[]{:S(2)}) collective-permute-start(bf16[2,2,256,128]{3,2,1,0:T(8,128)(2,1)} %get-tuple-element.177), channel_id=1, source_target_pairs={{0,4},{1,5},{2,6},{3,7},{4,0},{5,1},{6,2},{7,3},{8,12},{9,13},{10,... | collective-permute-start | bytes 786440 | tf_op jit(solution)/shard_map/ppermute | solution.py:830
  74.0 17.8 %collective-permute-start.10 = (f32[2,272,128]{2,1,0:T(8,128)}, f32[2,272,128]{2,1,0:T(8,128)S(1)}, u32[]{:S(2)}, u32[]{:S(2)}) collective-permute-start(f32[2,272,128]{2,1,0:T(8,128)} %get-tuple-element.121), channel_id=1, source_target_pairs={{0,16},{1,17},{2,18},{3,19},{4,20},{5,21},{6,22},{7,23},{8,24},{9,... | collective-permute-start | bytes 835592 | tf_op jit(solution)/shard_map/ppermute | solution.py:1004
  77.5 14.3 %collective-permute-start.7 = (bf16[256,128]{1,0:T(8,128)(2,1)S(1)}, bf16[256,128]{1,0:T(8,128)(2,1)S(1)}, u32[]{:S(2)}, u32[]{:S(2)}) collective-permute-start(bf16[256,128]{1,0:T(8,128)(2,1)S(1)} %get-tuple-element.202), channel_id=1, source_target_pairs={{0,8},{1,9},{2,10},{3,11},{4,12},{5,13},{6,14},{7,15},{8,16},{9,17... | collective-permute-start | bytes 196616 | tf_op jit(solution)/shard_map/ppermute | solution.py:841
  78.9 14.0 %collective-permute-start.8 = (bf16[256,128]{1,0:T(8,128)(2,1)S(1)}, bf16[256,128]{1,0:T(8,128)(2,1)S(1)}, u32[]{:S(2)}, u32[]{:S(2)}) collective-permute-start(bf16[256,128]{1,0:T(8,128)(2,1)S(1)} %get-tuple-element.200), channel_id=1, source_target_pairs={{0,16},{1,17},{2,18},{3,19},{4,20},{5,21},{6,22},{7,23},{8,24},{9,... | collective-permute-start | bytes 196616 | tf_op jit(solution)/shard_map/ppermute | solution.py:841
  78.9 14.0 %collective-permute-start.9 = (bf16[256,128]{1,0:T(8,128)(2,1)S(1)}, bf16[256,128]{1,0:T(8,128)(2,1)S(1)}, u32[]{:S(2)}, u32[]{:S(2)}) collective-permute-start(bf16[256,128]{1,0:T(8,128)(2,1)S(1)} %get-tuple-element.199), channel_id=1, source_target_pairs={{0,24},{1,25},{2,26},{3,27},{4,28},{5,29},{6,30},{7,31},{8,0},{9,1... | collective-permute-start | bytes 196616 | tf_op jit(solution)/shard_map/ppermute | solution.py:841
  91.8 6.4 %copy-start.3 = (bf16[2,2,2,2,272,128]{5,4,3,2,1,0:T(8,128)(2,1)S(1)}, bf16[2,2,2,2,272,128]{5,4,3,2,1,0:T(8,128)(2,1)}, u32[]{:S(2)}) copy-start(bf16[2,2,2,2,272,128]{5,4,3,2,1,0:T(8,128)(2,1)} %get-tuple-element.117) | copy-start | bytes 3342340
  91.8 6.4 %copy-start.10 = (f32[2,272,128]{2,1,0:T(8,128)}, f32[2,272,128]{2,1,0:T(8,128)S(1)}, u32[]{:S(2)}) copy-start(f32[2,272,128]{2,1,0:T(8,128)S(1)} %collective-permute-done.10) | copy-start | bytes 835588
  92.9 5.3 %collective-permute-start.11 = (bf16[2,2,2,2,272,128]{5,4,3,2,1,0:T(8,128)(2,1)}, bf16[2,2,2,2,272,128]{5,4,3,2,1,0:T(8,128)(2,1)S(1)}, u32[]{:S(2)}, u32[]{:S(2)}) collective-permute-start(bf16[2,2,2,2,272,128]{5,4,3,2,1,0:T(8,128)(2,1)} %get-tuple-element.128), channel_id=1, source_target_pairs={{0,1},{1,0},{2,3},{3,2},{4,5},{5,4},{6,7},{7,6},{8,9},{9,8},{10,11... | collective-permute-start | bytes 3342344 | tf_op jit(solution)/shard_map/ppermute | solution.py:1050
  95.2 3.0 %collective-permute-start.12 = (bf16[2,96,768]{2,1,0:T(8,128)(2,1)}, bf16[2,96,768]{2,1,0:T(8,128)(2,1)S(1)}, u32[]{:S(2)}, u32[]{:S(2)}) collective-permute-start(bf16[2,96,768]{2,1,0:T(8,128)(2,1)} %get-tuple-element.130), channel_id=1, source_target_pairs={{0,1},{1,0},{2,3},{3,2},{4,5},{5,4},{6,7},{7,6},{8,9},{9,8},{10,11... | collective-permute-start | bytes 884744 | tf_op jit(solution)/shard_map/ppermute | solution.py:1054
  98.2 8.1 %copy-start.8 = (bf16[2,96,768]{2,1,0:T(8,128)(2,1)}, bf16[2,96,768]{2,1,0:T(8,128)(2,1)S(1)}, u32[]{:S(2)}) copy-start(bf16[2,96,768]{2,1,0:T(8,128)(2,1)S(1)} %collective-permute-done.12.ctx_cross) | copy-start | bytes 884740
  99.4 12.7 %collective-permute-start.13 = (bf16[2,2,272,128]{3,2,1,0:T(8,128)(2,1)}, bf16[2,2,272,128]{3,2,1,0:T(8,128)(2,1)S(1)}, u32[]{:S(2)}, u32[]{:S(2)}) collective-permute-start(bf16[2,2,272,128]{3,2,1,0:T(8,128)(2,1)} %get-tuple-element.174), channel_id=1, source_target_pairs={{0,4},{1,5},{2,6},{3,7},{4,0},{5,1},{6,2},{7,3},{8,12},{9,13},{10,... | collective-permute-start | bytes 835592 | tf_op jit(solution)/shard_map/ppermute | solution.py:830
  100.6 11.5 %collective-permute-start.14 = (bf16[2,2,272,128]{3,2,1,0:T(8,128)(2,1)}, bf16[2,2,272,128]{3,2,1,0:T(8,128)(2,1)S(1)}, u32[]{:S(2)}, u32[]{:S(2)}) collective-permute-start(bf16[2,2,272,128]{3,2,1,0:T(8,128)(2,1)} %get-tuple-element.173), channel_id=1, source_target_pairs={{0,2},{1,3},{2,0},{3,1},{4,6},{5,7},{6,4},{7,5},{8,10},{9,11},{10,... | collective-permute-start | bytes 835592 | tf_op jit(solution)/shard_map/ppermute | solution.py:830
  100.9 13.4 %collective-permute-start.15 = (bf16[2,2,272,128]{3,2,1,0:T(8,128)(2,1)}, bf16[2,2,272,128]{3,2,1,0:T(8,128)(2,1)S(1)}, u32[]{:S(2)}, u32[]{:S(2)}) collective-permute-start(bf16[2,2,272,128]{3,2,1,0:T(8,128)(2,1)} %get-tuple-element.172), channel_id=1, source_target_pairs={{0,6},{1,7},{2,4},{3,5},{4,2},{5,3},{6,0},{7,1},{8,14},{9,15},{10,... | collective-permute-start | bytes 835592 | tf_op jit(solution)/shard_map/ppermute | solution.py:830
  102.1 5.6 %collective-permute-start.16 = (bf16[256,128]{1,0:T(8,128)(2,1)S(1)}, bf16[256,128]{1,0:T(8,128)(2,1)S(1)}, u32[]{:S(2)}, u32[]{:S(2)}) collective-permute-start(bf16[256,128]{1,0:T(8,128)(2,1)S(1)} %get-tuple-element.133), channel_id=1, source_target_pairs={{0,8},{1,9},{2,10},{3,11},{4,12},{5,13},{6,14},{7,15},{8,16},{9,17... | collective-permute-start | bytes 196616 | tf_op jit(solution)/shard_map/ppermute | solution.py:850
  103.1 8.2 %collective-permute-start.17 = (bf16[256,128]{1,0:T(8,128)(2,1)S(1)}, bf16[256,128]{1,0:T(8,128)(2,1)S(1)}, u32[]{:S(2)}, u32[]{:S(2)}) collective-permute-start(bf16[256,128]{1,0:T(8,128)(2,1)S(1)} %get-tuple-element.133), channel_id=1, source_target_pairs={{0,16},{1,17},{2,18},{3,19},{4,20},{5,21},{6,22},{7,23},{8,24},{9,... | collective-permute-start | bytes 196616 | tf_op jit(solution)/shard_map/ppermute | solution.py:850
  107.6 4.5 %collective-permute-start.18 = (bf16[256,128]{1,0:T(8,128)(2,1)S(1)}, bf16[256,128]{1,0:T(8,128)(2,1)S(1)}, u32[]{:S(2)}, u32[]{:S(2)}) collective-permute-start(bf16[256,128]{1,0:T(8,128)(2,1)S(1)} %get-tuple-element.133), channel_id=1, source_target_pairs={{0,24},{1,25},{2,26},{3,27},{4,28},{5,29},{6,30},{7,31},{8,0},{9,1... | collective-permute-start | bytes 196616 | tf_op jit(solution)/shard_map/ppermute | solution.py:850
  114.5 13.6 %copy-start.12 = (f32[2,256,128]{2,1,0:T(8,128)S(1)}, f32[2,256,128]{2,1,0:T(8,128)}, u32[]{:S(2)}) copy-start(f32[2,256,128]{2,1,0:T(8,128)} %get-tuple-element.95) | copy-start | bytes 786436
  114.5 12.7 %collective-permute-start.23 = (bf16[2,96,768]{2,1,0:T(8,128)(2,1)S(1)}, bf16[2,96,768]{2,1,0:T(8,128)(2,1)S(1)}, u32[]{:S(2)}, u32[]{:S(2)}) collective-permute-start(bf16[2,96,768]{2,1,0:T(8,128)(2,1)S(1)} %pad_maximum_fusion.2), channel_id=1, source_target_pairs={{0,2},{1,3},{2,0},{3,1},{4,6},{5,7},{6,4},{7,5},{8,10},{9,11},{10,... | collective-permute-start | bytes 884744 | tf_op jit(solution)/shard_map/ppermute | solution.py:1065
  114.9 12.3 %collective-permute-start.22 = (bf16[1,2,2,256,128]{4,3,2,1,0:T(8,128)(2,1)S(1)}, bf16[1,2,2,256,128]{4,3,2,1,0:T(8,128)(2,1)S(1)}, u32[]{:S(2)}, u32[]{:S(2)}) collective-permute-start(bf16[1,2,2,256,128]{4,3,2,1,0:T(8,128)(2,1)S(1)} %bitcast.139), channel_id=1, source_target_pairs={{0,2},{1,3},{2,0},{3,1},{4,6},{5,7},{6,4},{7,5},{8,10},{9,11},{10,... | collective-permute-start | bytes 786440 | tf_op jit(solution)/shard_map/ppermute | solution.py:1064
  116.2 5.6 %collective-permute-start.19 = (bf16[272,128]{1,0:T(8,128)(2,1)S(1)}, bf16[272,128]{1,0:T(8,128)(2,1)S(1)}, u32[]{:S(2)}, u32[]{:S(2)}) collective-permute-start(bf16[272,128]{1,0:T(8,128)(2,1)S(1)} %get-tuple-element.192), channel_id=1, source_target_pairs={{0,8},{1,9},{2,10},{3,11},{4,12},{5,13},{6,14},{7,15},{8,16},{9,17... | collective-permute-start | bytes 208904 | tf_op jit(solution)/shard_map/ppermute | solution.py:841
  117.2 6.1 %collective-permute-start.20 = (bf16[272,128]{1,0:T(8,128)(2,1)S(1)}, bf16[272,128]{1,0:T(8,128)(2,1)S(1)}, u32[]{:S(2)}, u32[]{:S(2)}) collective-permute-start(bf16[272,128]{1,0:T(8,128)(2,1)S(1)} %get-tuple-element.191), channel_id=1, source_target_pairs={{0,16},{1,17},{2,18},{3,19},{4,20},{5,21},{6,22},{7,23},{8,24},{9,... | collective-permute-start | bytes 208904 | tf_op jit(solution)/shard_map/ppermute | solution.py:841
  120.4 4.7 %collective-permute-start.21 = (bf16[272,128]{1,0:T(8,128)(2,1)S(1)}, bf16[272,128]{1,0:T(8,128)(2,1)S(1)}, u32[]{:S(2)}, u32[]{:S(2)}) collective-permute-start(bf16[272,128]{1,0:T(8,128)(2,1)S(1)} %get-tuple-element.190), channel_id=1, source_target_pairs={{0,24},{1,25},{2,26},{3,27},{4,28},{5,29},{6,30},{7,31},{8,0},{9,1... | collective-permute-start | bytes 208904 | tf_op jit(solution)/shard_map/ppermute | solution.py:841
  127.2 6.7 %copy-start.9 = (bf16[2,96,768]{2,1,0:T(8,128)(2,1)}, bf16[2,96,768]{2,1,0:T(8,128)(2,1)S(1)}, u32[]{:S(2)}) copy-start(bf16[2,96,768]{2,1,0:T(8,128)(2,1)S(1)} %collective-permute-done.23.rest_0_) | copy-start | bytes 884740
  128.2 13.1 %collective-permute-start.27 = (bf16[2,2,2,256,128]{4,3,2,1,0:T(8,128)(2,1)S(1)}, bf16[2,2,2,256,128]{4,3,2,1,0:T(8,128)(2,1)S(1)}, u32[]{:S(2)}, u32[]{:S(2)}) collective-permute-start(bf16[2,2,2,256,128]{4,3,2,1,0:T(8,128)(2,1)S(1)} %pad_maximum_fusion.1), channel_id=1, source_target_pairs={{0,4},{1,5},{2,6},{3,7},{4,0},{5,1},{6,2},{7,3},{8,12},{9,13},{10,... | collective-permute-start | bytes 1572872 | tf_op jit(solution)/shard_map/ppermute | solution.py:1080
  129.5 5.7 %collective-permute-start.24 = (bf16[272,128]{1,0:T(8,128)(2,1)S(1)}, bf16[272,128]{1,0:T(8,128)(2,1)S(1)}, u32[]{:S(2)}, u32[]{:S(2)}) collective-permute-start(bf16[272,128]{1,0:T(8,128)(2,1)S(1)} %pad_maximum_fusion.7), channel_id=1, source_target_pairs={{0,8},{1,9},{2,10},{3,11},{4,12},{5,13},{6,14},{7,15},{8,16},{9,17... | collective-permute-start | bytes 208904 | tf_op jit(solution)/shard_map/ppermute | solution.py:850
  130.6 6.1 %collective-permute-start.25 = (bf16[272,128]{1,0:T(8,128)(2,1)S(1)}, bf16[272,128]{1,0:T(8,128)(2,1)S(1)}, u32[]{:S(2)}, u32[]{:S(2)}) collective-permute-start(bf16[272,128]{1,0:T(8,128)(2,1)S(1)} %pad_maximum_fusion.7), channel_id=1, source_target_pairs={{0,16},{1,17},{2,18},{3,19},{4,20},{5,21},{6,22},{7,23},{8,24},{9,... | collective-permute-start | bytes 208904 | tf_op jit(solution)/shard_map/ppermute | solution.py:850
  133.7 4.0 %collective-permute-start.26 = (bf16[272,128]{1,0:T(8,128)(2,1)S(1)}, bf16[272,128]{1,0:T(8,128)(2,1)S(1)}, u32[]{:S(2)}, u32[]{:S(2)}) collective-permute-start(bf16[272,128]{1,0:T(8,128)(2,1)S(1)} %pad_maximum_fusion.7), channel_id=1, source_target_pairs={{0,24},{1,25},{2,26},{3,27},{4,28},{5,29},{6,30},{7,31},{8,0},{9,1... | collective-permute-start | bytes 208904 | tf_op jit(solution)/shard_map/ppermute | solution.py:850
  133.9 7.4 %collective-permute-start.28 = (bf16[272,128]{1,0:T(8,128)(2,1)S(1)}, bf16[272,128]{1,0:T(8,128)(2,1)S(1)}, u32[]{:S(2)}, u32[]{:S(2)}) collective-permute-start(bf16[272,128]{1,0:T(8,128)(2,1)S(1)} %pad_maximum_fusion.8), channel_id=1, source_target_pairs={{0,16},{1,17},{2,18},{3,19},{4,20},{5,21},{6,22},{7,23},{8,24},{9,... | collective-permute-start | bytes 208904 | tf_op jit(solution)/shard_map/ppermute | solution.py:1080
  141.5 11.2 %copy-start = (bf16[4,2,2,256,128]{4,3,2,1,0:T(8,128)(2,1)}, bf16[4,2,2,256,128]{4,3,2,1,0:T(8,128)(2,1)S(1)}, u32[]{:S(2)}) copy-start(bf16[4,2,2,256,128]{4,3,2,1,0:T(8,128)(2,1)S(1)} %pad_maximum_fusion.near) | copy-start | bytes 3145732
  141.6 16.1 %copy-start.4 = (bf16[4,272,128]{2,1,0:T(8,128)(2,1)}, bf16[4,272,128]{2,1,0:T(8,128)(2,1)S(1)}, u32[]{:S(2)}) copy-start(bf16[4,272,128]{2,1,0:T(8,128)(2,1)S(1)} %pad_maximum_fusion.3) | copy-start | bytes 835588
  141.6 10.2 %collective-permute-start.29 = (bf16[4,2,2,256,128]{4,3,2,1,0:T(8,128)(2,1)S(1)}, bf16[4,2,2,256,128]{4,3,2,1,0:T(8,128)(2,1)S(1)}, u32[]{:S(2)}, u32[]{:S(2)}) collective-permute-start(bf16[4,2,2,256,128]{4,3,2,1,0:T(8,128)(2,1)S(1)} %pad_maximum_fusion.near), channel_id=1, source_target_pairs={{0,1},{1,0},{2,3},{3,2},{4,5},{5,4},{6,7},{7,6},{8,9},{9,8},{10,11... | collective-permute-start | bytes 3145736 | tf_op jit(solution)/shard_map/ppermute | solution.py:1086
  144.4 5.1 %collective-permute-start.30 = (bf16[512,128]{1,0:T(8,128)(2,1)S(1)}, bf16[512,128]{1,0:T(8,128)(2,1)S(1)}, u32[]{:S(2)}, u32[]{:S(2)}) collective-permute-start(bf16[512,128]{1,0:T(8,128)(2,1)S(1)} %get-tuple-element.157), channel_id=1, source_target_pairs={{0,2},{1,3},{2,0},{3,1},{4,6},{5,7},{6,4},{7,5},{8,10},{9,11},{10,... | collective-permute-start | bytes 393224 | tf_op jit(solution)/shard_map/ppermute | solution.py:1089
  144.8 15.9 %collective-permute-start.32 = (bf16[2,2,272,128]{3,2,1,0:T(8,128)(2,1)S(1)}, bf16[2,2,272,128]{3,2,1,0:T(8,128)(2,1)}, u32[]{:S(2)}, u32[]{:S(2)}) collective-permute-start(bf16[2,2,272,128]{3,2,1,0:T(8,128)(2,1)S(1)} %bitcast.143), channel_id=1, source_target_pairs={{0,4},{1,5},{2,6},{3,7},{4,0},{5,1},{6,2},{7,3},{8,12},{9,13},{10,... | collective-permute-start | bytes 835592 | tf_op jit(solution)/shard_map/ppermute | solution.py:864
  145.0 15.6 %collective-permute-start.33 = (bf16[2,2,272,128]{3,2,1,0:T(8,128)(2,1)S(1)}, bf16[2,2,272,128]{3,2,1,0:T(8,128)(2,1)}, u32[]{:S(2)}, u32[]{:S(2)}) collective-permute-start(bf16[2,2,272,128]{3,2,1,0:T(8,128)(2,1)S(1)} %bitcast.144), channel_id=1, source_target_pairs={{0,2},{1,3},{2,0},{3,1},{4,6},{5,7},{6,4},{7,5},{8,10},{9,11},{10,... | collective-permute-start | bytes 835592 | tf_op jit(solution)/shard_map/ppermute | solution.py:864
  146.2 15.2 %collective-permute-start.34 = (bf16[2,2,272,128]{3,2,1,0:T(8,128)(2,1)S(1)}, bf16[2,2,272,128]{3,2,1,0:T(8,128)(2,1)}, u32[]{:S(2)}, u32[]{:S(2)}) collective-permute-start(bf16[2,2,272,128]{3,2,1,0:T(8,128)(2,1)S(1)} %bitcast.145), channel_id=1, source_target_pairs={{0,6},{1,7},{2,4},{3,5},{4,2},{5,3},{6,0},{7,1},{8,14},{9,15},{10,... | collective-permute-start | bytes 835592 | tf_op jit(solution)/shard_map/ppermute | solution.py:864
  150.2 7.5 %collective-permute-start.31 = (bf16[2,512,128]{2,1,0:T(8,128)(2,1)}, bf16[2,512,128]{2,1,0:T(8,128)(2,1)}, u32[]{:S(2)}, u32[]{:S(2)}) collective-permute-start(bf16[2,512,128]{2,1,0:T(8,128)(2,1)} %pad_maximum_fusion.5.same), channel_id=1, source_target_pairs={{0,1},{1,0},{2,3},{3,2},{4,5},{5,4},{6,7},{7,6},{8,9},{9,8},{10,11... | collective-permute-start | bytes 786440 | tf_op jit(solution)/shard_map/ppermute | solution.py:1091
  152.8 13.2 %collective-permute-start.35 = (bf16[2,2,272,128]{3,2,1,0:T(8,128)(2,1)S(1)}, bf16[2,2,272,128]{3,2,1,0:T(8,128)(2,1)}, u32[]{:S(2)}, u32[]{:S(2)}) collective-permute-start(bf16[2,2,272,128]{3,2,1,0:T(8,128)(2,1)S(1)} %bitcast.146), channel_id=1, source_target_pairs={{0,1},{1,0},{2,3},{3,2},{4,5},{5,4},{6,7},{7,6},{8,9},{9,8},{10,11... | collective-permute-start | bytes 835592 | tf_op jit(solution)/shard_map/ppermute | solution.py:867
  157.7 5.2 %copy-start.2 = (f32[258288]{0:T(1024)S(1)}, f32[258288]{0:T(1024)}, u32[]{:S(2)}) copy-start(f32[258288]{0:T(1024)} %param.16) | copy-start | bytes 3099460
  161.4 4.6 %collective-permute-start.36 = (bf16[2,2,272,128]{3,2,1,0:T(8,128)(2,1)}, bf16[2,2,272,128]{3,2,1,0:T(8,128)(2,1)}, u32[]{:S(2)}, u32[]{:S(2)}) collective-permute-start(bf16[2,2,272,128]{3,2,1,0:T(8,128)(2,1)} %collective-permute-done.32.refs_1_), channel_id=1, source_target_pairs={{0,1},{1,0},{2,3},{3,2},{4,5},{5,4},{6,7},{7,6},{8,9},{9,8},{10,11... | collective-permute-start | bytes 835592 | tf_op jit(solution)/shard_map/ppermute | solution.py:867
  162.4 3.6 %collective-permute-start.37 = (bf16[2,2,272,128]{3,2,1,0:T(8,128)(2,1)}, bf16[2,2,272,128]{3,2,1,0:T(8,128)(2,1)}, u32[]{:S(2)}, u32[]{:S(2)}) collective-permute-start(bf16[2,2,272,128]{3,2,1,0:T(8,128)(2,1)} %collective-permute-done.33.refs_2_), channel_id=1, source_target_pairs={{0,1},{1,0},{2,3},{3,2},{4,5},{5,4},{6,7},{7,6},{8,9},{9,8},{10,11... | collective-permute-start | bytes 835592 | tf_op jit(solution)/shard_map/ppermute | solution.py:867
  162.4 3.6 %collective-permute-start.38 = (bf16[2,2,272,128]{3,2,1,0:T(8,128)(2,1)}, bf16[2,2,272,128]{3,2,1,0:T(8,128)(2,1)}, u32[]{:S(2)}, u32[]{:S(2)}) collective-permute-start(bf16[2,2,272,128]{3,2,1,0:T(8,128)(2,1)} %collective-permute-done.34.refs_3_), channel_id=1, source_target_pairs={{0,1},{1,0},{2,3},{3,2},{4,5},{5,4},{6,7},{7,6},{8,9},{9,8},{10,11... | collective-permute-start | bytes 835592 | tf_op jit(solution)/shard_map/ppermute | solution.py:867
  (10 other events, 21.8 us)

commit v3 on v2

--- a/solution.py
+++ b/solution.py
@@ -356,7 +356,7 @@
             mixed[rows, pl.ds(pl.multiple_of(half * LANES, LANES), WIDE)] += fold_six(o, hmasks)
         return 0
 
-    lax.fori_loop(0, 2 * IMG, tgt_body, 0, unroll=2)
+    lax.fori_loop(0, 2 * IMG, tgt_body, 0, unroll=4)
     send_out(probs_t, probs_t_hbm)
 
     for c in copies[3:]:

time: 171 us -> 171 us (level)
  no operation moved by 1% of the time
where the time goes in v3:
time: 171 us; the launch traced here: 170 us
  Pallas kernels  82.4 us (48%)
  starting transfers between devices  46.1 us (27%)
  waiting for transfers between devices  22.7 us (13%)
  other arithmetic  10.8 us (6%)
  local copies, waits for them, and re-layouts  7.12 us (4%)
    pallas_call x1, Pallas kernels, per_device(): pl.pallas_call(forward, out_shape=out_specs + [shape(*s) for s in written...  32.5 us
    pallas_call x1, Pallas kernels, per_device(): pl.pallas_call(functools.partial(attention_back_kernel, plan), out_shape=...  19.2 us
    pallas_call x1, Pallas kernels, per_device(): pl.pallas_call(functools.partial(backward_kernel, plan), out_shape=bwd_ou...  10.8 us
    ppermute x6, starting transfers between devices, z_gather(): return [lax.ppermute(mine, both, z_pairs(r)) for r in range(1, half)]  10.3 us
    ppermute x6, starting transfers between devices, z_send(): lax.ppermute(x, both, z_pairs(r))  7.74 us
    pallas_call x1, Pallas kernels, per_device(): pl.pallas_call(functools.partial(prep_kernel, plan), out_shape=[shape((8,...  7.54 us
    ppermute x6, waiting for transfers between devices, z_gather(): return [lax.ppermute(mine, both, z_pairs(r)) for r in range(1, half)]  6.6 us
    ppermute x6, starting transfers between devices, xy_send(): lax.ppermute(x, both, xy_pairs(a, b))  5.3 us
  transfers between devices with their start and end apart: 39, of which 16 were waited for; matrix products, arithmetic and copies ran while one was open for 7% of the time, Pallas kernels for 27%

profile of v3, /device:TPU:1, one launch (start us, length us, event | category | flops | bytes accessed | tf_op | source)
XLA Modules:
  0.0 170.3 jit_solution(13729731589711547102)
XLA Ops:
  0.7 1.1 constant_dynamic-slice_fusion
  1.8 2.7 %collective-permute-start = (bf16[96,768]{1,0:T(8,128)(2,1)S(1)}, bf16[96,768]{1,0:T(8,128)(2,1)S(1)}, u32[]{:S(2)}, u32[]{:S(2)}) collective-permute-start(bf16[96,768]{1,0:T(8,128)(2,1)S(1)} %get-tuple-element.183), channel_id=1, source_target_pairs={{0,1},{1,2},{2,3},{3,0},{4,5},{5,6},{6,7},{7,4},{8,9},{9,10},{10,1... | collective-permute-start | bytes 442376 | tf_op jit(solution)/shard_map/ppermute | solution.py:878
  5.6 7.5 %shard_map.128 = (f32[8,384]{1,0:T(8,128)}, f32[2,256,128]{2,1,0:T(8,128)}, bf16[768,384]{1,0:T(8,128)(2,1)}, bf16[384,1152]{1,0:T(8,128)(2,1)}, bf16[384,384]{1...) custom-call(s32[10]{0:T(128)} %stack.81.own_s.refs_1_.own_ref, ...), custom_call_target="tpu_custom_call" | custom-call | tf_op jit(solution)/shard_map/pallas_call | solution.py:897
  13.9 32.5 %shard_map.129 = (f32[8,384]{1,0:T(8,128)}, bf16[2,2,2,2,256,128]{5,4,3,2,1,0:T(8,128)(2,1)}, bf16[2,2,2,2,256,128]{5,4,3,2,1,0:T(8,128)(2,1)}, s32[8]{0:T(128)}...) custom-call(s32[1,4,4]{2,1,0:T(4,128)} %refs_0_.1, ...), custom_call_target="tpu_custom_call" | custom-call | tf_op jit(solution)/shard_map/pallas_call | solution.py:939
  46.4 1.4 collective-permute-start.3
  47.9 2.8 %pad_bitcast_fusion = (f32[2056,128]{1,0:T(8,128)}, f32[2056,128]{1,0:T(8,128)}) fusion(f32[258288]{0:T(1024)S(1)} %copy-done.1, f32[258288]{0:T(1024)} %param.15), kind=kLoop, calls=%fused_computation.1 | loop fusion | bytes 4171648 | tf_op jit(solution)/shard_map/reshape | solution.py:976
  50.7 1.1 fusion.7
  51.8 1.2 collective-permute-start.6
  53.0 1.2 collective-permute-start.5
  54.4 19.2 %shard_map.130 = (bf16[1024,1152]{1,0:T(8,128)(2,1)}, f32[2,256,128]{2,1,0:T(8,128)}, f32[2,272,128]{2,1,0:T(8,128)}) custom-call(s32[8]{0:T(128)} %get-tuple-element.96.seg_s, s32[10]{0:T(128)} %stack.81.own_s.refs_1_.own_ref, f32[1024,1152]{1,0:T(8,128)} %get-tuple-element.100.qkv_hbm, bf16[9,384,512]{2,1,0:T(8,128)(2,1)} %get-tuple-element.101.probs_c_hbm, ...), custom_call_target="tpu_custom_call" | custom-call | flops 10000000000 | bytes 20000000 | tf_op jit(solution)/shard_map/pallas_call | solution.py:983
  73.6 2.3 %collective-permute-start.10 = (f32[2,272,128]{2,1,0:T(8,128)}, f32[2,272,128]{2,1,0:T(8,128)S(1)}, u32[]{:S(2)}, u32[]{:S(2)}) collective-permute-start(f32[2,272,128]{2,1,0:T(8,128)} %get-tuple-element.121), channel_id=1, source_target_pairs={{0,16},{1,17},{2,18},{3,19},{4,20},{5,21},{6,22},{7,23},{8,24},{9,... | collective-permute-start | bytes 835592 | tf_op jit(solution)/shard_map/ppermute | solution.py:1004
  76.0 1.1 add_convert_fusion.5
  77.1 1.4 collective-permute-start.7
  78.6 2.1 %collective-permute-start.9 = (bf16[256,128]{1,0:T(8,128)(2,1)S(1)}, bf16[256,128]{1,0:T(8,128)(2,1)S(1)}, u32[]{:S(2)}, u32[]{:S(2)}) collective-permute-start(bf16[256,128]{1,0:T(8,128)(2,1)S(1)} %get-tuple-element.199), channel_id=1, source_target_pairs={{0,24},{1,25},{2,26},{3,27},{4,28},{5,29},{6,30},{7,31},{8,0},{9,1... | collective-permute-start | bytes 196616 | tf_op jit(solution)/shard_map/ppermute | solution.py:841
  80.7 10.8 %shard_map.131 = (bf16[2,2,2,2,272,128]{5,4,3,2,1,0:T(8,128)(2,1)}, bf16[2,2,2,2,272,128]{5,4,3,2,1,0:T(8,128)(2,1)}, bf16[2,96,768]{2,1,0:T(8,128)(2,1)}, bf16[2,96,768]{2,1,0:T(8,128)(2,1)}) custom-call(s32[10]{0:T(128)} %stack.81.own_s.refs_1_.own_ref, f32[8,384]{1,0:T(8,128)} %get-tuple-element.87.refs_2_.vec, f32[8,384]{1,0:T(8,128)} %get-tuple-element.111.small_in, ...), custom_call_target="tpu_custom_call" | custom-call | flops 5000000000 | bytes 15000000 | tf_op jit(solution)/shard_map/pallas_call | solution.py:1013
  92.5 2.3 %collective-permute-start.11 = (bf16[2,2,2,2,272,128]{5,4,3,2,1,0:T(8,128)(2,1)}, bf16[2,2,2,2,272,128]{5,4,3,2,1,0:T(8,128)(2,1)S(1)}, u32[]{:S(2)}, u32[]{:S(2)}) collective-permute-start(bf16[2,2,2,2,272,128]{5,4,3,2,1,0:T(8,128)(2,1)} %get-tuple-element.128), channel_id=1, source_target_pairs={{0,1},{1,0},{2,3},{3,2},{4,5},{5,4},{6,7},{7,6},{8,9},{9,8},{10,11... | collective-permute-start | bytes 3342344 | tf_op jit(solution)/shard_map/ppermute | solution.py:1050
  96.4 1.1 fusion.27
  97.9 1.1 fusion.1
  99.0 1.2 collective-permute-start.13
  100.5 1.2 collective-permute-start.15
  101.7 1.0 collective-permute-start.16
  102.7 3.2 %collective-permute-start.17 = (bf16[256,128]{1,0:T(8,128)(2,1)S(1)}, bf16[256,128]{1,0:T(8,128)(2,1)S(1)}, u32[]{:S(2)}, u32[]{:S(2)}) collective-permute-start(bf16[256,128]{1,0:T(8,128)(2,1)S(1)} %get-tuple-element.133), channel_id=1, source_target_pairs={{0,16},{1,17},{2,18},{3,19},{4,20},{5,21},{6,22},{7,23},{8,24},{9,... | collective-permute-start | bytes 196616 | tf_op jit(solution)/shard_map/ppermute | solution.py:850
  105.9 1.3 collective-permute-done.16
  107.2 1.7 %collective-permute-start.18 = (bf16[256,128]{1,0:T(8,128)(2,1)S(1)}, bf16[256,128]{1,0:T(8,128)(2,1)S(1)}, u32[]{:S(2)}, u32[]{:S(2)}) collective-permute-start(bf16[256,128]{1,0:T(8,128)(2,1)S(1)} %get-tuple-element.133), channel_id=1, source_target_pairs={{0,24},{1,25},{2,26},{3,27},{4,28},{5,29},{6,30},{7,31},{8,0},{9,1... | collective-permute-start | bytes 196616 | tf_op jit(solution)/shard_map/ppermute | solution.py:850
  109.0 1.9 %collective-permute-done.17 = bf16[256,128]{1,0:T(8,128)(2,1)S(1)} collective-permute-done((bf16[256,128]{1,0:T(8,128)(2,1)S(1)}, bf16[256,128]{1,0:T(8,128)(2,1)S(1)}, u32[]{:S(2)}, u32[]{:S(2)}) %collective-permute-start.17) | collective-permute-done | bytes 65568 | tf_op jit(solution)/shard_map/ppermute | solution.py:850
  111.7 2.2 %collective-permute-done.15 = bf16[2,2,272,128]{3,2,1,0:T(8,128)(2,1)S(1)} collective-permute-done((bf16[2,2,272,128]{3,2,1,0:T(8,128)(2,1)}, bf16[2,2,272,128]{3,2,1,0:T(8,128)(2,1)S(1)}, u32[]{:S(2)}, u32[]{:S(2)}) %collective-permute-start.15) | collective-permute-done | bytes 278560 | tf_op jit(solution)/shard_map/ppermute | solution.py:830
  114.5 1.3 collective-permute-start.22
  116.8 3.2 %collective-permute-start.20 = (bf16[272,128]{1,0:T(8,128)(2,1)S(1)}, bf16[272,128]{1,0:T(8,128)(2,1)S(1)}, u32[]{:S(2)}, u32[]{:S(2)}) collective-permute-start(bf16[272,128]{1,0:T(8,128)(2,1)S(1)} %get-tuple-element.191), channel_id=1, source_target_pairs={{0,16},{1,17},{2,18},{3,19},{4,20},{5,21},{6,22},{7,23},{8,24},{9,... | collective-permute-start | bytes 208904 | tf_op jit(solution)/shard_map/ppermute | solution.py:841
  121.4 1.5 collective-permute-done.20
  122.9 1.7 %collective-permute-done.21 = bf16[272,128]{1,0:T(8,128)(2,1)S(1)} collective-permute-done((bf16[272,128]{1,0:T(8,128)(2,1)S(1)}, bf16[272,128]{1,0:T(8,128)(2,1)S(1)}, u32[]{:S(2)}, u32[]{:S(2)}) %collective-permute-start.21) | collective-permute-done | bytes 69664 | tf_op jit(solution)/shard_map/ppermute | solution.py:841
  124.7 2.1 %collective-permute-done.22 = bf16[1,2,2,256,128]{4,3,2,1,0:T(8,128)(2,1)S(1)} collective-permute-done((bf16[1,2,2,256,128]{4,3,2,1,0:T(8,128)(2,1)S(1)}, bf16[1,2,2,256,128]{4,3,2,1,0:T(8,128)(2,1)S(1)}, u32[]{:S(2)}, u32[]{:S(2)}) %collective-permute-start.22) | collective-permute-done | bytes 262176 | tf_op jit(solution)/shard_map/ppermute | solution.py:1064
  127.8 1.3 collective-permute-start.27
  129.1 1.1 collective-permute-start.24
  130.2 3.2 %collective-permute-start.25 = (bf16[272,128]{1,0:T(8,128)(2,1)S(1)}, bf16[272,128]{1,0:T(8,128)(2,1)S(1)}, u32[]{:S(2)}, u32[]{:S(2)}) collective-permute-start(bf16[272,128]{1,0:T(8,128)(2,1)S(1)} %pad_maximum_fusion.7), channel_id=1, source_target_pairs={{0,16},{1,17},{2,18},{3,19},{4,20},{5,21},{6,22},{7,23},{8,24},{9,... | collective-permute-start | bytes 208904 | tf_op jit(solution)/shard_map/ppermute | solution.py:850
  133.5 1.2 collective-permute-start.28
  134.8 1.5 collective-permute-done.25
  137.3 3.6 %collective-permute-done.28.given = bf16[272,128]{1,0:T(8,128)(2,1)S(1)} collective-permute-done((bf16[272,128]{1,0:T(8,128)(2,1)S(1)}, bf16[272,128]{1,0:T(8,128)(2,1)S(1)}, u32[]{:S(2)}, u32[]{:S(2)}) %collective-permute-start.28) | collective-permute-done | bytes 69664 | tf_op jit(solution)/shard_map/ppermute | solution.py:1080
  141.3 2.8 %collective-permute-start.29 = (bf16[4,2,2,256,128]{4,3,2,1,0:T(8,128)(2,1)S(1)}, bf16[4,2,2,256,128]{4,3,2,1,0:T(8,128)(2,1)S(1)}, u32[]{:S(2)}, u32[]{:S(2)}) collective-permute-start(bf16[4,2,2,256,128]{4,3,2,1,0:T(8,128)(2,1)S(1)} %pad_maximum_fusion.near), channel_id=1, source_target_pairs={{0,1},{1,0},{2,3},{3,2},{4,5},{5,4},{6,7},{7,6},{8,9},{9,8},{10,11... | collective-permute-start | bytes 3145736 | tf_op jit(solution)/shard_map/ppermute | solution.py:1086
  144.6 1.2 collective-permute-start.33
  145.8 1.2 collective-permute-start.34
  147.0 2.1 %collective-permute-done.30 = bf16[512,128]{1,0:T(8,128)(2,1)S(1)} collective-permute-done((bf16[512,128]{1,0:T(8,128)(2,1)S(1)}, bf16[512,128]{1,0:T(8,128)(2,1)S(1)}, u32[]{:S(2)}, u32[]{:S(2)}) %collective-permute-start.30) | collective-permute-done | bytes 131104 | tf_op jit(solution)/shard_map/ppermute | solution.py:1089
  149.9 1.6 collective-permute-start.31
  151.4 1.0 copy-done.5
  152.4 4.9 %shard_map.132 = (f32[16143,128]{1,0:T(8,128)}, f32[8,128]{1,0:T(8,128)}) custom-call(s32[10]{0:T(128)} %stack.81.own_s.refs_1_.own_ref, bf16[4,2,2,256,128]{4,3,2,1,0:T(8,128)(2,1)} %copy-done, bf16[4,2,2,256,128]{4,3,2,1,0:T(8,128)(2,1)} %copy-done.5), custom_call_target="tpu_custom_call" | custom-call | tf_op jit(solution)/shard_map/pallas_call | solution.py:1096
  157.4 2.9 %shard_map.133 = (f32[2048,128]{1,0:T(8,128)}, bf16[384,768]{1,0:T(8,128)(2,1)}) custom-call(s32[10]{0:T(128)} %stack.81.own_s.refs_1_.own_ref, bf16[2,512,128]{2,1,0:T(8,128)(2,1)} %pad_maximum_fusion.5.same, bf16[2,512,128]{2,1,0:T(8,128)(2,1)} %collective-permute-done.31.cross, bf16[272,128]{1,0:T(8,128)(2,1)} %copy-done.11, ...), custom_call_target="tpu_custom_call" | custom-call | tf_op jit(solution)/shard_map/pallas_call | solution.py:1111
  161.0 1.0 collective-permute-start.36
  162.5 3.1 %fusion = (f32[258288]{0:T(1024)}, f32[258288]{0:T(1024)}) fusion(f32[258288]{0:T(1024)S(1)} %copy-done.2, f32[262144]{0:T(1024)} %bitcast.149, f32[258288]{0:T(1024)} %param.15), kind=kLoop, calls=%fused_computation.4 | loop fusion | flops 1549728 | bytes 5165760 | tf_op jit(solution)/shard_map/add | solution.py:1125
  165.6 4.5 %shard_map.134 = f32[16143,128]{1,0:T(8,128)} custom-call(s32[10]{0:T(128)} %stack.81.own_s.refs_1_.own_ref, bf16[2,2,272,128]{3,2,1,0:T(8,128)(2,1)} %bitcast.147, bf16[2,2,272,128]{3,2,1,0:T(8,128)(2,1)} %collective-permute-done.32.refs_1_, bf16[2,2,272,128]{3,2,1,0:T(8,128)(2,1)} %collective-permute-done.33.refs_2_, ...), custom_call_target="tpu_custom_call", output_to_operand_aliasing={{}: (10, {})} | custom-call | tf_op jit(solution)/shard_map/pallas_call | solution.py:1130
  (108 shorter events, 14.2 us)
Async XLA Ops:
  1.8 11.4 %collective-permute-start = (bf16[96,768]{1,0:T(8,128)(2,1)S(1)}, bf16[96,768]{1,0:T(8,128)(2,1)S(1)}, u32[]{:S(2)}, u32[]{:S(2)}) collective-permute-start(bf16[96,768]{1,0:T(8,128)(2,1)S(1)} %get-tuple-element.183), channel_id=1, source_target_pairs={{0,1},{1,2},{2,3},{3,0},{4,5},{5,6},{6,7},{7,4},{8,9},{9,10},{10,1... | collective-permute-start | bytes 442376 | tf_op jit(solution)/shard_map/ppermute | solution.py:878
  4.4 8.7 %collective-permute-start.1 = (bf16[96,768]{1,0:T(8,128)(2,1)S(1)}, bf16[96,768]{1,0:T(8,128)(2,1)S(1)}, u32[]{:S(2)}, u32[]{:S(2)}) collective-permute-start(bf16[96,768]{1,0:T(8,128)(2,1)S(1)} %get-tuple-element.182), channel_id=1, source_target_pairs={{0,2},{1,3},{2,0},{3,1},{4,6},{5,7},{6,4},{7,5},{8,10},{9,11},{10,... | collective-permute-start | bytes 442376 | tf_op jit(solution)/shard_map/ppermute | solution.py:878
  4.4 8.7 %collective-permute-start.2 = (bf16[96,768]{1,0:T(8,128)(2,1)S(1)}, bf16[96,768]{1,0:T(8,128)(2,1)S(1)}, u32[]{:S(2)}, u32[]{:S(2)}) collective-permute-start(bf16[96,768]{1,0:T(8,128)(2,1)S(1)} %get-tuple-element.181), channel_id=1, source_target_pairs={{0,3},{1,0},{2,1},{3,2},{4,7},{5,4},{6,5},{7,6},{8,11},{9,8},{10,9... | collective-permute-start | bytes 442376 | tf_op jit(solution)/shard_map/ppermute | solution.py:878
  13.9 34.0 %copy-start.1 = (f32[258288]{0:T(1024)S(1)}, f32[258288]{0:T(1024)}, u32[]{:S(2)}) copy-start(f32[258288]{0:T(1024)} %param.16) | copy-start | bytes 3099460
  46.4 4.2 %collective-permute-start.3 = (bf16[2,2,2,2,256,128]{5,4,3,2,1,0:T(8,128)(2,1)}, bf16[2,2,2,2,256,128]{5,4,3,2,1,0:T(8,128)(2,1)S(1)}, u32[]{:S(2)}, u32[]{:S(2)}) collective-permute-start(bf16[2,2,2,2,256,128]{5,4,3,2,1,0:T(8,128)(2,1)} %get-tuple-element.99), channel_id=1, source_target_pairs={{0,1},{1,0},{2,3},{3,2},{4,5},{5,4},{6,7},{7,6},{8,9},{9,8},{10,11... | collective-permute-start | bytes 3145736 | tf_op jit(solution)/shard_map/ppermute | solution.py:973
  51.8 24.2 %collective-permute-start.6 = (bf16[2,2,256,128]{3,2,1,0:T(8,128)(2,1)}, bf16[2,2,256,128]{3,2,1,0:T(8,128)(2,1)S(1)}, u32[]{:S(2)}, u32[]{:S(2)}) collective-permute-start(bf16[2,2,256,128]{3,2,1,0:T(8,128)(2,1)} %get-tuple-element.176), channel_id=1, source_target_pairs={{0,6},{1,7},{2,4},{3,5},{4,2},{5,3},{6,0},{7,1},{8,14},{9,15},{10,... | collective-permute-start | bytes 786440 | tf_op jit(solution)/shard_map/ppermute | solution.py:830
  53.0 23.0 %collective-permute-start.5 = (bf16[2,2,256,128]{3,2,1,0:T(8,128)(2,1)}, bf16[2,2,256,128]{3,2,1,0:T(8,128)(2,1)S(1)}, u32[]{:S(2)}, u32[]{:S(2)}) collective-permute-start(bf16[2,2,256,128]{3,2,1,0:T(8,128)(2,1)} %get-tuple-element.175), channel_id=1, source_target_pairs={{0,2},{1,3},{2,0},{3,1},{4,6},{5,7},{6,4},{7,5},{8,10},{9,11},{10,... | collective-permute-start | bytes 786440 | tf_op jit(solution)/shard_map/ppermute | solution.py:830
  54.2 21.8 %collective-permute-start.4 = (bf16[2,2,256,128]{3,2,1,0:T(8,128)(2,1)}, bf16[2,2,256,128]{3,2,1,0:T(8,128)(2,1)}, u32[]{:S(2)}, u32[]{:S(2)}) collective-permute-start(bf16[2,2,256,128]{3,2,1,0:T(8,128)(2,1)} %get-tuple-element.177), channel_id=1, source_target_pairs={{0,4},{1,5},{2,6},{3,7},{4,0},{5,1},{6,2},{7,3},{8,12},{9,13},{10,... | collective-permute-start | bytes 786440 | tf_op jit(solution)/shard_map/ppermute | solution.py:830
  73.6 17.9 %collective-permute-start.10 = (f32[2,272,128]{2,1,0:T(8,128)}, f32[2,272,128]{2,1,0:T(8,128)S(1)}, u32[]{:S(2)}, u32[]{:S(2)}) collective-permute-start(f32[2,272,128]{2,1,0:T(8,128)} %get-tuple-element.121), channel_id=1, source_target_pairs={{0,16},{1,17},{2,18},{3,19},{4,20},{5,21},{6,22},{7,23},{8,24},{9,... | collective-permute-start | bytes 835592 | tf_op jit(solution)/shard_map/ppermute | solution.py:1004
  77.1 14.4 %collective-permute-start.7 = (bf16[256,128]{1,0:T(8,128)(2,1)S(1)}, bf16[256,128]{1,0:T(8,128)(2,1)S(1)}, u32[]{:S(2)}, u32[]{:S(2)}) collective-permute-start(bf16[256,128]{1,0:T(8,128)(2,1)S(1)} %get-tuple-element.202), channel_id=1, source_target_pairs={{0,8},{1,9},{2,10},{3,11},{4,12},{5,13},{6,14},{7,15},{8,16},{9,17... | collective-permute-start | bytes 196616 | tf_op jit(solution)/shard_map/ppermute | solution.py:841
  78.5 14.0 %collective-permute-start.8 = (bf16[256,128]{1,0:T(8,128)(2,1)S(1)}, bf16[256,128]{1,0:T(8,128)(2,1)S(1)}, u32[]{:S(2)}, u32[]{:S(2)}) collective-permute-start(bf16[256,128]{1,0:T(8,128)(2,1)S(1)} %get-tuple-element.200), channel_id=1, source_target_pairs={{0,16},{1,17},{2,18},{3,19},{4,20},{5,21},{6,22},{7,23},{8,24},{9,... | collective-permute-start | bytes 196616 | tf_op jit(solution)/shard_map/ppermute | solution.py:841
  78.6 13.9 %collective-permute-start.9 = (bf16[256,128]{1,0:T(8,128)(2,1)S(1)}, bf16[256,128]{1,0:T(8,128)(2,1)S(1)}, u32[]{:S(2)}, u32[]{:S(2)}) collective-permute-start(bf16[256,128]{1,0:T(8,128)(2,1)S(1)} %get-tuple-element.199), channel_id=1, source_target_pairs={{0,24},{1,25},{2,26},{3,27},{4,28},{5,29},{6,30},{7,31},{8,0},{9,1... | collective-permute-start | bytes 196616 | tf_op jit(solution)/shard_map/ppermute | solution.py:841
  91.5 6.4 %copy-start.3 = (bf16[2,2,2,2,272,128]{5,4,3,2,1,0:T(8,128)(2,1)S(1)}, bf16[2,2,2,2,272,128]{5,4,3,2,1,0:T(8,128)(2,1)}, u32[]{:S(2)}) copy-start(bf16[2,2,2,2,272,128]{5,4,3,2,1,0:T(8,128)(2,1)} %get-tuple-element.117) | copy-start | bytes 3342340
  91.5 6.4 %copy-start.10 = (f32[2,272,128]{2,1,0:T(8,128)}, f32[2,272,128]{2,1,0:T(8,128)S(1)}, u32[]{:S(2)}) copy-start(f32[2,272,128]{2,1,0:T(8,128)S(1)} %collective-permute-done.10) | copy-start | bytes 835588
  92.5 5.3 %collective-permute-start.11 = (bf16[2,2,2,2,272,128]{5,4,3,2,1,0:T(8,128)(2,1)}, bf16[2,2,2,2,272,128]{5,4,3,2,1,0:T(8,128)(2,1)S(1)}, u32[]{:S(2)}, u32[]{:S(2)}) collective-permute-start(bf16[2,2,2,2,272,128]{5,4,3,2,1,0:T(8,128)(2,1)} %get-tuple-element.128), channel_id=1, source_target_pairs={{0,1},{1,0},{2,3},{3,2},{4,5},{5,4},{6,7},{7,6},{8,9},{9,8},{10,11... | collective-permute-start | bytes 3342344 | tf_op jit(solution)/shard_map/ppermute | solution.py:1050
  94.9 3.0 %collective-permute-start.12 = (bf16[2,96,768]{2,1,0:T(8,128)(2,1)}, bf16[2,96,768]{2,1,0:T(8,128)(2,1)S(1)}, u32[]{:S(2)}, u32[]{:S(2)}) collective-permute-start(bf16[2,96,768]{2,1,0:T(8,128)(2,1)} %get-tuple-element.130), channel_id=1, source_target_pairs={{0,1},{1,0},{2,3},{3,2},{4,5},{5,4},{6,7},{7,6},{8,9},{9,8},{10,11... | collective-permute-start | bytes 884744 | tf_op jit(solution)/shard_map/ppermute | solution.py:1054
  97.9 8.1 %copy-start.8 = (bf16[2,96,768]{2,1,0:T(8,128)(2,1)}, bf16[2,96,768]{2,1,0:T(8,128)(2,1)S(1)}, u32[]{:S(2)}) copy-start(bf16[2,96,768]{2,1,0:T(8,128)(2,1)S(1)} %collective-permute-done.12.ctx_cross) | copy-start | bytes 884740
  99.0 12.7 %collective-permute-start.13 = (bf16[2,2,272,128]{3,2,1,0:T(8,128)(2,1)}, bf16[2,2,272,128]{3,2,1,0:T(8,128)(2,1)S(1)}, u32[]{:S(2)}, u32[]{:S(2)}) collective-permute-start(bf16[2,2,272,128]{3,2,1,0:T(8,128)(2,1)} %get-tuple-element.174), channel_id=1, source_target_pairs={{0,4},{1,5},{2,6},{3,7},{4,0},{5,1},{6,2},{7,3},{8,12},{9,13},{10,... | collective-permute-start | bytes 835592 | tf_op jit(solution)/shard_map/ppermute | solution.py:830
  100.3 11.5 %collective-permute-start.14 = (bf16[2,2,272,128]{3,2,1,0:T(8,128)(2,1)}, bf16[2,2,272,128]{3,2,1,0:T(8,128)(2,1)S(1)}, u32[]{:S(2)}, u32[]{:S(2)}) collective-permute-start(bf16[2,2,272,128]{3,2,1,0:T(8,128)(2,1)} %get-tuple-element.173), channel_id=1, source_target_pairs={{0,2},{1,3},{2,0},{3,1},{4,6},{5,7},{6,4},{7,5},{8,10},{9,11},{10,... | collective-permute-start | bytes 835592 | tf_op jit(solution)/shard_map/ppermute | solution.py:830
  100.5 13.4 %collective-permute-start.15 = (bf16[2,2,272,128]{3,2,1,0:T(8,128)(2,1)}, bf16[2,2,272,128]{3,2,1,0:T(8,128)(2,1)S(1)}, u32[]{:S(2)}, u32[]{:S(2)}) collective-permute-start(bf16[2,2,272,128]{3,2,1,0:T(8,128)(2,1)} %get-tuple-element.172), channel_id=1, source_target_pairs={{0,6},{1,7},{2,4},{3,5},{4,2},{5,3},{6,0},{7,1},{8,14},{9,15},{10,... | collective-permute-start | bytes 835592 | tf_op jit(solution)/shard_map/ppermute | solution.py:830
  101.7 5.6 %collective-permute-start.16 = (bf16[256,128]{1,0:T(8,128)(2,1)S(1)}, bf16[256,128]{1,0:T(8,128)(2,1)S(1)}, u32[]{:S(2)}, u32[]{:S(2)}) collective-permute-start(bf16[256,128]{1,0:T(8,128)(2,1)S(1)} %get-tuple-element.133), channel_id=1, source_target_pairs={{0,8},{1,9},{2,10},{3,11},{4,12},{5,13},{6,14},{7,15},{8,16},{9,17... | collective-permute-start | bytes 196616 | tf_op jit(solution)/shard_map/ppermute | solution.py:850
  102.7 8.2 %collective-permute-start.17 = (bf16[256,128]{1,0:T(8,128)(2,1)S(1)}, bf16[256,128]{1,0:T(8,128)(2,1)S(1)}, u32[]{:S(2)}, u32[]{:S(2)}) collective-permute-start(bf16[256,128]{1,0:T(8,128)(2,1)S(1)} %get-tuple-element.133), channel_id=1, source_target_pairs={{0,16},{1,17},{2,18},{3,19},{4,20},{5,21},{6,22},{7,23},{8,24},{9,... | collective-permute-start | bytes 196616 | tf_op jit(solution)/shard_map/ppermute | solution.py:850
  107.2 4.5 %collective-permute-start.18 = (bf16[256,128]{1,0:T(8,128)(2,1)S(1)}, bf16[256,128]{1,0:T(8,128)(2,1)S(1)}, u32[]{:S(2)}, u32[]{:S(2)}) collective-permute-start(bf16[256,128]{1,0:T(8,128)(2,1)S(1)} %get-tuple-element.133), channel_id=1, source_target_pairs={{0,24},{1,25},{2,26},{3,27},{4,28},{5,29},{6,30},{7,31},{8,0},{9,1... | collective-permute-start | bytes 196616 | tf_op jit(solution)/shard_map/ppermute | solution.py:850
  114.1 13.6 %copy-start.12 = (f32[2,256,128]{2,1,0:T(8,128)S(1)}, f32[2,256,128]{2,1,0:T(8,128)}, u32[]{:S(2)}) copy-start(f32[2,256,128]{2,1,0:T(8,128)} %get-tuple-element.95) | copy-start | bytes 786436
  114.1 12.7 %collective-permute-start.23 = (bf16[2,96,768]{2,1,0:T(8,128)(2,1)S(1)}, bf16[2,96,768]{2,1,0:T(8,128)(2,1)S(1)}, u32[]{:S(2)}, u32[]{:S(2)}) collective-permute-start(bf16[2,96,768]{2,1,0:T(8,128)(2,1)S(1)} %pad_maximum_fusion.2), channel_id=1, source_target_pairs={{0,2},{1,3},{2,0},{3,1},{4,6},{5,7},{6,4},{7,5},{8,10},{9,11},{10,... | collective-permute-start | bytes 884744 | tf_op jit(solution)/shard_map/ppermute | solution.py:1065
  114.5 12.3 %collective-permute-start.22 = (bf16[1,2,2,256,128]{4,3,2,1,0:T(8,128)(2,1)S(1)}, bf16[1,2,2,256,128]{4,3,2,1,0:T(8,128)(2,1)S(1)}, u32[]{:S(2)}, u32[]{:S(2)}) collective-permute-start(bf16[1,2,2,256,128]{4,3,2,1,0:T(8,128)(2,1)S(1)} %bitcast.139), channel_id=1, source_target_pairs={{0,2},{1,3},{2,0},{3,1},{4,6},{5,7},{6,4},{7,5},{8,10},{9,11},{10,... | collective-permute-start | bytes 786440 | tf_op jit(solution)/shard_map/ppermute | solution.py:1064
  115.8 5.6 %collective-permute-start.19 = (bf16[272,128]{1,0:T(8,128)(2,1)S(1)}, bf16[272,128]{1,0:T(8,128)(2,1)S(1)}, u32[]{:S(2)}, u32[]{:S(2)}) collective-permute-start(bf16[272,128]{1,0:T(8,128)(2,1)S(1)} %get-tuple-element.192), channel_id=1, source_target_pairs={{0,8},{1,9},{2,10},{3,11},{4,12},{5,13},{6,14},{7,15},{8,16},{9,17... | collective-permute-start | bytes 208904 | tf_op jit(solution)/shard_map/ppermute | solution.py:841
  116.8 6.1 %collective-permute-start.20 = (bf16[272,128]{1,0:T(8,128)(2,1)S(1)}, bf16[272,128]{1,0:T(8,128)(2,1)S(1)}, u32[]{:S(2)}, u32[]{:S(2)}) collective-permute-start(bf16[272,128]{1,0:T(8,128)(2,1)S(1)} %get-tuple-element.191), channel_id=1, source_target_pairs={{0,16},{1,17},{2,18},{3,19},{4,20},{5,21},{6,22},{7,23},{8,24},{9,... | collective-permute-start | bytes 208904 | tf_op jit(solution)/shard_map/ppermute | solution.py:841
  120.0 4.7 %collective-permute-start.21 = (bf16[272,128]{1,0:T(8,128)(2,1)S(1)}, bf16[272,128]{1,0:T(8,128)(2,1)S(1)}, u32[]{:S(2)}, u32[]{:S(2)}) collective-permute-start(bf16[272,128]{1,0:T(8,128)(2,1)S(1)} %get-tuple-element.190), channel_id=1, source_target_pairs={{0,24},{1,25},{2,26},{3,27},{4,28},{5,29},{6,30},{7,31},{8,0},{9,1... | collective-permute-start | bytes 208904 | tf_op jit(solution)/shard_map/ppermute | solution.py:841
  126.8 6.7 %copy-start.9 = (bf16[2,96,768]{2,1,0:T(8,128)(2,1)}, bf16[2,96,768]{2,1,0:T(8,128)(2,1)S(1)}, u32[]{:S(2)}) copy-start(bf16[2,96,768]{2,1,0:T(8,128)(2,1)S(1)} %collective-permute-done.23.rest_0_) | copy-start | bytes 884740
  127.8 13.1 %collective-permute-start.27 = (bf16[2,2,2,256,128]{4,3,2,1,0:T(8,128)(2,1)S(1)}, bf16[2,2,2,256,128]{4,3,2,1,0:T(8,128)(2,1)S(1)}, u32[]{:S(2)}, u32[]{:S(2)}) collective-permute-start(bf16[2,2,2,256,128]{4,3,2,1,0:T(8,128)(2,1)S(1)} %pad_maximum_fusion.1), channel_id=1, source_target_pairs={{0,4},{1,5},{2,6},{3,7},{4,0},{5,1},{6,2},{7,3},{8,12},{9,13},{10,... | collective-permute-start | bytes 1572872 | tf_op jit(solution)/shard_map/ppermute | solution.py:1080
  129.1 5.7 %collective-permute-start.24 = (bf16[272,128]{1,0:T(8,128)(2,1)S(1)}, bf16[272,128]{1,0:T(8,128)(2,1)S(1)}, u32[]{:S(2)}, u32[]{:S(2)}) collective-permute-start(bf16[272,128]{1,0:T(8,128)(2,1)S(1)} %pad_maximum_fusion.7), channel_id=1, source_target_pairs={{0,8},{1,9},{2,10},{3,11},{4,12},{5,13},{6,14},{7,15},{8,16},{9,17... | collective-permute-start | bytes 208904 | tf_op jit(solution)/shard_map/ppermute | solution.py:850
  130.2 6.1 %collective-permute-start.25 = (bf16[272,128]{1,0:T(8,128)(2,1)S(1)}, bf16[272,128]{1,0:T(8,128)(2,1)S(1)}, u32[]{:S(2)}, u32[]{:S(2)}) collective-permute-start(bf16[272,128]{1,0:T(8,128)(2,1)S(1)} %pad_maximum_fusion.7), channel_id=1, source_target_pairs={{0,16},{1,17},{2,18},{3,19},{4,20},{5,21},{6,22},{7,23},{8,24},{9,... | collective-permute-start | bytes 208904 | tf_op jit(solution)/shard_map/ppermute | solution.py:850
  133.4 4.0 %collective-permute-start.26 = (bf16[272,128]{1,0:T(8,128)(2,1)S(1)}, bf16[272,128]{1,0:T(8,128)(2,1)S(1)}, u32[]{:S(2)}, u32[]{:S(2)}) collective-permute-start(bf16[272,128]{1,0:T(8,128)(2,1)S(1)} %pad_maximum_fusion.7), channel_id=1, source_target_pairs={{0,24},{1,25},{2,26},{3,27},{4,28},{5,29},{6,30},{7,31},{8,0},{9,1... | collective-permute-start | bytes 208904 | tf_op jit(solution)/shard_map/ppermute | solution.py:850
  133.5 7.4 %collective-permute-start.28 = (bf16[272,128]{1,0:T(8,128)(2,1)S(1)}, bf16[272,128]{1,0:T(8,128)(2,1)S(1)}, u32[]{:S(2)}, u32[]{:S(2)}) collective-permute-start(bf16[272,128]{1,0:T(8,128)(2,1)S(1)} %pad_maximum_fusion.8), channel_id=1, source_target_pairs={{0,16},{1,17},{2,18},{3,19},{4,20},{5,21},{6,22},{7,23},{8,24},{9,... | collective-permute-start | bytes 208904 | tf_op jit(solution)/shard_map/ppermute | solution.py:1080
  141.2 11.2 %copy-start = (bf16[4,2,2,256,128]{4,3,2,1,0:T(8,128)(2,1)}, bf16[4,2,2,256,128]{4,3,2,1,0:T(8,128)(2,1)S(1)}, u32[]{:S(2)}) copy-start(bf16[4,2,2,256,128]{4,3,2,1,0:T(8,128)(2,1)S(1)} %pad_maximum_fusion.near) | copy-start | bytes 3145732
  141.2 16.1 %copy-start.4 = (bf16[4,272,128]{2,1,0:T(8,128)(2,1)}, bf16[4,272,128]{2,1,0:T(8,128)(2,1)S(1)}, u32[]{:S(2)}) copy-start(bf16[4,272,128]{2,1,0:T(8,128)(2,1)S(1)} %pad_maximum_fusion.3) | copy-start | bytes 835588
  141.3 10.2 %collective-permute-start.29 = (bf16[4,2,2,256,128]{4,3,2,1,0:T(8,128)(2,1)S(1)}, bf16[4,2,2,256,128]{4,3,2,1,0:T(8,128)(2,1)S(1)}, u32[]{:S(2)}, u32[]{:S(2)}) collective-permute-start(bf16[4,2,2,256,128]{4,3,2,1,0:T(8,128)(2,1)S(1)} %pad_maximum_fusion.near), channel_id=1, source_target_pairs={{0,1},{1,0},{2,3},{3,2},{4,5},{5,4},{6,7},{7,6},{8,9},{9,8},{10,11... | collective-permute-start | bytes 3145736 | tf_op jit(solution)/shard_map/ppermute | solution.py:1086
  144.1 5.1 %collective-permute-start.30 = (bf16[512,128]{1,0:T(8,128)(2,1)S(1)}, bf16[512,128]{1,0:T(8,128)(2,1)S(1)}, u32[]{:S(2)}, u32[]{:S(2)}) collective-permute-start(bf16[512,128]{1,0:T(8,128)(2,1)S(1)} %get-tuple-element.157), channel_id=1, source_target_pairs={{0,2},{1,3},{2,0},{3,1},{4,6},{5,7},{6,4},{7,5},{8,10},{9,11},{10,... | collective-permute-start | bytes 393224 | tf_op jit(solution)/shard_map/ppermute | solution.py:1089
  144.4 15.9 %collective-permute-start.32 = (bf16[2,2,272,128]{3,2,1,0:T(8,128)(2,1)S(1)}, bf16[2,2,272,128]{3,2,1,0:T(8,128)(2,1)}, u32[]{:S(2)}, u32[]{:S(2)}) collective-permute-start(bf16[2,2,272,128]{3,2,1,0:T(8,128)(2,1)S(1)} %bitcast.143), channel_id=1, source_target_pairs={{0,4},{1,5},{2,6},{3,7},{4,0},{5,1},{6,2},{7,3},{8,12},{9,13},{10,... | collective-permute-start | bytes 835592 | tf_op jit(solution)/shard_map/ppermute | solution.py:864
  144.6 15.7 %collective-permute-start.33 = (bf16[2,2,272,128]{3,2,1,0:T(8,128)(2,1)S(1)}, bf16[2,2,272,128]{3,2,1,0:T(8,128)(2,1)}, u32[]{:S(2)}, u32[]{:S(2)}) collective-permute-start(bf16[2,2,272,128]{3,2,1,0:T(8,128)(2,1)S(1)} %bitcast.144), channel_id=1, source_target_pairs={{0,2},{1,3},{2,0},{3,1},{4,6},{5,7},{6,4},{7,5},{8,10},{9,11},{10,... | collective-permute-start | bytes 835592 | tf_op jit(solution)/shard_map/ppermute | solution.py:864
  145.8 15.2 %collective-permute-start.34 = (bf16[2,2,272,128]{3,2,1,0:T(8,128)(2,1)S(1)}, bf16[2,2,272,128]{3,2,1,0:T(8,128)(2,1)}, u32[]{:S(2)}, u32[]{:S(2)}) collective-permute-start(bf16[2,2,272,128]{3,2,1,0:T(8,128)(2,1)S(1)} %bitcast.145), channel_id=1, source_target_pairs={{0,6},{1,7},{2,4},{3,5},{4,2},{5,3},{6,0},{7,1},{8,14},{9,15},{10,... | collective-permute-start | bytes 835592 | tf_op jit(solution)/shard_map/ppermute | solution.py:864
  149.9 7.5 %collective-permute-start.31 = (bf16[2,512,128]{2,1,0:T(8,128)(2,1)}, bf16[2,512,128]{2,1,0:T(8,128)(2,1)}, u32[]{:S(2)}, u32[]{:S(2)}) collective-permute-start(bf16[2,512,128]{2,1,0:T(8,128)(2,1)} %pad_maximum_fusion.5.same), channel_id=1, source_target_pairs={{0,1},{1,0},{2,3},{3,2},{4,5},{5,4},{6,7},{7,6},{8,9},{9,8},{10,11... | collective-permute-start | bytes 786440 | tf_op jit(solution)/shard_map/ppermute | solution.py:1091
  152.4 13.1 %collective-permute-start.35 = (bf16[2,2,272,128]{3,2,1,0:T(8,128)(2,1)S(1)}, bf16[2,2,272,128]{3,2,1,0:T(8,128)(2,1)}, u32[]{:S(2)}, u32[]{:S(2)}) collective-permute-start(bf16[2,2,272,128]{3,2,1,0:T(8,128)(2,1)S(1)} %bitcast.146), channel_id=1, source_target_pairs={{0,1},{1,0},{2,3},{3,2},{4,5},{5,4},{6,7},{7,6},{8,9},{9,8},{10,11... | collective-permute-start | bytes 835592 | tf_op jit(solution)/shard_map/ppermute | solution.py:867
  157.4 5.1 %copy-start.2 = (f32[258288]{0:T(1024)S(1)}, f32[258288]{0:T(1024)}, u32[]{:S(2)}) copy-start(f32[258288]{0:T(1024)} %param.16) | copy-start | bytes 3099460
  161.0 4.6 %collective-permute-start.36 = (bf16[2,2,272,128]{3,2,1,0:T(8,128)(2,1)}, bf16[2,2,272,128]{3,2,1,0:T(8,128)(2,1)}, u32[]{:S(2)}, u32[]{:S(2)}) collective-permute-start(bf16[2,2,272,128]{3,2,1,0:T(8,128)(2,1)} %collective-permute-done.32.refs_1_), channel_id=1, source_target_pairs={{0,1},{1,0},{2,3},{3,2},{4,5},{5,4},{6,7},{7,6},{8,9},{9,8},{10,11... | collective-permute-start | bytes 835592 | tf_op jit(solution)/shard_map/ppermute | solution.py:867
  162.0 3.6 %collective-permute-start.37 = (bf16[2,2,272,128]{3,2,1,0:T(8,128)(2,1)}, bf16[2,2,272,128]{3,2,1,0:T(8,128)(2,1)}, u32[]{:S(2)}, u32[]{:S(2)}) collective-permute-start(bf16[2,2,272,128]{3,2,1,0:T(8,128)(2,1)} %collective-permute-done.33.refs_2_), channel_id=1, source_target_pairs={{0,1},{1,0},{2,3},{3,2},{4,5},{5,4},{6,7},{7,6},{8,9},{9,8},{10,11... | collective-permute-start | bytes 835592 | tf_op jit(solution)/shard_map/ppermute | solution.py:867
  162.0 3.6 %collective-permute-start.38 = (bf16[2,2,272,128]{3,2,1,0:T(8,128)(2,1)}, bf16[2,2,272,128]{3,2,1,0:T(8,128)(2,1)}, u32[]{:S(2)}, u32[]{:S(2)}) collective-permute-start(bf16[2,2,272,128]{3,2,1,0:T(8,128)(2,1)} %collective-permute-done.34.refs_3_), channel_id=1, source_target_pairs={{0,1},{1,0},{2,3},{3,2},{4,5},{5,4},{6,7},{7,6},{8,9},{9,8},{10,11... | collective-permute-start | bytes 835592 | tf_op jit(solution)/shard_map/ppermute | solution.py:867
  (10 other events, 21.8 us)
